TPU v7x, 32 devices: a whole 2x2x4 slice. The times are simulated.
32 devices in a mesh: parts: 2 (over y), rows: 8 (over z, x), head: 2 (over core).
Axes of the slice: x: 2, y: 2, z: 4, core: 2. Of those that a mesh axis runs over, the one named last changes fastest.
Arguments:
- prefill_states: bfloat16 [16, 128, 32, 128], P(('parts', 'rows'), 'head'), parts along dimension 0, may hold values from -0.5 to 0.5
- src_slot: int32 [16], P('parts'), parts along dimension 0, may hold values from 0 to 7, each once
- dst_slot: int32 [16], P('parts'), parts along dimension 0, may hold values from 0 to 15, as said below
- resident_states: bfloat16 [32, 128, 32, 128], P(('parts', 'rows'), 'head'), parts along dimension 0, may hold values from -0.5 to 0.5
- x_new: bfloat16 [4, 32, 128, 32], P(None, ('parts', 'rows'), 'head'), parts along dimension 1, may hold values from -6 to 6
- z_gate: bfloat16 [4, 32, 128, 32], P(None, ('parts', 'rows'), 'head'), parts along dimension 1, may hold values from -6 to 6
- dt_raw: float32 [4, 32, 128], P(None, ('parts', 'rows'), 'head'), parts along dimension 1, may hold values from -5 to 5
- b_in: bfloat16 [4, 32, 4, 128], P(None, ('parts', 'rows')), parts along dimension 1, may hold values from -0.59765625 to 0.59765625
- c_in: bfloat16 [4, 32, 4, 128], P(None, ('parts', 'rows')), parts along dimension 1, may hold values from -6 to 6
- a_rate: float32 [128], P('head'), may hold values from 0.05 to 3
- dt_bias: float32 [128], P('head'), may hold values from -1.5 to 0.5
- skip_d: float32 [128], P('head'), may hold values from 0.5 to 1.5
- norm_gain: float32 [128, 32], P('head'), may hold values from 0.1 to 1.9
Outputs:
- decoded: bfloat16 [4, 32, 128, 32], P(None, ('parts', 'rows'), 'head'), parts along dimension 1
- final_states: bfloat16 [32, 128, 32, 128], P(('parts', 'rows'), 'head'), parts along dimension 0
There are 2 independent parts, one for each index of `parts`. A program takes and returns all parts, laid end to end along the dimension named above; an argument that names none is the same for every part. Nothing has to cross between parts.
Inputs may be any that keep to these rules, and one draw needn't show every extreme that they name: `dst_slot`: distinct decode rows; the 2 rows of some one index of rows are all listed. `src_slot`: each prefill slot is named once.
All inputs are finite; a program needn't handle non-finite values.
Results may differ from a plain program's by a relative error of at most 0.001.
Values may be sent and summed in bfloat16 or wider, within the bound.
No kernel may reach another device: no remote copies, remote signals or barrier semaphores. Data moves between devices by JAX's collectives and lax.ppermute only.
A program may use at most 64 MiB of HBM per device.

v0:
```python
import jax
import jax.numpy as jnp
from jax import lax
from jax.sharding import PartitionSpec as P

HEADS = 128
GROUPS = 4


def advance(
    hidden_state, x_steps, z_steps, dt_steps, b_steps, c_steps, rate, bias, skip_gain, gain
):
    outputs = []
    for step_index in range(x_steps.shape[0]):
        inputs = x_steps[step_index].astype(jnp.float32)
        step_size = jax.nn.softplus(dt_steps[step_index] + bias[None, :])
        retained = jnp.exp(-rate[None, :] * step_size)
        b_now = b_steps[step_index].astype(jnp.float32)
        c_now = c_steps[step_index].astype(jnp.float32)
        hidden_state = (
            retained[:, :, None, None] * hidden_state
            + (step_size[:, :, None] * inputs)[:, :, :, None] * b_now[:, :, None, :]
        )
        readout = (
            jnp.sum(hidden_state * c_now[:, :, None, :], axis=-1)
            + skip_gain[None, :, None] * inputs
        )
        gated_out = readout * jax.nn.silu(z_steps[step_index].astype(jnp.float32))
        squares = jnp.mean(gated_out * gated_out, axis=(1, 2), keepdims=True)
        normed = gated_out * lax.rsqrt(squares + 1e-05) * gain[None]
        outputs.append(normed.astype(jnp.bfloat16))
    return (jnp.stack(outputs), hidden_state.astype(jnp.bfloat16))


def local(
    prefill_states,
    src_slot,
    dst_slot,
    resident_states,
    x_new,
    z_gate,
    dt_raw,
    b_in,
    c_in,
    a_rate,
    dt_bias,
    skip_d,
    norm_gain,
):
    row_count = resident_states.shape[0]
    local_heads = resident_states.shape[1]
    channels = resident_states.shape[2]
    entries = resident_states.shape[3]
    shards = lax.axis_size("rows")
    total_rows = shards * row_count
    matches = jnp.arange(total_rows, dtype=jnp.int32)[:, None] == dst_slot[None, :]
    listed = jnp.any(matches, axis=1)
    source = jnp.sum(jnp.where(matches, src_slot[None, :], 0), axis=1)
    flat_slots = prefill_states.reshape(prefill_states.shape[0], local_heads * channels, entries)
    spread = lax.all_to_all(flat_slots, "rows", split_axis=1, concat_axis=0, tiled=True)
    arrived = lax.all_to_all(
        jnp.take(spread, source, axis=0), "rows", split_axis=0, concat_axis=1, tiled=True
    )
    arrived = arrived.reshape(resident_states.shape)
    own_listed = lax.dynamic_slice_in_dim(listed, lax.axis_index("rows") * row_count, row_count)
    initial = jnp.where(own_listed[:, None, None, None], arrived, resident_states).astype(
        jnp.float32
    )
    per_group = HEADS // GROUPS
    local_groups = local_heads // per_group
    group_base = lax.axis_index("head") * local_groups
    pieces = []
    finals = []
    for group_index in range(local_groups):
        lower_head = group_index * per_group
        upper_head = lower_head + per_group
        outputs, final_part = advance(
            initial[:, lower_head:upper_head],
            x_new[:, :, lower_head:upper_head],
            z_gate[:, :, lower_head:upper_head],
            dt_raw[:, :, lower_head:upper_head],
            lax.dynamic_slice_in_dim(b_in, group_base + group_index, 1, 2),
            lax.dynamic_slice_in_dim(c_in, group_base + group_index, 1, 2),
            a_rate[lower_head:upper_head],
            dt_bias[lower_head:upper_head],
            skip_d[lower_head:upper_head],
            norm_gain[lower_head:upper_head],
        )
        pieces.append(outputs)
        finals.append(final_part)
    return (jnp.concatenate(pieces, 2), jnp.concatenate(finals, 1))


def solution(mesh):
    placed = (
        P(("parts", "rows"), "head", None, None),
        P("parts"),
        P("parts"),
        P(("parts", "rows"), "head", None, None),
        P(None, ("parts", "rows"), "head", None),
        P(None, ("parts", "rows"), "head", None),
        P(None, ("parts", "rows"), "head"),
        P(None, ("parts", "rows"), None, None),
        P(None, ("parts", "rows"), None, None),
        P("head"),
        P("head"),
        P("head"),
        P("head", None),
    )
    return jax.shard_map(
        local,
        mesh=mesh,
        in_specs=placed,
        out_specs=(
            P(None, ("parts", "rows"), "head", None),
            P(("parts", "rows"), "head", None, None),
        ),
        check_vma=False,
    )
```

profile of v0, /device:TPU:0, one launch (start us, length us, event | category | flops | bytes accessed | tf_op | source)
XLA Modules:
  0.0 79.2 jit_solution(3454351215663811429)
XLA Ops:
  0.6 1.8 %copy.120 = bf16[1,2048,128]{2,0,1:T(2,128)(2,1)S(1)} copy(bf16[1,2048,128]{2,1,0:T(8,128)(2,1)} %bitcast.331) | data formatting | bytes 1048576 | tf_op jit(solution)/shard_map/reshape | solution.py:59
  2.5 0.5 broadcast.468
  3.0 11.5 %reduce = bf16[2048,128]{1,0:T(8,128)(2,1)S(1)} reduce(bf16[2048,1,128]{2,1,0:T(2,128)(2,1)S(1)} %bitcast.330, bf16[]{:T(256)} %broadcast.468), dimensions={1}, to_apply=%bitcast.325.reduce_sub_computation | reduce | bytes 1048578
  14.5 0.9 %reshape.843 = bf16[8,2,16384]{2,1,0:T(2,128)(2,1)} reshape(bf16[2048,128]{1,0:T(8,128)(2,1)S(1)} %reduce) | data formatting | bytes 1048576
  15.5 7.3 %all-to-all-start = ((bf16[8,2,16384]{2,1,0:T(2,128)(2,1)}), bf16[8,2,16384]{2,1,0:T(2,128)(2,1)S(1)}, u32[]{:S(2)}, u32[]{:S(2)}) async-start(bf16[8,2,16384]{2,1,0:T(2,128)(2,1)} %reshape.843), calls=%async_computation | async-start | bytes 1048576 | tf_op jit(solution)/shard_map/all_to_all | solution.py:60
  22.7 0.1 fusion.156
  22.8 0.1 select_reduce_fusion
  23.0 0.1 fusion.175
  23.1 0.1 fusion.174
  23.2 14.0 %all-to-all-done = bf16[8,2,16384]{2,1,0:T(2,128)(2,1)S(1)} async-done(((bf16[8,2,16384]{2,1,0:T(2,128)(2,1)}), bf16[8,2,16384]{2,1,0:T(2,128)(2,1)S(1)}, u32[]{:S(2)}, u32[]{:S(2)}) %all-to-all-start) | async-done | bytes 524320 | tf_op jit(solution)/shard_map/all_to_all | solution.py:60
  37.2 0.5 reshape.844
  37.8 0.7 gather_fusion
  38.6 1.1 %broadcast_select_fusion = bf16[16,256,128]{2,1,0:T(8,128)(2,1)} fusion(bf16[16,256,128]{2,1,0:T(8,128)(2,1)S(1)} %gather_fusion, pred[16]{0:T(512)(128)(4,1)S(1)} %compare_and_fusion), kind=kLoop, calls=%fused_computation.21 | loop fusion | flops 524288 | bytes 2097168 | tf_op jit(solution)/shard_map/jit(_take)/select_n | solution.py:62
  39.8 3.6 %all-to-all-start.1 = ((bf16[16,256,128]{2,1,0:T(8,128)(2,1)}), bf16[16,256,128]{2,1,0:T(8,128)(2,1)S(1)}, u32[]{:S(2)}, u32[]{:S(2)}) async-start(bf16[16,256,128]{2,1,0:T(8,128)(2,1)} %broadcast_select_fusion), calls=%async_computation.1 | async-start | bytes 2097152 | tf_op jit(solution)/shard_map/all_to_all | solution.py:61
  43.5 0.1 copy.111
  43.6 0.1 copy.112
  43.6 0.1 copy.105
  43.7 0.1 copy.103
  43.8 0.1 copy.113
  43.9 0.1 copy.94
  44.0 0.1 copy.114
  44.1 0.1 copy.117
  44.2 0.1 copy.115
  44.3 0.1 copy.116
  44.4 0.1 copy.118
  44.5 0.1 copy.104
  44.6 0.1 copy.106
  44.7 0.1 copy.109
  44.8 0.1 copy.107
  44.9 0.1 copy.108
  45.0 0.1 copy.110
  45.1 0.1 dynamic_slice.15
  45.4 0.1 multiply_exponential_fusion.4
  45.5 0.1 fusion.33
  45.6 0.1 fusion.25
  45.7 0.1 fusion.21
  45.8 0.1 fusion.29
  45.9 23.5 %all-to-all-done.1 = bf16[16,256,128]{2,1,0:T(8,128)(2,1)S(1)} async-done(((bf16[16,256,128]{2,1,0:T(8,128)(2,1)}), bf16[16,256,128]{2,1,0:T(8,128)(2,1)S(1)}, u32[]{:S(2)}, u32[]{:S(2)}) %all-to-all-start.1) | async-done | bytes 1048608 | tf_op jit(solution)/shard_map/all_to_all | solution.py:61
  69.4 0.3 select_convert_fusion
  69.8 1.5 %multiply_reduce_fusion.7 = (f32[2,32,32]{2,1,0:T(8,128)S(1)}, f32[2,32,32]{2,1,0:T(8,128)S(1)}) fusion(f32[2,64,32,128]{3,2,1,0:T(8,128)S(1)} %select_convert_fusion, f32[2,128]{1,0:T(2,128)S(1)} %bitcast.336, f32[2,128]{1,0:T(2,128)S(1)} %bitcast.332, f32[2,32,32]{2,1,0:T(8,128)S(1)} %get-tuple-element.125, f32[2,32]{1,0:T(2,128)S(1)} %get-tuple-element.88, ...), kind=kLoop, calls=%fused_computation.19 | loop fusion | flops 2617344 | bytes 2134528 | tf_op jit(solution)/shard_map/reduce_sum | solution.py:25
  71.3 2.7 %multiply_reduce_fusion.1 = (f32[2,32,32]{2,1,0:T(8,128)S(1)}, f32[2,32,32]{2,1,0:T(8,128)S(1)}, f32[2,32,32]{2,1,0:T(8,128)S(1)}, bf16[2,32,32,128]{3,2,1,0:T(8,128)(2,1)S(1)}) fusion(f32[2,128]{1,0:T(2,128)S(1)} %bitcast.349, f32[2,128]{1,0:T(2,128)S(1)} %bitcast.344, f32[2,32,32]{2,1,0:T(8,128)S(1)} %get-tuple-element.119, f32[2,128]{1,0:T(2,128)S(1)} %bitcast.345, ...), kind=kLoop, calls=%fused_computation.8 | loop fusion | flops 4974592 | bytes 1638400 | tf_op jit(solution)/shard_map/reduce_sum | solution.py:25
  73.9 0.2 fusion.75
  74.2 2.7 %multiply_reduce_fusion.5 = (f32[2,32,32]{2,1,0:T(8,128)S(1)}, f32[2,32,32]{2,1,0:T(8,128)S(1)}, f32[2,32,32]{2,1,0:T(8,128)S(1)}, bf16[2,32,32,128]{3,2,1,0:T(8,128)(2,1)S(1)}) fusion(f32[2,128]{1,0:T(2,128)S(1)} %bitcast.342, f32[2,128]{1,0:T(2,128)S(1)} %bitcast.339, f32[2,32,32]{2,1,0:T(8,128)S(1)} %get-tuple-element.123, f32[2,128]{1,0:T(2,128)S(1)} %bitcast.340, ...), kind=kLoop, calls=%fused_computation.15 | loop fusion | flops 4974592 | bytes 1638400 | tf_op jit(solution)/shard_map/reduce_sum | solution.py:25
  76.9 0.2 fusion.39
  77.1 0.1 fusion.80
  77.2 0.1 fusion.44
  77.4 0.7 copy.101
  78.1 1.1 %pad_maximum_fusion = bf16[2,64,32,128]{3,2,1,0:T(8,128)(2,1)} fusion(bf16[2,32,32,128]{3,2,1,0:T(8,128)(2,1)S(1)} %get-tuple-element.41, bf16[2,32,32,128]{3,2,1,0:T(8,128)(2,1)S(1)} %get-tuple-element.40), kind=kLoop, calls=%fused_computation.5 | loop fusion | flops 524288 | bytes 2097152 | tf_op jit(solution)/shard_map/concatenate | solution.py:91
  (44 shorter events, 0.7 us)
Async XLA Ops:
  2.4 20.3 %copy-start.11 = (s32[8]{0:T(128)S(1)}, s32[8]{0:T(128)}, u32[]{:S(2)}) copy-start(s32[8]{0:T(128)} %param.15) | copy-start | bytes 100
  2.4 20.4 %copy-start.10 = (s32[8]{0:T(128)S(1)}, s32[8]{0:T(128)}, u32[]{:S(2)}) copy-start(s32[8]{0:T(128)} %param.14) | copy-start | bytes 100
  2.5 20.5 %copy-start.3 = (f32[64,32]{0,1:T(8,128)S(1)}, f32[64,32]{0,1:T(8,128)}, u32[]{:S(2)}) copy-start(f32[64,32]{0,1:T(8,128)} %param.25) | copy-start | bytes 24580
  2.5 20.5 %copy-start.1 = (bf16[4,2,64,32]{2,3,1,0:T(8,128)(2,1)S(1)}, bf16[4,2,64,32]{2,3,1,0:T(8,128)(2,1)}, u32[]{:S(2)}) copy-start(bf16[4,2,64,32]{2,3,1,0:T(8,128)(2,1)} %param.17) | copy-start | bytes 98308
  2.5 20.6 %copy-start.2 = (bf16[4,2,64,32]{2,3,1,0:T(8,128)(2,1)S(1)}, bf16[4,2,64,32]{2,3,1,0:T(8,128)(2,1)}, u32[]{:S(2)}) copy-start(bf16[4,2,64,32]{2,3,1,0:T(8,128)(2,1)} %param.18) | copy-start | bytes 98308
  15.5 21.7 %all-to-all-start = ((bf16[8,2,16384]{2,1,0:T(2,128)(2,1)}), bf16[8,2,16384]{2,1,0:T(2,128)(2,1)S(1)}, u32[]{:S(2)}, u32[]{:S(2)}) async-start(bf16[8,2,16384]{2,1,0:T(2,128)(2,1)} %reshape.843), calls=%async_computation | async-start | bytes 1048576 | tf_op jit(solution)/shard_map/all_to_all | solution.py:60
  38.6 4.8 %copy-start.5 = (bf16[4,2,4,128]{3,2,1,0:T(4,128)(2,1)S(1)}, bf16[4,2,4,128]{3,2,1,0:T(4,128)(2,1)}, u32[]{:S(2)}) copy-start(bf16[4,2,4,128]{3,2,1,0:T(4,128)(2,1)} %param.20) | copy-start | bytes 24580
  38.6 4.8 %copy-start.6 = (bf16[4,2,4,128]{3,2,1,0:T(4,128)(2,1)S(1)}, bf16[4,2,4,128]{3,2,1,0:T(4,128)(2,1)}, u32[]{:S(2)}) copy-start(bf16[4,2,4,128]{3,2,1,0:T(4,128)(2,1)} %param.21) | copy-start | bytes 24580
  38.6 6.6 %copy-start.7 = (f32[64]{0:T(128)S(1)}, f32[64]{0:T(128)}, u32[]{:S(2)}) copy-start(f32[64]{0:T(128)} %param.22) | copy-start | bytes 772
  38.6 6.7 %copy-start.8 = (f32[64]{0:T(128)S(1)}, f32[64]{0:T(128)}, u32[]{:S(2)}) copy-start(f32[64]{0:T(128)} %param.23) | copy-start | bytes 772
  38.6 6.7 %copy-start.9 = (f32[64]{0:T(128)S(1)}, f32[64]{0:T(128)}, u32[]{:S(2)}) copy-start(f32[64]{0:T(128)} %param.24) | copy-start | bytes 772
  38.6 6.8 %copy-start.4 = (f32[4,2,64]{2,1,0:T(2,128)S(1)}, f32[4,2,64]{2,1,0:T(2,128)}, u32[]{:S(2)}) copy-start(f32[4,2,64]{2,1,0:T(2,128)} %param.19) | copy-start | bytes 6148
  39.8 29.6 %all-to-all-start.1 = ((bf16[16,256,128]{2,1,0:T(8,128)(2,1)}), bf16[16,256,128]{2,1,0:T(8,128)(2,1)S(1)}, u32[]{:S(2)}, u32[]{:S(2)}) async-start(bf16[16,256,128]{2,1,0:T(8,128)(2,1)} %broadcast_select_fusion), calls=%async_computation.1 | async-start | bytes 2097152 | tf_op jit(solution)/shard_map/all_to_all | solution.py:61
  43.4 26.0 %copy-start = (bf16[2,64,32,128]{3,2,1,0:T(8,128)(2,1)S(1)}, bf16[2,64,32,128]{3,2,1,0:T(8,128)(2,1)}, u32[]{:S(2)}) copy-start(bf16[2,64,32,128]{3,2,1,0:T(8,128)(2,1)} %param.16) | copy-start | bytes 3145732
where the time goes:
time: 79.5 us; the launch traced here: 79.2 us
  waiting for transfers between devices  37.5 us (47%)
  other arithmetic  22.3 us (28%)
  starting transfers between devices  10.9 us (14%)
  local copies, waits for them, and re-layouts  7.56 us (10%)
  between operations  0.97 us (1%)
    all_to_all x1, waiting for transfers between devices, local(): lax.all_to_all(jnp.take(spread, source, axis=0), 'rows', split_axis=0, co...  23.5 us
    all_to_all x1, waiting for transfers between devices, local(): lax.all_to_all(flat_slots, 'rows', split_axis=1, concat_axis=0, tiled=True)  14 us
    unnamed x1, other arithmetic  11.5 us
    all_to_all x1, starting transfers between devices, local(): lax.all_to_all(flat_slots, 'rows', split_axis=1, concat_axis=0, tiled=True)  7.25 us
    reduce_sum x3, other arithmetic, advance(): jnp.sum(hidden_state * c_now[:, :, None, :], axis=-1)  6.83 us
    unnamed x45, local copies, waits for them, and re-layouts  4.31 us
    all_to_all x1, starting transfers between devices, local(): lax.all_to_all(jnp.take(spread, source, axis=0), 'rows', split_axis=0, co...  3.64 us
    reshape x1, local copies, waits for them, and re-layouts, local(): prefill_states.reshape(prefill_states.shape[0], local_heads * channels, e...  1.8 us
  transfers between devices with their start and end apart: 2, of which 2 were waited for; matrix products, arithmetic and copies ran while one was open for 4% of the time, Pallas kernels for 0%

commit v1 on v0

v1 whole, which is shorter than its diff:
```python
import functools

import jax
import jax.numpy as jnp
from jax import lax
from jax.experimental import pallas as pl
from jax.experimental.pallas import tpu as pltpu
from jax.sharding import PartitionSpec as P

HEADS = 128
GROUPS = 4
F32 = jnp.float32
BF16 = jnp.bfloat16


def split_terms(value):
    terms = []
    for _ in range(3):
        head = lax.reduce_precision(value, 8, 7)
        terms.append(head)
        value = value - head
    return terms


def gather_kernel(count, slots_ref, held_ref, out_ref, sem):
    def copy(i):
        return pltpu.make_async_copy(held_ref.at[slots_ref[i]], out_ref.at[i], sem.at[i])

    for i in range(count):
        copy(i).start()
    for i in range(count):
        copy(i).wait()


def gather_pieces(slots, held):
    count = slots.shape[0]
    return pl.pallas_call(
        functools.partial(gather_kernel, count),
        grid_spec=pltpu.PrefetchScalarGridSpec(
            num_scalar_prefetch=1,
            grid=(1,),
            in_specs=[pl.BlockSpec(memory_space=pl.ANY)],
            out_specs=pl.BlockSpec(memory_space=pl.ANY),
            scratch_shapes=[pltpu.SemaphoreType.DMA((count,))],
        ),
        out_shape=jax.ShapeDtypeStruct((count,) + held.shape[1:], held.dtype),
    )(slots, held)


def decode_kernel(
    rows, groups, pieces, info_ref, recv_ref, resident_ref, c_ref, left_ref, right_ref,
    carry_ref, base_ref, gate_ref, gain_ref, decoded_ref, final_ref, state, sem,
):
    span = recv_ref.shape[2]

    def each(r, act):
        listed = info_ref[r]
        mask = info_ref[rows + r]

        def piece(q):
            here = pl.ds(pl.multiple_of(q * span, 16), span)

            @pl.when(listed == 1)
            def _():
                act(pltpu.make_async_copy(
                    recv_ref.at[q ^ mask, r], state.at[r, here], sem.at[r]))

            @pl.when(listed == 0)
            def _():
                act(pltpu.make_async_copy(
                    resident_ref.at[r, here], state.at[r, here], sem.at[r]))

        if pieces <= 8:
            for q in range(pieces):
                piece(q)
        else:
            pl.loop(0, pieces)(piece)

    for r in range(rows):
        each(r, lambda copy: copy.start())
    for r in range(rows):
        each(r, lambda copy: copy.wait())
    block = state.shape[1] // groups
    for g in range(groups):
        lanes = slice(g * block, (g + 1) * block)
        seen = None
        for r in range(rows):
            initial = state[r, lanes]
            part = lax.dot_general(
                c_ref[r, g], initial, (((1,), (1,)), ((), ())), preferred_element_type=F32)
            seen = part if seen is None else seen + part
            moved = lax.dot_general(
                left_ref[r, :, lanes], right_ref[r, g], (((0,), (0,)), ((), ())),
                preferred_element_type=F32)
            width = initial.shape[1]
            final_ref[r, lanes] = (
                moved[:, width:] * initial.astype(F32) + moved[:, :width]).astype(BF16)
        readout = carry_ref[:, lanes] * seen + base_ref[:, lanes]
        gated = readout * gate_ref[:, lanes]
        squares = jnp.mean(gated * gated, axis=1, keepdims=True)
        normed = gated * lax.rsqrt(squares + 1e-05) * gain_ref[:, lanes]
        decoded_ref[:, lanes] = normed.astype(BF16)


def decode(info, recv, resident, c_rows, left, right, carry, base, gate, gain):
    rows, flat, entries = resident.shape
    groups = c_rows.shape[1]
    whole = pl.BlockSpec(memory_space=pltpu.VMEM)
    anywhere = pl.BlockSpec(memory_space=pl.ANY)
    return pl.pallas_call(
        functools.partial(decode_kernel, rows, groups, recv.shape[0]),
        grid_spec=pltpu.PrefetchScalarGridSpec(
            num_scalar_prefetch=1,
            grid=(1,),
            in_specs=[anywhere, anywhere] + [whole] * 7,
            out_specs=[whole, whole],
            scratch_shapes=[
                pltpu.VMEM((rows, flat, entries), BF16),
                pltpu.SemaphoreType.DMA((rows,)),
            ],
        ),
        out_shape=[
            jax.ShapeDtypeStruct(base.shape, BF16),
            jax.ShapeDtypeStruct((rows, flat, entries), BF16),
        ],
        compiler_params=pltpu.CompilerParams(vmem_limit_bytes=32 * 1024 * 1024),
    )(info, recv, resident, c_rows, left, right, carry, base, gate, gain)


def prepare(x_new, z_gate, dt_raw, b_in, c_in, a_rate, dt_bias, skip_d, norm_gain):
    steps, rows, heads, channels = x_new.shape
    groups, entries = b_in.shape[2:]
    flat = heads * channels

    def over_channels(value):
        return jnp.broadcast_to(value[..., None], value.shape + (channels,)).reshape(
            value.shape[:-1] + (flat,))

    x = x_new.reshape(steps, rows, flat).astype(F32)
    delta = jax.nn.softplus(dt_raw + dt_bias)
    kept = jnp.exp(-a_rate * delta)
    bc = jnp.sum(
        c_in.astype(F32)[:, None] * b_in.astype(F32)[None], axis=-1)
    bc = jnp.repeat(bc, heads // groups, axis=-1)
    carry, weights, factors = [], [], []
    for t in range(steps):
        carry.append(kept[t] if t == 0 else carry[-1] * kept[t])
        weights = [w * kept[t] for w in weights] + [delta[t]]
        for s in range(t + 1):
            factor = weights[s] * bc[t, s]
            factors.append(factor + skip_d if s == t else factor)
    lanes = over_channels(jnp.stack(factors + carry + weights))
    base, at = [], 0
    for t in range(steps):
        base.append(sum(lanes[at + s] * x[s] for s in range(t + 1)))
        at += t + 1
    carry_lanes = lanes[at:at + steps]
    moved = lanes[at + steps:] * x
    left = [p[s] for p in split_terms(moved) for s in range(steps)]
    left += split_terms(carry_lanes[-1])
    left.append(jnp.zeros_like(left[0]))
    left = jnp.stack(left, axis=1).astype(BF16)
    b_rows = jnp.moveaxis(b_in, 0, 2)
    none = jnp.zeros((rows, groups, 3 * steps, entries), BF16)
    ones = jnp.ones((rows, groups, 3, entries), BF16)
    right = jnp.concatenate([
        jnp.concatenate([b_rows] * 3 + [none[:, :, :4]], 2),
        jnp.concatenate([none, ones, none[:, :, :1]], 2),
    ], 3)
    own = jnp.eye(rows, dtype=BF16)[:, None, None, :, None]
    c_rows = jnp.moveaxis(c_in, 0, 2)[:, :, :, None] * own
    gate = jax.nn.silu(z_gate.reshape(steps, rows, flat).astype(F32))
    both = steps * rows
    return (
        c_rows.reshape(rows, groups, both, entries),
        left,
        right,
        carry_lanes.reshape(both, flat),
        jnp.stack(base).reshape(both, flat),
        gate.reshape(both, flat),
        norm_gain.reshape(1, flat),
    )


def local(
    prefill_states, src_slot, dst_slot, resident_states, x_new, z_gate, dt_raw, b_in, c_in,
    a_rate, dt_bias, skip_d, norm_gain,
):
    row_count, local_heads, channels, entries = resident_states.shape
    flat = local_heads * channels
    shards = lax.axis_size("rows")
    me = lax.axis_index("rows")
    quarter = shards // 2
    matches = jnp.arange(shards * row_count, dtype=jnp.int32)[:, None] == dst_slot[None, :]
    listed = jnp.any(matches, axis=1).astype(jnp.int32)
    source = jnp.sum(jnp.where(matches, src_slot[None, :], 0), axis=1)

    span = flat // quarter
    pieces = prefill_states.reshape(quarter, span, entries)
    few = shards == 8
    if few:
        held = [pieces[0]]
        for k in range(1, shards):
            held.append(lax.ppermute(
                pieces[k % quarter], "rows", [(i, i ^ k) for i in range(shards)]))
        held = jnp.stack(held)
        slots = source ^ me
        mask = source % quarter
    else:
        held = lax.all_to_all(
            jnp.concatenate([pieces, pieces]), "rows", split_axis=0, concat_axis=0, tiled=True)
        slots = source
        mask = jnp.zeros_like(source)
    half_rows = quarter * row_count
    slots = lax.dynamic_slice_in_dim(slots, (me // quarter) * half_rows, half_rows)
    halves = [[h * quarter + i for i in range(quarter)] for h in range(2)]
    sent = gather_pieces(slots, held).reshape(quarter, row_count * span, entries)
    recv = lax.all_to_all(
        sent, "rows", split_axis=0, concat_axis=0, tiled=True, axis_index_groups=halves)
    recv = recv.reshape(quarter, row_count, span, entries)

    groups = local_heads // (HEADS // GROUPS)
    group_base = lax.axis_index("head") * groups
    ready = prepare(
        x_new, z_gate, dt_raw,
        lax.dynamic_slice_in_dim(b_in, group_base, groups, 2),
        lax.dynamic_slice_in_dim(c_in, group_base, groups, 2),
        a_rate, dt_bias, skip_d, norm_gain)
    info = jnp.concatenate([
        lax.dynamic_slice_in_dim(listed, me * row_count, row_count),
        lax.dynamic_slice_in_dim(mask, me * row_count, row_count)])
    decoded, final = decode(
        info, recv, resident_states.reshape(row_count, flat, entries), *ready)
    return (decoded.reshape(x_new.shape), final.reshape(resident_states.shape))


def solution(mesh):
    placed = (
        P(("parts", "rows"), "head", None, None),
        P("parts"),
        P("parts"),
        P(("parts", "rows"), "head", None, None),
        P(None, ("parts", "rows"), "head", None),
        P(None, ("parts", "rows"), "head", None),
        P(None, ("parts", "rows"), "head"),
        P(None, ("parts", "rows"), None, None),
        P(None, ("parts", "rows"), None, None),
        P("head"),
        P("head"),
        P("head"),
        P("head", None),
    )
    return jax.shard_map(
        local,
        mesh=mesh,
        in_specs=placed,
        out_specs=(
            P(None, ("parts", "rows"), "head", None),
            P(("parts", "rows"), "head", None, None),
        ),
        check_vma=False,
    )
```

time: 79.5 us -> 89.6 us (1.13)
  Pallas kernels: 0 us -> 37.6 us
  other arithmetic: 22.3 us -> 0.8 us
  waiting for transfers between devices: 37.5 us -> 20.9 us
  starting transfers between devices: 10.9 us -> 16.3 us
  local copies, waits for them, and re-layouts: 7.56 us -> 12.3 us
    pallas_call x0 -> x2, Pallas kernels: none -> 37.6 us  [the longest x1 33.6 us: gather_pieces(): pl.pallas_call(functools.partial(gather_kernel, count), grid_spec=pltpu.P...]
    all_to_all x2 -> x1, waiting for transfers between devices: 37.5 us -> 10.6 us  [local(): lax.all_to_all(sent, 'rows', split_axis=0, concat_axis=0, tiled=True, axi...]
    ppermute x0 -> x7, starting transfers between devices: none -> 12.6 us  [local(): lax.ppermute(pieces[k % quarter], 'rows', [(i, i ^ k) for i in range(shar...]
    unnamed x1 -> x0, other arithmetic: 11.5 us -> none
    ppermute x0 -> x7, waiting for transfers between devices: none -> 10.4 us  [local(): lax.ppermute(pieces[k % quarter], 'rows', [(i, i ^ k) for i in range(shar...]
    all_to_all x2 -> x1, starting transfers between devices: 10.9 us -> 3.66 us  [local(): lax.all_to_all(sent, 'rows', split_axis=0, concat_axis=0, tiled=True, axi...]
    reduce_sum x5 -> x1, other arithmetic: 7.24 us -> 0.1 us  [prepare(): bc = jnp.sum(c_in.astype(F32)[:, None] * b_in.astype(F32)[None], axis=-1)]
    broadcast_in_dim x0 -> x24, local copies, waits for them, and re-layouts: none -> 2.15 us  [the longest x23 2.06 us: over_channels(): jnp.broadcast_to(value[..., None], value.shape + (channels,))]
  transfers between devices with their start and end apart: 2 -> 8, of which waited for: 2 -> 2; matrix products, arithmetic and copies ran while one was open for 4% -> 7% of each run, Pallas kernels for 0% -> 0%
where the time goes in v1:
time: 89.6 us; the launch traced here: 89.1 us
  Pallas kernels  37.6 us (42%)
  waiting for transfers between devices  20.9 us (23%)
  starting transfers between devices  16.3 us (18%)
  local copies, waits for them, and re-layouts  12.3 us (14%)
  between operations  1.29 us (1%)
    pallas_call x1, Pallas kernels, gather_pieces(): pl.pallas_call(functools.partial(gather_kernel, count), grid_spec=pltpu.P...  33.6 us
    ppermute x7, starting transfers between devices, local(): lax.ppermute(pieces[k % quarter], 'rows', [(i, i ^ k) for i in range(shar...  12.6 us
    all_to_all x1, waiting for transfers between devices, local(): lax.all_to_all(sent, 'rows', split_axis=0, concat_axis=0, tiled=True, axi...  10.6 us
    ppermute x7, waiting for transfers between devices, local(): lax.ppermute(pieces[k % quarter], 'rows', [(i, i ^ k) for i in range(shar...  10.4 us
    unnamed x37, local copies, waits for them, and re-layouts  5.51 us
    pallas_call x1, Pallas kernels, decode(): pl.pallas_call(functools.partial(decode_kernel, rows, groups, recv.shape[...  3.96 us
    all_to_all x1, starting transfers between devices, local(): lax.all_to_all(sent, 'rows', split_axis=0, concat_axis=0, tiled=True, axi...  3.66 us
    broadcast_in_dim x23, local copies, waits for them, and re-layouts, over_channels(): jnp.broadcast_to(value[..., None], value.shape + (channels,))  2.06 us
  transfers between devices with their start and end apart: 8, of which 2 were waited for; matrix products, arithmetic and copies ran while one was open for 7% of the time, Pallas kernels for 0%

profile of v1, /device:TPU:0, one launch (start us, length us, event | category | flops | bytes accessed | tf_op | source)
XLA Modules:
  0.0 89.1 jit_solution(11005779452891013302)
XLA Ops:
  0.6 1.1 %fusion.30 = (bf16[1,16,32,128]{3,2,1,0:T(8,128)(2,1)S(1)}, bf16[1,16,32,128]{3,2,1,0:T(8,128)(2,1)S(1)}, bf16[1,16,32,128]{3,2,1,0:T(8,128)(2,1)S(1)}, bf16[1,16,32,128]{3,2,1,0:T(8,128)(2,1)S(1)}) fusion(bf16[1,64,32,128]{3,2,1,0:T(8,128)(2,1)} %param.13), kind=kLoop, calls=%fused_computation.103 | loop fusion | bytes 1048576 | tf_op jit(solution)/shard_map/slice | solution.py:205
  1.8 3.0 %collective-permute-start = (bf16[512,128]{1,0:T(8,128)(2,1)S(1)}, bf16[512,128]{1,0:T(8,128)(2,1)S(1)}, u32[]{:S(2)}, u32[]{:S(2)}) collective-permute-start(bf16[512,128]{1,0:T(8,128)(2,1)S(1)} %bitcast.164), channel_id=1, source_target_pairs={{0,2},{2,0},{4,6},{6,4},{8,10},{10,8},{12,14},{14,12},{1,3},{3,1},... | collective-permute-start | bytes 393224 | tf_op jit(solution)/shard_map/ppermute | solution.py:204
  4.8 2.6 %collective-permute-start.4 = (bf16[512,128]{1,0:T(8,128)(2,1)S(1)}, bf16[512,128]{1,0:T(8,128)(2,1)S(1)}, u32[]{:S(2)}, u32[]{:S(2)}) collective-permute-start(bf16[512,128]{1,0:T(8,128)(2,1)S(1)} %bitcast.165), channel_id=1, source_target_pairs={{0,10},{2,8},{4,14},{6,12},{8,2},{10,0},{12,6},{14,4},{1,11},{3,9}... | collective-permute-start | bytes 393224 | tf_op jit(solution)/shard_map/ppermute | solution.py:204
  7.3 1.6 %collective-permute-start.1 = (bf16[512,128]{1,0:T(8,128)(2,1)S(1)}, bf16[512,128]{1,0:T(8,128)(2,1)S(1)}, u32[]{:S(2)}, u32[]{:S(2)}) collective-permute-start(bf16[512,128]{1,0:T(8,128)(2,1)S(1)} %bitcast.162), channel_id=1, source_target_pairs={{0,4},{2,6},{4,0},{6,2},{8,12},{10,14},{12,8},{14,10},{1,5},{3,7},... | collective-permute-start | bytes 393224 | tf_op jit(solution)/shard_map/ppermute | solution.py:204
  8.9 1.8 %collective-permute-start.2 = (bf16[512,128]{1,0:T(8,128)(2,1)S(1)}, bf16[512,128]{1,0:T(8,128)(2,1)S(1)}, u32[]{:S(2)}, u32[]{:S(2)}) collective-permute-start(bf16[512,128]{1,0:T(8,128)(2,1)S(1)} %bitcast.160), channel_id=1, source_target_pairs={{0,6},{2,4},{4,2},{6,0},{8,14},{10,12},{12,10},{14,8},{1,7},{3,5},... | collective-permute-start | bytes 393224 | tf_op jit(solution)/shard_map/ppermute | solution.py:204
  10.7 0.7 copy-done.12
  11.6 0.5 copy-done.8
  12.1 0.1 copy-done.7
  12.2 0.1 multiply_reduce_fusion
  12.3 0.1 copy.365
  12.6 0.1 reshape.242
  12.7 0.4 copy-done.13
  13.2 0.6 copy-done.9
  13.9 0.1 copy.348
  14.1 0.2 mul.221
  14.5 0.1 broadcast_in_dim.84
  14.7 0.1 broadcast_in_dim.98
  14.9 0.1 slice.248
  15.1 0.1 broadcast_in_dim.96
  15.3 0.1 slice.243
  15.5 0.1 broadcast_in_dim.94
  15.6 0.1 slice.239
  15.8 0.1 broadcast_in_dim.106
  16.0 0.1 slice.254
  16.2 0.1 broadcast_in_dim.104
  16.4 0.1 broadcast_in_dim.102
  16.5 0.1 broadcast_in_dim.100
  16.7 0.1 broadcast_in_dim.92
  16.9 0.1 broadcast_in_dim.90
  17.1 0.1 broadcast_in_dim.88
  17.9 0.6 dynamic_slice.17.slots_ref
  18.5 3.0 %collective-permute-start.6 = (bf16[512,128]{1,0:T(8,128)(2,1)S(1)}, bf16[512,128]{1,0:T(8,128)(2,1)S(1)}, u32[]{:S(2)}, u32[]{:S(2)}) collective-permute-start(bf16[512,128]{1,0:T(8,128)(2,1)S(1)} %bitcast.161), channel_id=1, source_target_pairs={{0,14},{2,12},{4,10},{6,8},{8,6},{10,4},{12,2},{14,0},{1,15},{3,13... | collective-permute-start | bytes 393224 | tf_op jit(solution)/shard_map/ppermute | solution.py:204
  21.5 0.6 collective-permute-start.3
  22.2 10.3 %collective-permute-done.3 = bf16[512,128]{1,0:T(8,128)(2,1)S(1)} collective-permute-done((bf16[512,128]{1,0:T(8,128)(2,1)S(1)}, bf16[512,128]{1,0:T(8,128)(2,1)S(1)}, u32[]{:S(2)}, u32[]{:S(2)}) %collective-permute-start.3) | collective-permute-done | bytes 131104 | tf_op jit(solution)/shard_map/ppermute | solution.py:204
  32.7 1.0 %copy-done.1 = bf16[8,512,128]{2,1,0:T(8,128)(2,1)} copy-done((bf16[8,512,128]{2,1,0:T(8,128)(2,1)}, bf16[8,512,128]{2,1,0:T(8,128)(2,1)S(1)}, u32[]{:S(2)}) %copy-start.1) | copy-done | bytes 1048600
  33.7 33.6 %shard_map.140 = bf16[8,512,128]{2,1,0:T(8,128)(2,1)} custom-call(s32[8]{0:T(128)} %dynamic_slice.17.slots_ref, bf16[8,512,128]{2,1,0:T(8,128)(2,1)} %copy-done.1), custom_call_target="tpu_custom_call" | custom-call | tf_op jit(solution)/shard_map/pallas_call | solution.py:37
  67.3 3.7 %all-to-all-start = ((bf16[4,1024,128]{2,1,0:T(8,128)(2,1)}), bf16[4,1024,128]{2,1,0:T(8,128)(2,1)S(1)}, u32[]{:S(2)}, u32[]{:S(2)}) async-start(bf16[4,1024,128]{2,1,0:T(8,128)(2,1)} %bitcast.157), calls=%async_computation | async-start | bytes 2097152 | tf_op jit(solution)/shard_map/all_to_all | solution.py:218
  71.0 0.1 broadcast_in_dim.85
  71.1 0.1 reshape.241.carry_ref
  71.4 0.1 copy.370
  71.5 0.1 reshape.247
  71.6 0.6 copy-done.4
  72.4 0.4 stack.68.left_ref
  73.0 0.6 copy-done.5
  73.7 10.6 %all-to-all-done = bf16[4,1024,128]{2,1,0:T(8,128)(2,1)S(1)} async-done(((bf16[4,1024,128]{2,1,0:T(8,128)(2,1)}), bf16[4,1024,128]{2,1,0:T(8,128)(2,1)S(1)}, u32[]{:S(2)}, u32[]{:S(2)}) %all-to-all-start) | async-done | bytes 1048608 | tf_op jit(solution)/shard_map/all_to_all | solution.py:218
  84.2 4.0 %shard_map.141 = (bf16[8,2048]{1,0:T(8,128)(2,1)S(1)}, bf16[2,2048,128]{2,1,0:T(8,128)(2,1)}) custom-call(s32[4]{0:T(128)S(1)} %pad_add_fusion.info_ref, bf16[4,2,512,128]{3,2,1,0:T(8,128)(2,1)S(1)} %bitcast.155, bf16[2,2048,128]{2,1,0:T(8,128)(2,1)S(1)} %bitcast.156, bf16[2,2,8,128]{3,2,1,0:T(8,128)(2,1)S(1)} %broadcast_multiply_fusion.1.c_ref, ...), custom_call_target="tpu_custom_call" | custom-call | tf_op jit(solution)/shard_map/pallas_call | solution.py:110
  88.2 0.1 reshape.245
  88.4 0.7 copy.372
  (104 shorter events, 3.0 us)
Async XLA Ops:
  1.8 16.7 %collective-permute-start = (bf16[512,128]{1,0:T(8,128)(2,1)S(1)}, bf16[512,128]{1,0:T(8,128)(2,1)S(1)}, u32[]{:S(2)}, u32[]{:S(2)}) collective-permute-start(bf16[512,128]{1,0:T(8,128)(2,1)S(1)} %bitcast.164), channel_id=1, source_target_pairs={{0,2},{2,0},{4,6},{6,4},{8,10},{10,8},{12,14},{14,12},{1,3},{3,1},... | collective-permute-start | bytes 393224 | tf_op jit(solution)/shard_map/ppermute | solution.py:204
  4.8 27.9 %collective-permute-start.4 = (bf16[512,128]{1,0:T(8,128)(2,1)S(1)}, bf16[512,128]{1,0:T(8,128)(2,1)S(1)}, u32[]{:S(2)}, u32[]{:S(2)}) collective-permute-start(bf16[512,128]{1,0:T(8,128)(2,1)S(1)} %bitcast.165), channel_id=1, source_target_pairs={{0,10},{2,8},{4,14},{6,12},{8,2},{10,0},{12,6},{14,4},{1,11},{3,9}... | collective-permute-start | bytes 393224 | tf_op jit(solution)/shard_map/ppermute | solution.py:204
  7.3 4.2 %copy-start.11 = (s32[8]{0:T(128)S(1)}, s32[8]{0:T(128)}, u32[]{:S(2)}) copy-start(s32[8]{0:T(128)} %param.14) | copy-start | bytes 100
  7.3 14.2 %collective-permute-start.1 = (bf16[512,128]{1,0:T(8,128)(2,1)S(1)}, bf16[512,128]{1,0:T(8,128)(2,1)S(1)}, u32[]{:S(2)}, u32[]{:S(2)}) collective-permute-start(bf16[512,128]{1,0:T(8,128)(2,1)S(1)} %bitcast.162), channel_id=1, source_target_pairs={{0,4},{2,6},{4,0},{6,2},{8,12},{10,14},{12,8},{14,10},{1,5},{3,7},... | collective-permute-start | bytes 393224 | tf_op jit(solution)/shard_map/ppermute | solution.py:204
  8.9 23.7 %collective-permute-start.5 = (bf16[512,128]{1,0:T(8,128)(2,1)S(1)}, bf16[512,128]{1,0:T(8,128)(2,1)S(1)}, u32[]{:S(2)}, u32[]{:S(2)}) collective-permute-start(bf16[512,128]{1,0:T(8,128)(2,1)S(1)} %bitcast.163), channel_id=1, source_target_pairs={{0,12},{2,14},{4,8},{6,10},{8,4},{10,6},{12,0},{14,2},{1,13},{3,15... | collective-permute-start | bytes 393224 | tf_op jit(solution)/shard_map/ppermute | solution.py:204
  8.9 13.3 %collective-permute-start.2 = (bf16[512,128]{1,0:T(8,128)(2,1)S(1)}, bf16[512,128]{1,0:T(8,128)(2,1)S(1)}, u32[]{:S(2)}, u32[]{:S(2)}) collective-permute-start(bf16[512,128]{1,0:T(8,128)(2,1)S(1)} %bitcast.160), channel_id=1, source_target_pairs={{0,6},{2,4},{4,2},{6,0},{8,14},{10,12},{12,10},{14,8},{1,7},{3,5},... | collective-permute-start | bytes 393224 | tf_op jit(solution)/shard_map/ppermute | solution.py:204
  10.7 0.7 copy-start.12
  11.4 0.7 copy-start.8
  11.5 0.7 copy-start.7
  12.4 0.7 copy-start.13
  12.5 0.7 copy-start.6
  12.5 0.7 copy-start.10
  12.6 1.3 %copy-start.2 = (bf16[4,2,64,32]{2,3,1,0:T(8,128)(2,1)S(1)}, bf16[4,2,64,32]{2,3,1,0:T(8,128)(2,1)}, u32[]{:S(2)}) copy-start(bf16[4,2,64,32]{2,3,1,0:T(8,128)(2,1)} %param.17) | copy-start | bytes 98308
  13.2 0.7 copy-start.9
  18.5 14.2 %collective-permute-start.6 = (bf16[512,128]{1,0:T(8,128)(2,1)S(1)}, bf16[512,128]{1,0:T(8,128)(2,1)S(1)}, u32[]{:S(2)}, u32[]{:S(2)}) collective-permute-start(bf16[512,128]{1,0:T(8,128)(2,1)S(1)} %bitcast.161), channel_id=1, source_target_pairs={{0,14},{2,12},{4,10},{6,8},{8,6},{10,4},{12,2},{14,0},{1,15},{3,13... | collective-permute-start | bytes 393224 | tf_op jit(solution)/shard_map/ppermute | solution.py:204
  21.5 11.1 %collective-permute-start.3 = (bf16[512,128]{1,0:T(8,128)(2,1)S(1)}, bf16[512,128]{1,0:T(8,128)(2,1)S(1)}, u32[]{:S(2)}, u32[]{:S(2)}) collective-permute-start(bf16[512,128]{1,0:T(8,128)(2,1)S(1)} %bitcast.159), channel_id=1, source_target_pairs={{0,8},{2,10},{4,12},{6,14},{8,0},{10,2},{12,4},{14,6},{1,9},{3,11}... | collective-permute-start | bytes 393224 | tf_op jit(solution)/shard_map/ppermute | solution.py:204
  32.7 1.0 %copy-start.1 = (bf16[8,512,128]{2,1,0:T(8,128)(2,1)}, bf16[8,512,128]{2,1,0:T(8,128)(2,1)S(1)}, u32[]{:S(2)}) copy-start(bf16[8,512,128]{2,1,0:T(8,128)(2,1)S(1)} %bitcast_dynamic-update-slice_fusion.held_ref) | copy-start | bytes 3145732
  67.3 4.0 %copy-start.3 = (bf16[4,2,64,32]{2,3,1,0:T(8,128)(2,1)S(1)}, bf16[4,2,64,32]{2,3,1,0:T(8,128)(2,1)}, u32[]{:S(2)}) copy-start(bf16[4,2,64,32]{2,3,1,0:T(8,128)(2,1)} %param.18) | copy-start | bytes 98308
  67.3 16.9 %all-to-all-start = ((bf16[4,1024,128]{2,1,0:T(8,128)(2,1)}), bf16[4,1024,128]{2,1,0:T(8,128)(2,1)S(1)}, u32[]{:S(2)}, u32[]{:S(2)}) async-start(bf16[4,1024,128]{2,1,0:T(8,128)(2,1)} %bitcast.157), calls=%async_computation | async-start | bytes 2097152 | tf_op jit(solution)/shard_map/all_to_all | solution.py:218
  71.0 13.2 %copy-start = (bf16[2,64,32,128]{3,2,1,0:T(8,128)(2,1)S(1)}, bf16[2,64,32,128]{3,2,1,0:T(8,128)(2,1)}, u32[]{:S(2)}) copy-start(bf16[2,64,32,128]{3,2,1,0:T(8,128)(2,1)} %param.16) | copy-start | bytes 3145732
  71.5 0.7 copy-start.4
  72.9 0.7 copy-start.5

commit v2 on v0

v2 whole, which is shorter than its diff:
```python
import functools

import jax
import jax.numpy as jnp
from jax import lax
from jax.experimental import pallas as pl
from jax.experimental.pallas import tpu as pltpu
from jax.sharding import PartitionSpec as P

HEADS = 128
GROUPS = 4
F32 = jnp.float32
BF16 = jnp.bfloat16
VMEM = pl.BlockSpec(memory_space=pltpu.VMEM)
SMEM = pl.BlockSpec(memory_space=pltpu.SMEM)
ANY = pl.BlockSpec(memory_space=pl.ANY)


def gather_kernel(group, slots_ref, held_ref, out_ref):
    count = out_ref.shape[0]

    def one(i):
        out_ref[i] = held_ref[slots_ref[i], group]

    if count <= 16:
        for i in range(count):
            one(i)
    else:
        pl.loop(0, count)(one)


def gather_pieces(group, slots, held):
    return pl.pallas_call(
        functools.partial(gather_kernel, group),
        in_specs=[SMEM, VMEM],
        out_specs=VMEM,
        out_shape=jax.ShapeDtypeStruct(slots.shape + held.shape[2:], held.dtype),
        compiler_params=pltpu.CompilerParams(vmem_limit_bytes=4 * 1024 * 1024),
    )(slots, held)


def split_terms(value):
    terms = []
    for _ in range(3):
        head = value.astype(BF16).astype(F32)
        terms.append(head)
        value = value - head
    return terms


def prepare_kernel(
    rows, x_ref, z_ref, dt_ref, b_ref, c_ref, head_ref,
    base_ref, carry_ref, gate_ref, left_ref, right_ref, seen_ref,
):
    both, flat = x_ref.shape
    steps = both // rows
    groups = b_ref.shape[0]
    entries = b_ref.shape[2]
    width = flat // groups
    row = lax.broadcasted_iota(jnp.int32, (both, 1), 0)

    def earlier(value, by):
        return value if by == 0 else pltpu.roll(value, by * rows, 0)

    x = x_ref[...].astype(F32)
    z = z_ref[...].astype(F32)
    gate_ref[...] = z / (1.0 + jnp.exp(-z))
    rate, bias, skip = head_ref[0:1], head_ref[1:2], head_ref[2:3]
    logit = dt_ref[...] + bias
    delta = jnp.maximum(logit, 0.0) + jnp.log1p(jnp.exp(-jnp.abs(logit)))
    kept = jnp.exp(-rate * delta)
    carry = kept
    later = jnp.where(row < both - rows, pltpu.roll(kept, both - rows, 0), 1.0)
    reach = 1
    rest = later
    while reach < steps:
        carry = carry * jnp.where(row >= reach * rows, earlier(carry, reach), 1.0)
        rest = rest * jnp.where(
            row < both - reach * rows, pltpu.roll(rest, both - reach * rows, 0), 1.0)
        reach *= 2
    carry_ref[...] = carry

    base = skip * x
    weight = jnp.ones_like(kept)
    for by in range(steps):
        if by:
            weight = weight * earlier(kept, by - 1)
        term = weight * earlier(delta, by) * earlier(x, by)
        parts = []
        for g in range(groups):
            b = b_ref[g].astype(F32)
            c = c_ref[g].astype(F32)
            match = jnp.sum(c * earlier(b, by), axis=1, keepdims=True)
            parts.append(match * term[:, g * width:(g + 1) * width])
        total = jnp.concatenate(parts, axis=1)
        base = base + jnp.where(row >= by * rows, total, 0.0)
    base_ref[...] = base

    left = split_terms(delta * rest * x) + split_terms(carry)
    left_ref[...] = jnp.concatenate(left, axis=0).astype(BF16)
    none = jnp.zeros((3 * both, entries), F32)
    for g in range(groups):
        b = b_ref[g].astype(F32)
        c = c_ref[g].astype(F32)
        right, seen = [], []
        for r in range(rows):
            mine = row % rows == r
            last = jnp.where(row == both - rows + r, 1.0, 0.0) + jnp.zeros((both, entries), F32)
            picked = jnp.where(mine, b, 0.0)
            right.append(jnp.concatenate([picked] * 3 + [none], axis=0))
            right.append(jnp.concatenate([none] + [last] * 3, axis=0))
            seen.append(jnp.where(mine, c, 0.0))
        right_ref[g] = jnp.concatenate(right, axis=1).astype(BF16)
        seen_ref[g] = jnp.concatenate(seen, axis=1).astype(BF16)


def prepare(x_new, z_gate, dt_raw, b_in, c_in, a_rate, dt_bias, skip_d):
    steps, rows, heads, channels = x_new.shape
    groups, entries = b_in.shape[2:]
    flat = heads * channels
    both = steps * rows

    def over_channels(value):
        return jnp.broadcast_to(value[..., None], value.shape + (channels,)).reshape(
            value.shape[0], flat)

    def wide(*shape):
        return jax.ShapeDtypeStruct(shape, F32 if len(shape) == 2 else BF16)

    return pl.pallas_call(
        functools.partial(prepare_kernel, rows),
        in_specs=[VMEM] * 6,
        out_specs=[VMEM] * 6,
        out_shape=[
            wide(both, flat), wide(both, flat), wide(both, flat),
            jax.ShapeDtypeStruct((6 * both, flat), BF16),
            wide(groups, 6 * both, 2 * rows * entries),
            wide(groups, both, rows * entries),
        ],
        compiler_params=pltpu.CompilerParams(vmem_limit_bytes=8 * 1024 * 1024),
    )(
        x_new.reshape(both, flat), z_gate.reshape(both, flat),
        over_channels(dt_raw.reshape(both, heads)),
        jnp.moveaxis(b_in, 2, 0).reshape(groups, both, entries),
        jnp.moveaxis(c_in, 2, 0).reshape(groups, both, entries),
        over_channels(jnp.stack([a_rate, dt_bias, skip_d])),
    )


def decode_kernel(rows, groups, parts, info_ref, *refs):
    recv_refs, refs = refs[:groups * parts], refs[groups * parts:]
    (resident_ref, base_ref, carry_ref, gate_ref, left_ref, right_ref, seen_ref, gain_ref,
     decoded_ref, final_ref, state, ready, sem, out_sem) = refs
    pieces, span = recv_refs[0].shape[0] * parts, recv_refs[0].shape[2]
    block, entries = state.shape[1] // groups, state.shape[2]

    def each(g, r, act):
        listed = info_ref[r]
        mask = info_ref[rows + r]

        def piece(q):
            here = pl.ds(pl.multiple_of(g * block + q * span, 16), span)
            spot = q ^ mask
            for p in range(parts):
                recv_ref = recv_refs[g * parts + p]

                @pl.when((listed == 1) & ((spot == p) | (parts == 1)))
                def _():
                    act(pltpu.make_async_copy(
                        recv_ref.at[spot if parts == 1 else 0, r], state.at[r, here],
                        sem.at[g, r]))

        @pl.when(listed == 0)
        def _():
            here = pl.ds(g * block, block)
            act(pltpu.make_async_copy(
                resident_ref.at[r, here], state.at[r, here], sem.at[g, r]))

        if pieces <= 8:
            for q in range(pieces):
                piece(q)
        else:
            pl.loop(0, pieces)(piece)

    def result(g, r):
        here = pl.ds(g * block, block)
        return pltpu.make_async_copy(
            ready.at[r, here], final_ref.at[r, here], out_sem.at[g, r])

    for g in range(groups):
        for r in range(rows):
            each(g, r, lambda copy: copy.start())
    for g in range(groups):
        for r in range(rows):
            each(g, r, lambda copy: copy.wait())
        lanes = slice(g * block, (g + 1) * block)
        step = 256
        for first in range(g * block, (g + 1) * block, step):
            here = slice(first, first + step)
            moved = lax.dot_general(
                left_ref[:, here], right_ref[g], (((0,), (0,)), ((), ())),
                preferred_element_type=F32)
            for r in range(rows):
                at = 2 * r * entries
                ready[r, here] = (
                    moved[:, at + entries:at + 2 * entries] * state[r, here].astype(F32)
                    + moved[:, at:at + entries]).astype(BF16)
        for r in range(rows):
            result(g, r).start()
        initial = jnp.concatenate([state[r, lanes] for r in range(rows)], axis=1)
        seen = lax.dot_general(
            seen_ref[g], initial, (((1,), (1,)), ((), ())), preferred_element_type=F32)
        readout = carry_ref[:, lanes] * seen + base_ref[:, lanes]
        gated = readout * gate_ref[:, lanes]
        squares = jnp.mean(gated * gated, axis=1, keepdims=True)
        normed = gated * lax.rsqrt(squares + 1e-05) * gain_ref[:, lanes]
        decoded_ref[:, lanes] = normed.astype(BF16)
    for g in range(groups):
        for r in range(rows):
            result(g, r).wait()


def decode(info, recv, resident, ready, gain):
    rows, flat, entries = resident.shape
    groups, parts = len(recv), len(recv[0])
    return pl.pallas_call(
        functools.partial(decode_kernel, rows, groups, parts),
        in_specs=[SMEM] + [ANY] * (1 + groups * parts) + [VMEM] * 7,
        out_specs=[VMEM, ANY],
        scratch_shapes=[
            pltpu.VMEM((rows, flat, entries), BF16),
            pltpu.VMEM((rows, flat, entries), BF16),
            pltpu.SemaphoreType.DMA((groups, rows)),
            pltpu.SemaphoreType.DMA((groups, rows)),
        ],
        out_shape=[
            jax.ShapeDtypeStruct(ready[0].shape, BF16),
            jax.ShapeDtypeStruct((rows, flat, entries), BF16),
        ],
        compiler_params=pltpu.CompilerParams(vmem_limit_bytes=16 * 1024 * 1024),
    )(info, *[part for group in recv for part in group], resident, *ready, gain)


def local(
    prefill_states, src_slot, dst_slot, resident_states, x_new, z_gate, dt_raw, b_in, c_in,
    a_rate, dt_bias, skip_d, norm_gain,
):
    row_count, local_heads, channels, entries = resident_states.shape
    flat = local_heads * channels
    shards = lax.axis_size("rows")
    me = lax.axis_index("rows")
    quarter = shards // 2
    matches = jnp.arange(shards * row_count, dtype=jnp.int32)[:, None] == dst_slot[None, :]
    listed = jnp.any(matches, axis=1).astype(jnp.int32)
    source = jnp.sum(jnp.where(matches, src_slot[None, :], 0), axis=1)

    groups = local_heads // (HEADS // GROUPS)
    span = flat // quarter // groups
    half_rows = quarter * row_count
    halves = [[h * quarter + i for i in range(quarter)] for h in range(2)]

    def exchange(value, groups=None):
        return lax.all_to_all(
            value, "rows", split_axis=0, concat_axis=0, tiled=True, axis_index_groups=groups)

    def hand(value, k):
        return lax.ppermute(value, "rows", [(i, i ^ k) for i in range(shards)])

    pieces = prefill_states.reshape(groups, quarter, span, entries)
    here = jnp.arange(shards * row_count, dtype=jnp.int32) // row_count
    if shards == 8:
        held = jnp.stack([pieces[:, 0]] + [
            hand(pieces[:, k % quarter], k) for k in range(1, shards)])
        slots = source ^ me
        mask = (source ^ here) % quarter
    else:
        pieces = jnp.moveaxis(pieces, 0, 1)
        held = exchange(jnp.concatenate([pieces, pieces]).reshape(
            shards, groups * span, entries)).reshape(shards, groups, span, entries)
        slots = source
        mask = jnp.zeros_like(source)
    slots = lax.dynamic_slice_in_dim(slots, (me // quarter) * half_rows, half_rows)
    own = lax.dynamic_slice_in_dim(mask, me * row_count, row_count)
    recv = []
    if shards == 8:
        order = (jnp.arange(quarter)[:, None] ^ (me % quarter)) * row_count + jnp.arange(row_count)
        slots = slots[order.reshape(half_rows)]
    for g in range(groups):
        sent = gather_pieces(g, slots, held).reshape(quarter, row_count, span, entries)
        if shards == 8:
            recv.append([sent[:1]] + [hand(sent[k:k + 1], k) for k in range(1, quarter)])
        else:
            sent = exchange(sent.reshape(quarter, row_count * span, entries), halves)
            recv.append([sent.reshape(quarter, row_count, span, entries)])

    groups = local_heads // (HEADS // GROUPS)
    group_base = lax.axis_index("head") * groups
    ready = prepare(
        x_new, z_gate, dt_raw,
        lax.dynamic_slice_in_dim(b_in, group_base, groups, 2),
        lax.dynamic_slice_in_dim(c_in, group_base, groups, 2),
        a_rate, dt_bias, skip_d)
    info = jnp.concatenate([
        lax.dynamic_slice_in_dim(listed, me * row_count, row_count), own])
    decoded, final = decode(
        info, recv, resident_states.reshape(row_count, flat, entries), ready,
        norm_gain.reshape(1, flat))
    return (decoded.reshape(x_new.shape), final.reshape(resident_states.shape))


def solution(mesh):
    placed = (
        P(("parts", "rows"), "head", None, None),
        P("parts"),
        P("parts"),
        P(("parts", "rows"), "head", None, None),
        P(None, ("parts", "rows"), "head", None),
        P(None, ("parts", "rows"), "head", None),
        P(None, ("parts", "rows"), "head"),
        P(None, ("parts", "rows"), None, None),
        P(None, ("parts", "rows"), None, None),
        P("head"),
        P("head"),
        P("head"),
        P("head", None),
    )
    return jax.shard_map(
        local,
        mesh=mesh,
        in_specs=placed,
        out_specs=(
            P(None, ("parts", "rows"), "head", None),
            P(("parts", "rows"), "head", None, None),
        ),
        check_vma=False,
    )
```

time: 79.5 us -> 52.1 us (0.66)
  other arithmetic: 22.3 us -> 0.36 us
  waiting for transfers between devices: 37.5 us -> 18 us
  starting transfers between devices: 10.9 us -> 19.5 us
  Pallas kernels: 0 us -> 5.74 us
    all_to_all x2 -> x0, waiting for transfers between devices: 37.5 us -> none  [the longest x1 23.5 us: local(): lax.all_to_all(jnp.take(spread, source, axis=0), 'rows', split_axis=0, co...]
    ppermute x0 -> x13, starting transfers between devices: none -> 19.5 us  [hand(): return lax.ppermute(value, 'rows', [(i, i ^ k) for i in range(shards)])]
    ppermute x0 -> x13, waiting for transfers between devices: none -> 18 us  [hand(): return lax.ppermute(value, 'rows', [(i, i ^ k) for i in range(shards)])]
    unnamed x1 -> x0, other arithmetic: 11.5 us -> none
    all_to_all x2 -> x0, starting transfers between devices: 10.9 us -> none  [the longest x1 7.25 us: local(): lax.all_to_all(flat_slots, 'rows', split_axis=1, concat_axis=0, tiled=True)]
    reduce_sum x5 -> x0, other arithmetic: 7.24 us -> none  [the longest x3 6.83 us: advance(): jnp.sum(hidden_state * c_now[:, :, None, :], axis=-1)]
    pallas_call x0 -> x4, Pallas kernels: none -> 5.74 us  [the longest x1 4.36 us: decode(): pl.pallas_call(functools.partial(decode_kernel, rows, groups, parts), in_...]
    squeeze x0 -> x1, local copies, waits for them, and re-layouts: none -> 1.14 us  [local(): pieces[:, k % quarter]]
  transfers between devices with their start and end apart: 2 -> 13, of which waited for: 2 -> 7; matrix products, arithmetic and copies ran while one was open for 4% -> 7% of each run, Pallas kernels for 0% -> 0%
where the time goes in v2:
time: 52.1 us; the launch traced here: 51.8 us
  starting transfers between devices  19.5 us (37%)
  waiting for transfers between devices  18 us (35%)
  local copies, waits for them, and re-layouts  7.15 us (14%)
  Pallas kernels  5.74 us (11%)
  between operations  0.96 us (2%)
    ppermute x13, starting transfers between devices, hand(): return lax.ppermute(value, 'rows', [(i, i ^ k) for i in range(shards)])  19.5 us
    ppermute x13, waiting for transfers between devices, hand(): return lax.ppermute(value, 'rows', [(i, i ^ k) for i in range(shards)])  18 us
    pallas_call x1, Pallas kernels, decode(): pl.pallas_call(functools.partial(decode_kernel, rows, groups, parts), in_...  4.36 us
    unnamed x35, local copies, waits for them, and re-layouts  3.9 us
    pallas_call x2, Pallas kernels, gather_pieces(): pl.pallas_call(functools.partial(gather_kernel, group), in_specs=[SMEM, V...  1.16 us
    squeeze x1, local copies, waits for them, and re-layouts, local(): pieces[:, k % quarter]  1.14 us
  transfers between devices with their start and end apart: 13, of which 7 were waited for; matrix products, arithmetic and copies ran while one was open for 7% of the time, Pallas kernels for 0%

profile of v2, /device:TPU:0, one launch (start us, length us, event | category | flops | bytes accessed | tf_op | source)
XLA Modules:
  0.0 51.8 jit_solution(16278310414829233015)
XLA Ops:
  0.6 1.1 %slice_bitcast_fusion.11 = (bf16[2,256,128]{2,1,0:T(8,128)(2,1)S(1)}, bf16[2,256,128]{2,1,0:T(8,128)(2,1)S(1)}, bf16[2,256,128]{2,1,0:T(8,128)(2,1)S(1)}, bf16[2,256,128]{2,1,0:T(8,128)(2,1)S(1)}) fusion(bf16[2,4,256,128]{3,2,1,0:T(8,128)(2,1)} %bitcast.71), kind=kLoop, calls=%fused_computation.20 | loop fusion | bytes 1048576 | tf_op jit(solution)/shard_map/squeeze | solution.py:273
  1.8 3.0 %collective-permute-start = (bf16[2,256,128]{2,1,0:T(8,128)(2,1)S(1)}, bf16[2,256,128]{2,1,0:T(8,128)(2,1)S(1)}, u32[]{:S(2)}, u32[]{:S(2)}) collective-permute-start(bf16[2,256,128]{2,1,0:T(8,128)(2,1)S(1)} %get-tuple-element.34), channel_id=1, source_target_pairs={{0,2},{2,0},{4,6},{6,4},{8,10},{10,8},{12,14},{14,12},{1,3},{3,1},... | collective-permute-start | bytes 393224 | tf_op jit(solution)/shard_map/ppermute | solution.py:267
  4.8 2.6 %collective-permute-start.4 = (bf16[2,256,128]{2,1,0:T(8,128)(2,1)S(1)}, bf16[2,256,128]{2,1,0:T(8,128)(2,1)S(1)}, u32[]{:S(2)}, u32[]{:S(2)}) collective-permute-start(bf16[2,256,128]{2,1,0:T(8,128)(2,1)S(1)} %get-tuple-element.34), channel_id=1, source_target_pairs={{0,10},{2,8},{4,14},{6,12},{8,2},{10,0},{12,6},{14,4},{1,11},{3,9}... | collective-permute-start | bytes 393224 | tf_op jit(solution)/shard_map/ppermute | solution.py:267
  7.3 1.6 %collective-permute-start.1 = (bf16[2,256,128]{2,1,0:T(8,128)(2,1)S(1)}, bf16[2,256,128]{2,1,0:T(8,128)(2,1)S(1)}, u32[]{:S(2)}, u32[]{:S(2)}) collective-permute-start(bf16[2,256,128]{2,1,0:T(8,128)(2,1)S(1)} %get-tuple-element.33), channel_id=1, source_target_pairs={{0,4},{2,6},{4,0},{6,2},{8,12},{10,14},{12,8},{14,10},{1,5},{3,7},... | collective-permute-start | bytes 393224 | tf_op jit(solution)/shard_map/ppermute | solution.py:267
  8.9 1.8 %collective-permute-start.2 = (bf16[2,256,128]{2,1,0:T(8,128)(2,1)S(1)}, bf16[2,256,128]{2,1,0:T(8,128)(2,1)S(1)}, u32[]{:S(2)}, u32[]{:S(2)}) collective-permute-start(bf16[2,256,128]{2,1,0:T(8,128)(2,1)S(1)} %get-tuple-element.35), channel_id=1, source_target_pairs={{0,6},{2,4},{4,2},{6,0},{8,14},{10,12},{12,10},{14,8},{1,7},{3,5},... | collective-permute-start | bytes 393224 | tf_op jit(solution)/shard_map/ppermute | solution.py:267
  10.7 0.9 %bitcast_dynamic-update-slice_fusion = bf16[8,2,256,128]{3,2,1,0:T(8,128)(2,1)S(1)} fusion(bf16[2,4,256,128]{3,2,1,0:T(8,128)(2,1)} %bitcast.72), kind=kLoop, calls=%fused_computation.12 | loop fusion | bytes 262144
  11.7 0.6 %copy-done.10 = s32[8]{0:T(128)S(1)} copy-done((s32[8]{0:T(128)S(1)}, s32[8]{0:T(128)}, u32[]{:S(2)}) %copy-start.10) | copy-done | bytes 56
  12.3 0.1 select_reduce_fusion
  12.5 0.1 add.64
  12.6 0.5 copy-done.5
  13.2 0.1 dynamic_slice.17
  13.3 0.6 %gather_fusion = s32[8]{0:T(128)S(1)} fusion(s32[8]{0:T(128)S(1)} %dynamic_slice.17, s32[1024]{0:T(1024)S(1)} %pad_clamp_fusion), kind=kCustom, calls=%fused_computation | custom fusion | bytes 96 | tf_op jit(solution)/shard_map/gather | solution.py:287
  13.9 0.1 fusion
  14.0 3.0 %collective-permute-start.6 = (bf16[2,256,128]{2,1,0:T(8,128)(2,1)S(1)}, bf16[2,256,128]{2,1,0:T(8,128)(2,1)S(1)}, u32[]{:S(2)}, u32[]{:S(2)}) collective-permute-start(bf16[2,256,128]{2,1,0:T(8,128)(2,1)S(1)} %get-tuple-element.35), channel_id=1, source_target_pairs={{0,14},{2,12},{4,10},{6,8},{8,6},{10,4},{12,2},{14,0},{1,15},{3,13... | collective-permute-start | bytes 393224 | tf_op jit(solution)/shard_map/ppermute | solution.py:267
  17.0 0.6 %collective-permute-start.3 = (bf16[2,256,128]{2,1,0:T(8,128)(2,1)S(1)}, bf16[2,256,128]{2,1,0:T(8,128)(2,1)S(1)}, u32[]{:S(2)}, u32[]{:S(2)}) collective-permute-start(bf16[2,256,128]{2,1,0:T(8,128)(2,1)S(1)} %get-tuple-element.32), channel_id=1, source_target_pairs={{0,8},{2,10},{4,12},{6,14},{8,0},{10,2},{12,4},{14,6},{1,9},{3,11}... | collective-permute-start | bytes 393224 | tf_op jit(solution)/shard_map/ppermute | solution.py:267
  17.7 3.2 %collective-permute-done.2 = bf16[2,256,128]{2,1,0:T(8,128)(2,1)S(1)} collective-permute-done((bf16[2,256,128]{2,1,0:T(8,128)(2,1)S(1)}, bf16[2,256,128]{2,1,0:T(8,128)(2,1)S(1)}, u32[]{:S(2)}, u32[]{:S(2)}) %collective-permute-start.2) | collective-permute-done | bytes 131104 | tf_op jit(solution)/shard_map/ppermute | solution.py:267
  20.9 9.3 %collective-permute-done.3 = bf16[2,256,128]{2,1,0:T(8,128)(2,1)S(1)} collective-permute-done((bf16[2,256,128]{2,1,0:T(8,128)(2,1)S(1)}, bf16[2,256,128]{2,1,0:T(8,128)(2,1)S(1)}, u32[]{:S(2)}, u32[]{:S(2)}) %collective-permute-start.3) | collective-permute-done | bytes 131104 | tf_op jit(solution)/shard_map/ppermute | solution.py:267
  30.4 0.6 %shard_map.140 = bf16[8,256,128]{2,1,0:T(8,128)(2,1)S(1)} custom-call(s32[8]{0:T(128)S(1)} %gather_fusion, bf16[8,2,256,128]{3,2,1,0:T(8,128)(2,1)S(1)} %bitcast_dynamic-update-slice_fusion.1.held_ref), custom_call_target="tpu_custom_call" | custom-call | tf_op jit(solution)/shard_map/pallas_call | solution.py:33
  31.0 0.6 %shard_map.141 = bf16[8,256,128]{2,1,0:T(8,128)(2,1)S(1)} custom-call(s32[8]{0:T(128)S(1)} %gather_fusion, bf16[8,2,256,128]{3,2,1,0:T(8,128)(2,1)S(1)} %bitcast_dynamic-update-slice_fusion.1.held_ref), custom_call_target="tpu_custom_call" | custom-call | tf_op jit(solution)/shard_map/pallas_call | solution.py:33
  31.6 1.6 %collective-permute-start.7 = (bf16[1,2,256,128]{3,2,1,0:T(8,128)(2,1)S(1)}, bf16[1,2,256,128]{3,2,1,0:T(8,128)(2,1)S(1)}, u32[]{:S(2)}, u32[]{:S(2)}) collective-permute-start(bf16[1,2,256,128]{3,2,1,0:T(8,128)(2,1)S(1)} %get-tuple-element.30), channel_id=1, source_target_pairs={{0,2},{2,0},{4,6},{6,4},{8,10},{10,8},{12,14},{14,12},{1,3},{3,1},... | collective-permute-start | bytes 393224 | tf_op jit(solution)/shard_map/ppermute | solution.py:267
  33.2 0.7 %collective-permute-start.8 = (bf16[1,2,256,128]{3,2,1,0:T(8,128)(2,1)S(1)}, bf16[1,2,256,128]{3,2,1,0:T(8,128)(2,1)S(1)}, u32[]{:S(2)}, u32[]{:S(2)}) collective-permute-start(bf16[1,2,256,128]{3,2,1,0:T(8,128)(2,1)S(1)} %get-tuple-element.29), channel_id=1, source_target_pairs={{0,4},{2,6},{4,0},{6,2},{8,12},{10,14},{12,8},{14,10},{1,5},{3,7},... | collective-permute-start | bytes 393224 | tf_op jit(solution)/shard_map/ppermute | solution.py:267
  33.9 1.3 %collective-permute-start.9 = (bf16[1,2,256,128]{3,2,1,0:T(8,128)(2,1)S(1)}, bf16[1,2,256,128]{3,2,1,0:T(8,128)(2,1)S(1)}, u32[]{:S(2)}, u32[]{:S(2)}) collective-permute-start(bf16[1,2,256,128]{3,2,1,0:T(8,128)(2,1)S(1)} %get-tuple-element.28), channel_id=1, source_target_pairs={{0,6},{2,4},{4,2},{6,0},{8,14},{10,12},{12,10},{14,8},{1,7},{3,5},... | collective-permute-start | bytes 393224 | tf_op jit(solution)/shard_map/ppermute | solution.py:267
  35.2 1.6 %collective-permute-start.10 = (bf16[1,2,256,128]{3,2,1,0:T(8,128)(2,1)S(1)}, bf16[1,2,256,128]{3,2,1,0:T(8,128)(2,1)S(1)}, u32[]{:S(2)}, u32[]{:S(2)}) collective-permute-start(bf16[1,2,256,128]{3,2,1,0:T(8,128)(2,1)S(1)} %get-tuple-element.26), channel_id=1, source_target_pairs={{0,2},{2,0},{4,6},{6,4},{8,10},{10,8},{12,14},{14,12},{1,3},{3,1},... | collective-permute-start | bytes 393224 | tf_op jit(solution)/shard_map/ppermute | solution.py:267
  36.8 0.7 %collective-permute-start.11 = (bf16[1,2,256,128]{3,2,1,0:T(8,128)(2,1)S(1)}, bf16[1,2,256,128]{3,2,1,0:T(8,128)(2,1)S(1)}, u32[]{:S(2)}, u32[]{:S(2)}) collective-permute-start(bf16[1,2,256,128]{3,2,1,0:T(8,128)(2,1)S(1)} %get-tuple-element.25), channel_id=1, source_target_pairs={{0,4},{2,6},{4,0},{6,2},{8,12},{10,14},{12,8},{14,10},{1,5},{3,7},... | collective-permute-start | bytes 393224 | tf_op jit(solution)/shard_map/ppermute | solution.py:267
  37.5 0.2 collective-permute-done.7.refs_1_
  37.8 1.1 %collective-permute-start.12 = (bf16[1,2,256,128]{3,2,1,0:T(8,128)(2,1)S(1)}, bf16[1,2,256,128]{3,2,1,0:T(8,128)(2,1)S(1)}, u32[]{:S(2)}, u32[]{:S(2)}) collective-permute-start(bf16[1,2,256,128]{3,2,1,0:T(8,128)(2,1)S(1)} %get-tuple-element.24), channel_id=1, source_target_pairs={{0,6},{2,4},{4,2},{6,0},{8,14},{10,12},{12,10},{14,8},{1,7},{3,5},... | collective-permute-start | bytes 393224 | tf_op jit(solution)/shard_map/ppermute | solution.py:267
  38.9 0.1 dynamic_slice.16
  38.9 0.1 dynamic_slice.15
  39.0 0.1 copy.35
  39.1 0.2 reshape.90.x_ref
  39.3 0.1 copy.36
  39.5 0.2 reshape.91.z_ref
  39.6 0.1 broadcast_in_dim.34
  39.8 0.1 reshape.92.dt_ref
  40.0 0.1 broadcast_in_dim.35
  40.0 0.1 reshape.95.head_ref
  40.2 0.6 %copy-done.3 = f32[64,32]{0,1:T(8,128)S(1)} copy-done((f32[64,32]{0,1:T(8,128)S(1)}, f32[64,32]{0,1:T(8,128)}, u32[]{:S(2)}) %copy-start.3) | copy-done | bytes 8216
  40.8 0.1 copy.39
  40.8 0.1 reshape.96.refs_15_
  40.9 0.2 shard_map.142
  41.2 0.1 pad_add_fusion.info_ref
  41.2 0.9 %collective-permute-done.9.refs_3_ = bf16[1,2,256,128]{3,2,1,0:T(8,128)(2,1)S(1)} collective-permute-done((bf16[1,2,256,128]{3,2,1,0:T(8,128)(2,1)S(1)}, bf16[1,2,256,128]{3,2,1,0:T(8,128)(2,1)S(1)}, u32[]{:S(2)}, u32[]{:S(2)}) %collective-permute-start.9) | collective-permute-done | bytes 131104 | tf_op jit(solution)/shard_map/ppermute | solution.py:267
  42.2 0.5 collective-permute-done.10.refs_5_
  42.7 1.7 %collective-permute-done.11.refs_6_ = bf16[1,2,256,128]{3,2,1,0:T(8,128)(2,1)S(1)} collective-permute-done((bf16[1,2,256,128]{3,2,1,0:T(8,128)(2,1)S(1)}, bf16[1,2,256,128]{3,2,1,0:T(8,128)(2,1)S(1)}, u32[]{:S(2)}, u32[]{:S(2)}) %collective-permute-start.11) | collective-permute-done | bytes 131104 | tf_op jit(solution)/shard_map/ppermute | solution.py:267
  44.4 2.1 %collective-permute-done.12.refs_7_ = bf16[1,2,256,128]{3,2,1,0:T(8,128)(2,1)S(1)} collective-permute-done((bf16[1,2,256,128]{3,2,1,0:T(8,128)(2,1)S(1)}, bf16[1,2,256,128]{3,2,1,0:T(8,128)(2,1)S(1)}, u32[]{:S(2)}, u32[]{:S(2)}) %collective-permute-start.12) | collective-permute-done | bytes 131104 | tf_op jit(solution)/shard_map/ppermute | solution.py:267
  46.5 4.4 %shard_map.143 = (bf16[8,2048]{1,0:T(8,128)(2,1)S(1)}, bf16[2,2048,128]{2,1,0:T(8,128)(2,1)}) custom-call(s32[4]{0:T(128)S(1)} %pad_add_fusion.info_ref, bf16[1,2,256,128]{3,2,1,0:T(8,128)(2,1)S(1)} %get-tuple-element.31.refs_0_, bf16[1,2,256,128]{3,2,1,0:T(8,128)(2,1)S(1)} %collective-permute-done.7.refs_1_, ...), custom_call_target="tpu_custom_call" | custom-call | tf_op jit(solution)/shard_map/pallas_call | solution.py:226
  50.9 0.1 reshape.97
  51.0 0.7 %copy.40 = bf16[4,2,64,32]{2,3,1,0:T(8,128)(2,1)} copy(bf16[4,2,64,32]{3,2,1,0:T(8,128)(2,1)S(1)} %reshape.97) | data formatting | bytes 65536
  (47 shorter events, 0.5 us)
Async XLA Ops:
  1.8 12.2 %collective-permute-start = (bf16[2,256,128]{2,1,0:T(8,128)(2,1)S(1)}, bf16[2,256,128]{2,1,0:T(8,128)(2,1)S(1)}, u32[]{:S(2)}, u32[]{:S(2)}) collective-permute-start(bf16[2,256,128]{2,1,0:T(8,128)(2,1)S(1)} %get-tuple-element.34), channel_id=1, source_target_pairs={{0,2},{2,0},{4,6},{6,4},{8,10},{10,8},{12,14},{14,12},{1,3},{3,1},... | collective-permute-start | bytes 393224 | tf_op jit(solution)/shard_map/ppermute | solution.py:267
  4.8 25.5 %collective-permute-start.4 = (bf16[2,256,128]{2,1,0:T(8,128)(2,1)S(1)}, bf16[2,256,128]{2,1,0:T(8,128)(2,1)S(1)}, u32[]{:S(2)}, u32[]{:S(2)}) collective-permute-start(bf16[2,256,128]{2,1,0:T(8,128)(2,1)S(1)} %get-tuple-element.34), channel_id=1, source_target_pairs={{0,10},{2,8},{4,14},{6,12},{8,2},{10,0},{12,6},{14,4},{1,11},{3,9}... | collective-permute-start | bytes 393224 | tf_op jit(solution)/shard_map/ppermute | solution.py:267
  7.3 9.7 %collective-permute-start.1 = (bf16[2,256,128]{2,1,0:T(8,128)(2,1)S(1)}, bf16[2,256,128]{2,1,0:T(8,128)(2,1)S(1)}, u32[]{:S(2)}, u32[]{:S(2)}) collective-permute-start(bf16[2,256,128]{2,1,0:T(8,128)(2,1)S(1)} %get-tuple-element.33), channel_id=1, source_target_pairs={{0,4},{2,6},{4,0},{6,2},{8,12},{10,14},{12,8},{14,10},{1,5},{3,7},... | collective-permute-start | bytes 393224 | tf_op jit(solution)/shard_map/ppermute | solution.py:267
  8.9 21.4 %collective-permute-start.5 = (bf16[2,256,128]{2,1,0:T(8,128)(2,1)S(1)}, bf16[2,256,128]{2,1,0:T(8,128)(2,1)S(1)}, u32[]{:S(2)}, u32[]{:S(2)}) collective-permute-start(bf16[2,256,128]{2,1,0:T(8,128)(2,1)S(1)} %get-tuple-element.33), channel_id=1, source_target_pairs={{0,12},{2,14},{4,8},{6,10},{8,4},{10,6},{12,0},{14,2},{1,13},{3,15... | collective-permute-start | bytes 393224 | tf_op jit(solution)/shard_map/ppermute | solution.py:267
  8.9 12.0 %collective-permute-start.2 = (bf16[2,256,128]{2,1,0:T(8,128)(2,1)S(1)}, bf16[2,256,128]{2,1,0:T(8,128)(2,1)S(1)}, u32[]{:S(2)}, u32[]{:S(2)}) collective-permute-start(bf16[2,256,128]{2,1,0:T(8,128)(2,1)S(1)} %get-tuple-element.35), channel_id=1, source_target_pairs={{0,6},{2,4},{4,2},{6,0},{8,14},{10,12},{12,10},{14,8},{1,7},{3,5},... | collective-permute-start | bytes 393224 | tf_op jit(solution)/shard_map/ppermute | solution.py:267
  11.7 0.7 %copy-start.10 = (s32[8]{0:T(128)S(1)}, s32[8]{0:T(128)}, u32[]{:S(2)}) copy-start(s32[8]{0:T(128)} %param.14) | copy-start | bytes 100
  11.7 0.7 %copy-start.11 = (s32[8]{0:T(128)S(1)}, s32[8]{0:T(128)}, u32[]{:S(2)}) copy-start(s32[8]{0:T(128)} %param.15) | copy-start | bytes 100
  12.4 0.7 %copy-start.5 = (bf16[4,2,4,128]{3,2,1,0:T(4,128)(2,1)S(1)}, bf16[4,2,4,128]{3,2,1,0:T(4,128)(2,1)}, u32[]{:S(2)}) copy-start(bf16[4,2,4,128]{3,2,1,0:T(4,128)(2,1)} %param.21) | copy-start | bytes 24580
  12.4 0.7 %copy-start.6 = (bf16[4,2,4,128]{3,2,1,0:T(4,128)(2,1)S(1)}, bf16[4,2,4,128]{3,2,1,0:T(4,128)(2,1)}, u32[]{:S(2)}) copy-start(bf16[4,2,4,128]{3,2,1,0:T(4,128)(2,1)} %param.20) | copy-start | bytes 24580
  14.0 16.3 %collective-permute-start.6 = (bf16[2,256,128]{2,1,0:T(8,128)(2,1)S(1)}, bf16[2,256,128]{2,1,0:T(8,128)(2,1)S(1)}, u32[]{:S(2)}, u32[]{:S(2)}) collective-permute-start(bf16[2,256,128]{2,1,0:T(8,128)(2,1)S(1)} %get-tuple-element.35), channel_id=1, source_target_pairs={{0,14},{2,12},{4,10},{6,8},{8,6},{10,4},{12,2},{14,0},{1,15},{3,13... | collective-permute-start | bytes 393224 | tf_op jit(solution)/shard_map/ppermute | solution.py:267
  17.0 13.2 %collective-permute-start.3 = (bf16[2,256,128]{2,1,0:T(8,128)(2,1)S(1)}, bf16[2,256,128]{2,1,0:T(8,128)(2,1)S(1)}, u32[]{:S(2)}, u32[]{:S(2)}) collective-permute-start(bf16[2,256,128]{2,1,0:T(8,128)(2,1)S(1)} %get-tuple-element.32), channel_id=1, source_target_pairs={{0,8},{2,10},{4,12},{6,14},{8,0},{10,2},{12,4},{14,6},{1,9},{3,11}... | collective-permute-start | bytes 393224 | tf_op jit(solution)/shard_map/ppermute | solution.py:267
  31.6 6.2 %collective-permute-start.7 = (bf16[1,2,256,128]{3,2,1,0:T(8,128)(2,1)S(1)}, bf16[1,2,256,128]{3,2,1,0:T(8,128)(2,1)S(1)}, u32[]{:S(2)}, u32[]{:S(2)}) collective-permute-start(bf16[1,2,256,128]{3,2,1,0:T(8,128)(2,1)S(1)} %get-tuple-element.30), channel_id=1, source_target_pairs={{0,2},{2,0},{4,6},{6,4},{8,10},{10,8},{12,14},{14,12},{1,3},{3,1},... | collective-permute-start | bytes 393224 | tf_op jit(solution)/shard_map/ppermute | solution.py:267
  33.2 8.1 %collective-permute-start.8 = (bf16[1,2,256,128]{3,2,1,0:T(8,128)(2,1)S(1)}, bf16[1,2,256,128]{3,2,1,0:T(8,128)(2,1)S(1)}, u32[]{:S(2)}, u32[]{:S(2)}) collective-permute-start(bf16[1,2,256,128]{3,2,1,0:T(8,128)(2,1)S(1)} %get-tuple-element.29), channel_id=1, source_target_pairs={{0,4},{2,6},{4,0},{6,2},{8,12},{10,14},{12,8},{14,10},{1,5},{3,7},... | collective-permute-start | bytes 393224 | tf_op jit(solution)/shard_map/ppermute | solution.py:267
  33.9 8.3 %collective-permute-start.9 = (bf16[1,2,256,128]{3,2,1,0:T(8,128)(2,1)S(1)}, bf16[1,2,256,128]{3,2,1,0:T(8,128)(2,1)S(1)}, u32[]{:S(2)}, u32[]{:S(2)}) collective-permute-start(bf16[1,2,256,128]{3,2,1,0:T(8,128)(2,1)S(1)} %get-tuple-element.28), channel_id=1, source_target_pairs={{0,6},{2,4},{4,2},{6,0},{8,14},{10,12},{12,10},{14,8},{1,7},{3,5},... | collective-permute-start | bytes 393224 | tf_op jit(solution)/shard_map/ppermute | solution.py:267
  35.2 3.7 %copy-start.7 = (f32[64]{0:T(128)S(1)}, f32[64]{0:T(128)}, u32[]{:S(2)}) copy-start(f32[64]{0:T(128)} %param.24) | copy-start | bytes 772
  35.2 3.7 %copy-start.8 = (f32[64]{0:T(128)S(1)}, f32[64]{0:T(128)}, u32[]{:S(2)}) copy-start(f32[64]{0:T(128)} %param.23) | copy-start | bytes 772
  35.2 3.7 %copy-start.9 = (f32[64]{0:T(128)S(1)}, f32[64]{0:T(128)}, u32[]{:S(2)}) copy-start(f32[64]{0:T(128)} %param.22) | copy-start | bytes 772
  35.2 3.9 %copy-start.1 = (bf16[4,2,64,32]{2,3,1,0:T(8,128)(2,1)S(1)}, bf16[4,2,64,32]{2,3,1,0:T(8,128)(2,1)}, u32[]{:S(2)}) copy-start(bf16[4,2,64,32]{2,3,1,0:T(8,128)(2,1)} %param.17) | copy-start | bytes 98308
  35.2 4.2 %copy-start.2 = (bf16[4,2,64,32]{2,3,1,0:T(8,128)(2,1)S(1)}, bf16[4,2,64,32]{2,3,1,0:T(8,128)(2,1)}, u32[]{:S(2)}) copy-start(bf16[4,2,64,32]{2,3,1,0:T(8,128)(2,1)} %param.18) | copy-start | bytes 98308
  35.2 4.5 %copy-start.4 = (f32[4,2,64]{2,1,0:T(2,128)S(1)}, f32[4,2,64]{2,1,0:T(2,128)}, u32[]{:S(2)}) copy-start(f32[4,2,64]{2,1,0:T(2,128)} %param.19) | copy-start | bytes 6148
  35.2 11.3 %copy-start = (bf16[2,64,32,128]{3,2,1,0:T(8,128)(2,1)S(1)}, bf16[2,64,32,128]{3,2,1,0:T(8,128)(2,1)}, u32[]{:S(2)}) copy-start(bf16[2,64,32,128]{3,2,1,0:T(8,128)(2,1)} %param.16) | copy-start | bytes 3145732
  35.2 7.4 %collective-permute-start.10 = (bf16[1,2,256,128]{3,2,1,0:T(8,128)(2,1)S(1)}, bf16[1,2,256,128]{3,2,1,0:T(8,128)(2,1)S(1)}, u32[]{:S(2)}, u32[]{:S(2)}) collective-permute-start(bf16[1,2,256,128]{3,2,1,0:T(8,128)(2,1)S(1)} %get-tuple-element.26), channel_id=1, source_target_pairs={{0,2},{2,0},{4,6},{6,4},{8,10},{10,8},{12,14},{14,12},{1,3},{3,1},... | collective-permute-start | bytes 393224 | tf_op jit(solution)/shard_map/ppermute | solution.py:267
  36.8 7.6 %collective-permute-start.11 = (bf16[1,2,256,128]{3,2,1,0:T(8,128)(2,1)S(1)}, bf16[1,2,256,128]{3,2,1,0:T(8,128)(2,1)S(1)}, u32[]{:S(2)}, u32[]{:S(2)}) collective-permute-start(bf16[1,2,256,128]{3,2,1,0:T(8,128)(2,1)S(1)} %get-tuple-element.25), channel_id=1, source_target_pairs={{0,4},{2,6},{4,0},{6,2},{8,12},{10,14},{12,8},{14,10},{1,5},{3,7},... | collective-permute-start | bytes 393224 | tf_op jit(solution)/shard_map/ppermute | solution.py:267
  37.8 8.8 %collective-permute-start.12 = (bf16[1,2,256,128]{3,2,1,0:T(8,128)(2,1)S(1)}, bf16[1,2,256,128]{3,2,1,0:T(8,128)(2,1)S(1)}, u32[]{:S(2)}, u32[]{:S(2)}) collective-permute-start(bf16[1,2,256,128]{3,2,1,0:T(8,128)(2,1)S(1)} %get-tuple-element.24), channel_id=1, source_target_pairs={{0,6},{2,4},{4,2},{6,0},{8,14},{10,12},{12,10},{14,8},{1,7},{3,5},... | collective-permute-start | bytes 393224 | tf_op jit(solution)/shard_map/ppermute | solution.py:267
  40.0 0.7 %copy-start.3 = (f32[64,32]{0,1:T(8,128)S(1)}, f32[64,32]{0,1:T(8,128)}, u32[]{:S(2)}) copy-start(f32[64,32]{0,1:T(8,128)} %param.25) | copy-start | bytes 24580

commit v3 on v2

--- a/solution.py
+++ b/solution.py
@@ -16,25 +16,27 @@
 ANY = pl.BlockSpec(memory_space=pl.ANY)
 
 
-def gather_kernel(group, slots_ref, held_ref, out_ref):
-    count = out_ref.shape[0]
-
-    def one(i):
-        out_ref[i] = held_ref[slots_ref[i], group]
-
-    if count <= 16:
-        for i in range(count):
-            one(i)
-    else:
-        pl.loop(0, count)(one)
-
-
-def gather_pieces(group, slots, held):
+def gather_kernel(group, slots_ref, held_ref, *out_refs):
+    for k, out_ref in enumerate(out_refs):
+        rows = out_ref.shape[0]
+
+        def one(r):
+            out_ref[r] = held_ref[slots_ref[k * rows + r], group]
+
+        if rows <= 16:
+            for r in range(rows):
+                one(r)
+        else:
+            pl.loop(0, rows)(one)
+
+
+def gather_pieces(group, slots, held, parts):
+    shape = (slots.shape[0] // parts,) + held.shape[2:]
     return pl.pallas_call(
         functools.partial(gather_kernel, group),
         in_specs=[SMEM, VMEM],
-        out_specs=VMEM,
-        out_shape=jax.ShapeDtypeStruct(slots.shape + held.shape[2:], held.dtype),
+        out_specs=[VMEM] * parts,
+        out_shape=[jax.ShapeDtypeStruct(shape, held.dtype)] * parts,
         compiler_params=pltpu.CompilerParams(vmem_limit_bytes=4 * 1024 * 1024),
     )(slots, held)
 
@@ -147,98 +149,80 @@
     )
 
 
-def decode_kernel(rows, groups, parts, info_ref, *refs):
-    recv_refs, refs = refs[:groups * parts], refs[groups * parts:]
-    (resident_ref, base_ref, carry_ref, gate_ref, left_ref, right_ref, seen_ref, gain_ref,
-     decoded_ref, final_ref, state, ready, sem, out_sem) = refs
-    pieces, span = recv_refs[0].shape[0] * parts, recv_refs[0].shape[2]
-    block, entries = state.shape[1] // groups, state.shape[2]
-
-    def each(g, r, act):
-        listed = info_ref[r]
-        mask = info_ref[rows + r]
-
-        def piece(q):
-            here = pl.ds(pl.multiple_of(g * block + q * span, 16), span)
-            spot = q ^ mask
-            for p in range(parts):
-                recv_ref = recv_refs[g * parts + p]
-
-                @pl.when((listed == 1) & ((spot == p) | (parts == 1)))
-                def _():
-                    act(pltpu.make_async_copy(
-                        recv_ref.at[spot if parts == 1 else 0, r], state.at[r, here],
-                        sem.at[g, r]))
-
-        @pl.when(listed == 0)
-        def _():
-            here = pl.ds(g * block, block)
-            act(pltpu.make_async_copy(
-                resident_ref.at[r, here], state.at[r, here], sem.at[g, r]))
-
-        if pieces <= 8:
-            for q in range(pieces):
-                piece(q)
-        else:
-            pl.loop(0, pieces)(piece)
-
-    def result(g, r):
-        here = pl.ds(g * block, block)
+def decode_kernel(rows, group, parts, info_ref, *refs):
+    recv_refs, refs = refs[:parts], refs[parts:]
+    (resident_ref, base_ref, carry_ref, gate_ref, left_ref, right_ref, seen_ref,
+     gain_ref) = refs[:8]
+    decoded_ref, final_ref, ready, seen, out_sem = refs[-5:]
+    span, entries = recv_refs[0].shape[1:]
+    block = parts * span
+    start = group * block
+    lanes = slice(start, start + block)
+
+    def place(p, r):
+        return pl.multiple_of((info_ref[rows + r] ^ p) * span, span)
+
+    def result(p, r):
         return pltpu.make_async_copy(
-            ready.at[r, here], final_ref.at[r, here], out_sem.at[g, r])
-
-    for g in range(groups):
-        for r in range(rows):
-            each(g, r, lambda copy: copy.start())
-    for g in range(groups):
-        for r in range(rows):
-            each(g, r, lambda copy: copy.wait())
-        lanes = slice(g * block, (g + 1) * block)
-        step = 256
-        for first in range(g * block, (g + 1) * block, step):
-            here = slice(first, first + step)
+            ready.at[r, p], final_ref.at[r, pl.ds(start + place(p, r), span)],
+            out_sem.at[p, r])
+
+    for r in range(rows):
+        listed = info_ref[r] == 1
+        at = 2 * r * entries
+        for p in range(parts):
+            here = place(p, r)
+            initial = jnp.where(
+                listed, recv_refs[p][r], resident_ref[r, pl.ds(start + here, span)])
             moved = lax.dot_general(
-                left_ref[:, here], right_ref[g], (((0,), (0,)), ((), ())),
-                preferred_element_type=F32)
-            for r in range(rows):
-                at = 2 * r * entries
-                ready[r, here] = (
-                    moved[:, at + entries:at + 2 * entries] * state[r, here].astype(F32)
-                    + moved[:, at:at + entries]).astype(BF16)
-        for r in range(rows):
-            result(g, r).start()
-        initial = jnp.concatenate([state[r, lanes] for r in range(rows)], axis=1)
-        seen = lax.dot_general(
-            seen_ref[g], initial, (((1,), (1,)), ((), ())), preferred_element_type=F32)
-        readout = carry_ref[:, lanes] * seen + base_ref[:, lanes]
-        gated = readout * gate_ref[:, lanes]
-        squares = jnp.mean(gated * gated, axis=1, keepdims=True)
-        normed = gated * lax.rsqrt(squares + 1e-05) * gain_ref[:, lanes]
-        decoded_ref[:, lanes] = normed.astype(BF16)
-    for g in range(groups):
-        for r in range(rows):
-            result(g, r).wait()
-
-
-def decode(info, recv, resident, ready, gain):
+                left_ref[:, pl.ds(pl.multiple_of(start + here, span), span)],
+                right_ref[group, :, at:at + 2 * entries],
+                (((0,), (0,)), ((), ())), preferred_element_type=F32)
+            ready[r, p] = (
+                moved[:, entries:] * initial.astype(F32) + moved[:, :entries]).astype(BF16)
+            result(p, r).start()
+            part = lax.dot_general(
+                seen_ref[group, :, r * entries:(r + 1) * entries], initial,
+                (((1,), (1,)), ((), ())), preferred_element_type=F32)
+            seen[r, :, pl.ds(here, span)] = part
+    total = seen[0]
+    for r in range(1, rows):
+        total = total + seen[r]
+    readout = carry_ref[:, lanes] * total + base_ref[:, lanes]
+    gated = readout * gate_ref[:, lanes]
+    squares = jnp.mean(gated * gated, axis=1, keepdims=True)
+    normed = gated * lax.rsqrt(squares + 1e-05) * gain_ref[:, lanes]
+    if group:
+        decoded_ref[:, :start] = refs[8][...]
+    decoded_ref[:, lanes] = normed.astype(BF16)
+    for r in range(rows):
+        for p in range(parts):
+            result(p, r).wait()
+
+
+def decode(group, info, recv, resident, ready, gain, earlier):
     rows, flat, entries = resident.shape
-    groups, parts = len(recv), len(recv[0])
+    both = ready[0].shape[0]
+    groups = ready[4].shape[0]
+    block = flat // groups
+    parts, span = len(recv), block // len(recv)
+    count = 1 + parts + 1 + len(ready) + 1
     return pl.pallas_call(
-        functools.partial(decode_kernel, rows, groups, parts),
-        in_specs=[SMEM] + [ANY] * (1 + groups * parts) + [VMEM] * 7,
+        functools.partial(decode_kernel, rows, group, parts),
+        in_specs=[SMEM] + [VMEM] * (count - 1) + [VMEM, ANY][:len(earlier)],
         out_specs=[VMEM, ANY],
+        input_output_aliases={count + 1: 1} if earlier else {},
         scratch_shapes=[
-            pltpu.VMEM((rows, flat, entries), BF16),
-            pltpu.VMEM((rows, flat, entries), BF16),
-            pltpu.SemaphoreType.DMA((groups, rows)),
-            pltpu.SemaphoreType.DMA((groups, rows)),
+            pltpu.VMEM((rows, parts, span, entries), BF16),
+            pltpu.VMEM((rows, both, block), F32),
+            pltpu.SemaphoreType.DMA((parts, rows)),
         ],
         out_shape=[
-            jax.ShapeDtypeStruct(ready[0].shape, BF16),
+            jax.ShapeDtypeStruct((both, (group + 1) * block), BF16),
             jax.ShapeDtypeStruct((rows, flat, entries), BF16),
         ],
         compiler_params=pltpu.CompilerParams(vmem_limit_bytes=16 * 1024 * 1024),
-    )(info, *[part for group in recv for part in group], resident, *ready, gain)
+    )(info, *recv, resident, *ready, gain, *earlier)
 
 
 def local(
@@ -268,30 +252,32 @@
 
     pieces = prefill_states.reshape(groups, quarter, span, entries)
     here = jnp.arange(shards * row_count, dtype=jnp.int32) // row_count
-    if shards == 8:
-        held = jnp.stack([pieces[:, 0]] + [
-            hand(pieces[:, k % quarter], k) for k in range(1, shards)])
-        slots = source ^ me
+    few = shards == 8
+    recv = []
+    if few:
+        arrived = [pieces[:, 0]] + [
+            hand(pieces[:, k % quarter], k) for k in range(1, shards)]
+        held = jnp.stack(arrived)
+        order = jnp.arange(quarter)[:, None] ^ (me % quarter)
+        order = (order * row_count + jnp.arange(row_count)).reshape(half_rows)
+        slots = lax.dynamic_slice_in_dim(
+            source ^ me, (me // quarter) * half_rows, half_rows)[order]
+        for g in range(groups):
+            sent = gather_pieces(g, slots, held, quarter)
+            recv.append([sent[0]] + [hand(sent[k], k) for k in range(1, quarter)])
         mask = (source ^ here) % quarter
     else:
         pieces = jnp.moveaxis(pieces, 0, 1)
         held = exchange(jnp.concatenate([pieces, pieces]).reshape(
             shards, groups * span, entries)).reshape(shards, groups, span, entries)
-        slots = source
+        slots = lax.dynamic_slice_in_dim(source, (me // quarter) * half_rows, half_rows)
+        for g in range(groups):
+            sent, = gather_pieces(g, slots, held, 1)
+            sent = exchange(sent.reshape(quarter, row_count * span, entries), halves)
+            sent = jnp.moveaxis(sent.reshape(quarter, row_count, span, entries), 1, 0)
+            sent = sent.reshape(row_count, 4, quarter * span // 4, entries)
+            recv.append([sent[:, p] for p in range(4)])
         mask = jnp.zeros_like(source)
-    slots = lax.dynamic_slice_in_dim(slots, (me // quarter) * half_rows, half_rows)
-    own = lax.dynamic_slice_in_dim(mask, me * row_count, row_count)
-    recv = []
-    if shards == 8:
-        order = (jnp.arange(quarter)[:, None] ^ (me % quarter)) * row_count + jnp.arange(row_count)
-        slots = slots[order.reshape(half_rows)]
-    for g in range(groups):
-        sent = gather_pieces(g, slots, held).reshape(quarter, row_count, span, entries)
-        if shards == 8:
-            recv.append([sent[:1]] + [hand(sent[k:k + 1], k) for k in range(1, quarter)])
-        else:
-            sent = exchange(sent.reshape(quarter, row_count * span, entries), halves)
-            recv.append([sent.reshape(quarter, row_count, span, entries)])
 
     groups = local_heads // (HEADS // GROUPS)
     group_base = lax.axis_index("head") * groups
@@ -301,10 +287,13 @@
         lax.dynamic_slice_in_dim(c_in, group_base, groups, 2),
         a_rate, dt_bias, skip_d)
     info = jnp.concatenate([
-        lax.dynamic_slice_in_dim(listed, me * row_count, row_count), own])
-    decoded, final = decode(
-        info, recv, resident_states.reshape(row_count, flat, entries), ready,
-        norm_gain.reshape(1, flat))
+        lax.dynamic_slice_in_dim(listed, me * row_count, row_count),
+        lax.dynamic_slice_in_dim(mask, me * row_count, row_count)])
+    resident = resident_states.reshape(row_count, flat, entries)
+    outs = ()
+    for g in range(groups):
+        outs = decode(g, info, recv[g], resident, ready, norm_gain.reshape(1, flat), outs)
+    decoded, final = outs
     return (decoded.reshape(x_new.shape), final.reshape(resident_states.shape))
 
 

time: 52.1 us -> 49.6 us (0.952)
  waiting for transfers between devices: 18 us -> 17 us
  Pallas kernels: 5.74 us -> 4.92 us
  local copies, waits for them, and re-layouts: 7.15 us -> 6.59 us
    ppermute x13, waiting for transfers between devices: 18 us -> 17 us  [hand(): return lax.ppermute(value, 'rows', [(i, i ^ k) for i in range(shards)])]
    pallas_call x1 -> x2, Pallas kernels: 4.36 us -> 3.54 us  [decode(): pl.pallas_call(functools.partial(decode_kernel, rows, group, parts), in_s...]
  transfers between devices with their start and end apart: 13 -> 13, of which waited for: 7 -> 6; matrix products, arithmetic and copies ran while one was open for 7% -> 7% of each run, Pallas kernels for 0% -> 5%
where the time goes in v3:
time: 49.6 us; the launch traced here: 49.4 us
  starting transfers between devices  19.5 us (39%)
  waiting for transfers between devices  17 us (34%)
  local copies, waits for them, and re-layouts  6.59 us (13%)
  Pallas kernels  4.92 us (10%)
  between operations  0.95 us (2%)
    ppermute x13, starting transfers between devices, hand(): return lax.ppermute(value, 'rows', [(i, i ^ k) for i in range(shards)])  19.5 us
    ppermute x13, waiting for transfers between devices, hand(): return lax.ppermute(value, 'rows', [(i, i ^ k) for i in range(shards)])  17 us
    pallas_call x2, Pallas kernels, decode(): pl.pallas_call(functools.partial(decode_kernel, rows, group, parts), in_s...  3.54 us
    unnamed x35, local copies, waits for them, and re-layouts  3.42 us
    pallas_call x2, Pallas kernels, gather_pieces(): pl.pallas_call(functools.partial(gather_kernel, group), in_specs=[SMEM, V...  1.16 us
    squeeze x1, local copies, waits for them, and re-layouts, local(): pieces[:, k % quarter]  1.14 us
  transfers between devices with their start and end apart: 13, of which 6 were waited for; matrix products, arithmetic and copies ran while one was open for 7% of the time, Pallas kernels for 5%

profile of v3, /device:TPU:0, one launch (start us, length us, event | category | flops | bytes accessed | tf_op | source)
XLA Modules:
  0.0 49.4 jit_solution(8525785597652838746)
XLA Ops:
  0.6 1.1 %slice_bitcast_fusion.3 = (bf16[2,256,128]{2,1,0:T(8,128)(2,1)S(1)}, bf16[2,256,128]{2,1,0:T(8,128)(2,1)S(1)}, bf16[2,256,128]{2,1,0:T(8,128)(2,1)S(1)}, bf16[2,256,128]{2,1,0:T(8,128)(2,1)S(1)}) fusion(bf16[2,4,256,128]{3,2,1,0:T(8,128)(2,1)} %bitcast.57), kind=kLoop, calls=%fused_computation.12 | loop fusion | bytes 1048576 | tf_op jit(solution)/shard_map/squeeze | solution.py:259
  1.8 3.0 %collective-permute-start = (bf16[2,256,128]{2,1,0:T(8,128)(2,1)S(1)}, bf16[2,256,128]{2,1,0:T(8,128)(2,1)S(1)}, u32[]{:S(2)}, u32[]{:S(2)}) collective-permute-start(bf16[2,256,128]{2,1,0:T(8,128)(2,1)S(1)} %get-tuple-element.46), channel_id=1, source_target_pairs={{0,2},{2,0},{4,6},{6,4},{8,10},{10,8},{12,14},{14,12},{1,3},{3,1},... | collective-permute-start | bytes 393224 | tf_op jit(solution)/shard_map/ppermute | solution.py:251
  4.8 2.6 %collective-permute-start.4 = (bf16[2,256,128]{2,1,0:T(8,128)(2,1)S(1)}, bf16[2,256,128]{2,1,0:T(8,128)(2,1)S(1)}, u32[]{:S(2)}, u32[]{:S(2)}) collective-permute-start(bf16[2,256,128]{2,1,0:T(8,128)(2,1)S(1)} %get-tuple-element.46), channel_id=1, source_target_pairs={{0,10},{2,8},{4,14},{6,12},{8,2},{10,0},{12,6},{14,4},{1,11},{3,9}... | collective-permute-start | bytes 393224 | tf_op jit(solution)/shard_map/ppermute | solution.py:251
  7.3 1.6 %collective-permute-start.1 = (bf16[2,256,128]{2,1,0:T(8,128)(2,1)S(1)}, bf16[2,256,128]{2,1,0:T(8,128)(2,1)S(1)}, u32[]{:S(2)}, u32[]{:S(2)}) collective-permute-start(bf16[2,256,128]{2,1,0:T(8,128)(2,1)S(1)} %get-tuple-element.45), channel_id=1, source_target_pairs={{0,4},{2,6},{4,0},{6,2},{8,12},{10,14},{12,8},{14,10},{1,5},{3,7},... | collective-permute-start | bytes 393224 | tf_op jit(solution)/shard_map/ppermute | solution.py:251
  8.9 1.8 %collective-permute-start.2 = (bf16[2,256,128]{2,1,0:T(8,128)(2,1)S(1)}, bf16[2,256,128]{2,1,0:T(8,128)(2,1)S(1)}, u32[]{:S(2)}, u32[]{:S(2)}) collective-permute-start(bf16[2,256,128]{2,1,0:T(8,128)(2,1)S(1)} %get-tuple-element.47), channel_id=1, source_target_pairs={{0,6},{2,4},{4,2},{6,0},{8,14},{10,12},{12,10},{14,8},{1,7},{3,5},... | collective-permute-start | bytes 393224 | tf_op jit(solution)/shard_map/ppermute | solution.py:251
  10.7 0.1 iota_add_fusion
  10.8 0.1 add.64
  11.0 0.6 %copy-done.10 = s32[8]{0:T(128)S(1)} copy-done((s32[8]{0:T(128)S(1)}, s32[8]{0:T(128)}, u32[]{:S(2)}) %copy-start.10) | copy-done | bytes 56
  11.6 0.1 select_reduce_fusion
  11.7 0.1 dynamic_slice.17
  11.8 0.6 %gather_fusion = s32[8]{0:T(128)S(1)} fusion(s32[8]{0:T(128)S(1)} %dynamic_slice.17, s32[1024]{0:T(1024)S(1)} %pad_clamp_fusion), kind=kCustom, calls=%fused_computation | custom fusion | bytes 96 | tf_op jit(solution)/shard_map/gather | solution.py:263
  12.4 0.9 %bitcast_dynamic-update-slice_fusion = bf16[8,2,256,128]{3,2,1,0:T(8,128)(2,1)S(1)} fusion(bf16[2,4,256,128]{3,2,1,0:T(8,128)(2,1)} %bitcast.58), kind=kLoop, calls=%fused_computation.4 | loop fusion | bytes 262144
  13.4 3.0 %collective-permute-start.6 = (bf16[2,256,128]{2,1,0:T(8,128)(2,1)S(1)}, bf16[2,256,128]{2,1,0:T(8,128)(2,1)S(1)}, u32[]{:S(2)}, u32[]{:S(2)}) collective-permute-start(bf16[2,256,128]{2,1,0:T(8,128)(2,1)S(1)} %get-tuple-element.47), channel_id=1, source_target_pairs={{0,14},{2,12},{4,10},{6,8},{8,6},{10,4},{12,2},{14,0},{1,15},{3,13... | collective-permute-start | bytes 393224 | tf_op jit(solution)/shard_map/ppermute | solution.py:251
  16.4 0.2 collective-permute-done.1
  16.6 0.5 collective-permute-start.3
  17.1 3.9 %collective-permute-done.2 = bf16[2,256,128]{2,1,0:T(8,128)(2,1)S(1)} collective-permute-done((bf16[2,256,128]{2,1,0:T(8,128)(2,1)S(1)}, bf16[2,256,128]{2,1,0:T(8,128)(2,1)S(1)}, u32[]{:S(2)}, u32[]{:S(2)}) %collective-permute-start.2) | collective-permute-done | bytes 131104 | tf_op jit(solution)/shard_map/ppermute | solution.py:251
  20.9 9.3 %collective-permute-done.3 = bf16[2,256,128]{2,1,0:T(8,128)(2,1)S(1)} collective-permute-done((bf16[2,256,128]{2,1,0:T(8,128)(2,1)S(1)}, bf16[2,256,128]{2,1,0:T(8,128)(2,1)S(1)}, u32[]{:S(2)}, u32[]{:S(2)}) %collective-permute-start.3) | collective-permute-done | bytes 131104 | tf_op jit(solution)/shard_map/ppermute | solution.py:251
  30.4 0.6 %shard_map.142 = (bf16[2,256,128]{2,1,0:T(8,128)(2,1)S(1)}, bf16[2,256,128]{2,1,0:T(8,128)(2,1)S(1)}, bf16[2,256,128]{2,1,0:T(8,128)(2,1)S(1)}, bf16[2,256,128]{2,1,0:T(8,128)(2,1)S(1)}) custom-call(s32[8]{0:T(128)S(1)} %gather_fusion, bf16[8,2,256,128]{3,2,1,0:T(8,128)(2,1)S(1)} %bitcast_dynamic-update-slice_fusion.1.held_ref), custom_call_target="tpu_custom_call" | custom-call | tf_op jit(solution)/shard_map/pallas_call | solution.py:35
  31.0 1.6 %collective-permute-start.10 = (bf16[2,256,128]{2,1,0:T(8,128)(2,1)S(1)}, bf16[2,256,128]{2,1,0:T(8,128)(2,1)S(1)}, u32[]{:S(2)}, u32[]{:S(2)}) collective-permute-start(bf16[2,256,128]{2,1,0:T(8,128)(2,1)S(1)} %get-tuple-element.31), channel_id=1, source_target_pairs={{0,2},{2,0},{4,6},{6,4},{8,10},{10,8},{12,14},{14,12},{1,3},{3,1},... | collective-permute-start | bytes 393224 | tf_op jit(solution)/shard_map/ppermute | solution.py:251
  32.6 0.1 fusion
  32.7 0.6 %shard_map.140 = (bf16[2,256,128]{2,1,0:T(8,128)(2,1)S(1)}, bf16[2,256,128]{2,1,0:T(8,128)(2,1)S(1)}, bf16[2,256,128]{2,1,0:T(8,128)(2,1)S(1)}, bf16[2,256,128]{2,1,0:T(8,128)(2,1)S(1)}) custom-call(s32[8]{0:T(128)S(1)} %gather_fusion, bf16[8,2,256,128]{3,2,1,0:T(8,128)(2,1)S(1)} %bitcast_dynamic-update-slice_fusion.1.held_ref), custom_call_target="tpu_custom_call" | custom-call | tf_op jit(solution)/shard_map/pallas_call | solution.py:35
  33.3 0.8 %collective-permute-start.11 = (bf16[2,256,128]{2,1,0:T(8,128)(2,1)S(1)}, bf16[2,256,128]{2,1,0:T(8,128)(2,1)S(1)}, u32[]{:S(2)}, u32[]{:S(2)}) collective-permute-start(bf16[2,256,128]{2,1,0:T(8,128)(2,1)S(1)} %get-tuple-element.32), channel_id=1, source_target_pairs={{0,4},{2,6},{4,0},{6,2},{8,12},{10,14},{12,8},{14,10},{1,5},{3,7},... | collective-permute-start | bytes 393224 | tf_op jit(solution)/shard_map/ppermute | solution.py:251
  34.1 1.3 %collective-permute-start.12 = (bf16[2,256,128]{2,1,0:T(8,128)(2,1)S(1)}, bf16[2,256,128]{2,1,0:T(8,128)(2,1)S(1)}, u32[]{:S(2)}, u32[]{:S(2)}) collective-permute-start(bf16[2,256,128]{2,1,0:T(8,128)(2,1)S(1)} %get-tuple-element.33), channel_id=1, source_target_pairs={{0,6},{2,4},{4,2},{6,0},{8,14},{10,12},{12,10},{14,8},{1,7},{3,5},... | collective-permute-start | bytes 393224 | tf_op jit(solution)/shard_map/ppermute | solution.py:251
  35.4 1.5 %collective-permute-start.7 = (bf16[2,256,128]{2,1,0:T(8,128)(2,1)S(1)}, bf16[2,256,128]{2,1,0:T(8,128)(2,1)S(1)}, u32[]{:S(2)}, u32[]{:S(2)}) collective-permute-start(bf16[2,256,128]{2,1,0:T(8,128)(2,1)S(1)} %get-tuple-element.21), channel_id=1, source_target_pairs={{0,2},{2,0},{4,6},{6,4},{8,10},{10,8},{12,14},{14,12},{1,3},{3,1},... | collective-permute-start | bytes 393224 | tf_op jit(solution)/shard_map/ppermute | solution.py:251
  36.9 0.7 %collective-permute-start.8 = (bf16[2,256,128]{2,1,0:T(8,128)(2,1)S(1)}, bf16[2,256,128]{2,1,0:T(8,128)(2,1)S(1)}, u32[]{:S(2)}, u32[]{:S(2)}) collective-permute-start(bf16[2,256,128]{2,1,0:T(8,128)(2,1)S(1)} %get-tuple-element.22), channel_id=1, source_target_pairs={{0,4},{2,6},{4,0},{6,2},{8,12},{10,14},{12,8},{14,10},{1,5},{3,7},... | collective-permute-start | bytes 393224 | tf_op jit(solution)/shard_map/ppermute | solution.py:251
  37.6 1.3 %collective-permute-start.9 = (bf16[2,256,128]{2,1,0:T(8,128)(2,1)S(1)}, bf16[2,256,128]{2,1,0:T(8,128)(2,1)S(1)}, u32[]{:S(2)}, u32[]{:S(2)}) collective-permute-start(bf16[2,256,128]{2,1,0:T(8,128)(2,1)S(1)} %get-tuple-element.23), channel_id=1, source_target_pairs={{0,6},{2,4},{4,2},{6,0},{8,14},{10,12},{12,10},{14,8},{1,7},{3,5},... | collective-permute-start | bytes 393224 | tf_op jit(solution)/shard_map/ppermute | solution.py:251
  38.9 0.1 dynamic_slice.16
  39.0 0.1 dynamic_slice.15
  39.1 0.1 broadcast_in_dim.34
  39.2 0.1 reshape.83.dt_ref
  39.4 0.1 copy.36
  39.5 0.2 reshape.81.x_ref
  39.7 0.1 copy.37
  39.8 0.2 reshape.82.z_ref
  40.0 0.1 broadcast_in_dim.35
  40.1 0.1 reshape.86.head_ref
  40.2 0.6 %copy-done.3 = f32[64,32]{0,1:T(8,128)S(1)} copy-done((f32[64,32]{0,1:T(8,128)S(1)}, f32[64,32]{0,1:T(8,128)}, u32[]{:S(2)}) %copy-start.3) | copy-done | bytes 8216
  40.8 0.1 copy.40
  40.9 0.1 reshape.87.refs_11_
  41.0 0.2 shard_map.141
  41.2 0.1 pad_add_fusion.info_ref
  41.3 1.1 %collective-permute-done.12.refs_3_ = bf16[2,256,128]{2,1,0:T(8,128)(2,1)S(1)} collective-permute-done((bf16[2,256,128]{2,1,0:T(8,128)(2,1)S(1)}, bf16[2,256,128]{2,1,0:T(8,128)(2,1)S(1)}, u32[]{:S(2)}, u32[]{:S(2)}) %collective-permute-start.12) | collective-permute-done | bytes 131104 | tf_op jit(solution)/shard_map/ppermute | solution.py:251
  42.4 1.8 %shard_map.143 = (bf16[8,1024]{1,0:T(8,128)(2,1)S(1)}, bf16[2,2048,128]{2,1,0:T(8,128)(2,1)}) custom-call(s32[4]{0:T(128)S(1)} %pad_add_fusion.info_ref, bf16[2,256,128]{2,1,0:T(8,128)(2,1)S(1)} %get-tuple-element.30.refs_0_, bf16[2,256,128]{2,1,0:T(8,128)(2,1)S(1)} %collective-permute-done.10.refs_1_, ...), custom_call_target="tpu_custom_call" | custom-call | tf_op jit(solution)/shard_map/pallas_call | solution.py:210
  44.2 0.4 collective-permute-done.8.refs_2_
  44.6 2.2 %collective-permute-done.9.refs_3_ = bf16[2,256,128]{2,1,0:T(8,128)(2,1)S(1)} collective-permute-done((bf16[2,256,128]{2,1,0:T(8,128)(2,1)S(1)}, bf16[2,256,128]{2,1,0:T(8,128)(2,1)S(1)}, u32[]{:S(2)}, u32[]{:S(2)}) %collective-permute-start.9) | collective-permute-done | bytes 131104 | tf_op jit(solution)/shard_map/ppermute | solution.py:251
  46.7 1.8 %shard_map.144 = (bf16[8,2048]{1,0:T(8,128)(2,1)S(1)}, bf16[2,2048,128]{2,1,0:T(8,128)(2,1)}) custom-call(s32[4]{0:T(128)S(1)} %pad_add_fusion.info_ref, bf16[2,256,128]{2,1,0:T(8,128)(2,1)S(1)} %get-tuple-element.20.refs_0_, bf16[2,256,128]{2,1,0:T(8,128)(2,1)S(1)} %collective-permute-done.7.refs_1_, ...), custom_call_target="tpu_custom_call", output_to_operand_aliasing={{1}: (14, {})} | custom-call | tf_op jit(solution)/shard_map/pallas_call | solution.py:210
  48.5 0.1 reshape.88
  48.7 0.7 %copy.41 = bf16[4,2,64,32]{2,3,1,0:T(8,128)(2,1)} copy(bf16[4,2,64,32]{3,2,1,0:T(8,128)(2,1)S(1)} %reshape.88) | data formatting | bytes 65536
  (46 shorter events, 0.3 us)
Async XLA Ops:
  1.8 11.6 %collective-permute-start = (bf16[2,256,128]{2,1,0:T(8,128)(2,1)S(1)}, bf16[2,256,128]{2,1,0:T(8,128)(2,1)S(1)}, u32[]{:S(2)}, u32[]{:S(2)}) collective-permute-start(bf16[2,256,128]{2,1,0:T(8,128)(2,1)S(1)} %get-tuple-element.46), channel_id=1, source_target_pairs={{0,2},{2,0},{4,6},{6,4},{8,10},{10,8},{12,14},{14,12},{1,3},{3,1},... | collective-permute-start | bytes 393224 | tf_op jit(solution)/shard_map/ppermute | solution.py:251
  4.8 25.5 %collective-permute-start.4 = (bf16[2,256,128]{2,1,0:T(8,128)(2,1)S(1)}, bf16[2,256,128]{2,1,0:T(8,128)(2,1)S(1)}, u32[]{:S(2)}, u32[]{:S(2)}) collective-permute-start(bf16[2,256,128]{2,1,0:T(8,128)(2,1)S(1)} %get-tuple-element.46), channel_id=1, source_target_pairs={{0,10},{2,8},{4,14},{6,12},{8,2},{10,0},{12,6},{14,4},{1,11},{3,9}... | collective-permute-start | bytes 393224 | tf_op jit(solution)/shard_map/ppermute | solution.py:251
  7.3 9.2 %collective-permute-start.1 = (bf16[2,256,128]{2,1,0:T(8,128)(2,1)S(1)}, bf16[2,256,128]{2,1,0:T(8,128)(2,1)S(1)}, u32[]{:S(2)}, u32[]{:S(2)}) collective-permute-start(bf16[2,256,128]{2,1,0:T(8,128)(2,1)S(1)} %get-tuple-element.45), channel_id=1, source_target_pairs={{0,4},{2,6},{4,0},{6,2},{8,12},{10,14},{12,8},{14,10},{1,5},{3,7},... | collective-permute-start | bytes 393224 | tf_op jit(solution)/shard_map/ppermute | solution.py:251
  8.9 21.4 %collective-permute-start.5 = (bf16[2,256,128]{2,1,0:T(8,128)(2,1)S(1)}, bf16[2,256,128]{2,1,0:T(8,128)(2,1)S(1)}, u32[]{:S(2)}, u32[]{:S(2)}) collective-permute-start(bf16[2,256,128]{2,1,0:T(8,128)(2,1)S(1)} %get-tuple-element.45), channel_id=1, source_target_pairs={{0,12},{2,14},{4,8},{6,10},{8,4},{10,6},{12,0},{14,2},{1,13},{3,15... | collective-permute-start | bytes 393224 | tf_op jit(solution)/shard_map/ppermute | solution.py:251
  8.9 12.0 %collective-permute-start.2 = (bf16[2,256,128]{2,1,0:T(8,128)(2,1)S(1)}, bf16[2,256,128]{2,1,0:T(8,128)(2,1)S(1)}, u32[]{:S(2)}, u32[]{:S(2)}) collective-permute-start(bf16[2,256,128]{2,1,0:T(8,128)(2,1)S(1)} %get-tuple-element.47), channel_id=1, source_target_pairs={{0,6},{2,4},{4,2},{6,0},{8,14},{10,12},{12,10},{14,8},{1,7},{3,5},... | collective-permute-start | bytes 393224 | tf_op jit(solution)/shard_map/ppermute | solution.py:251
  10.9 0.7 %copy-start.10 = (s32[8]{0:T(128)S(1)}, s32[8]{0:T(128)}, u32[]{:S(2)}) copy-start(s32[8]{0:T(128)} %param.14) | copy-start | bytes 100
  11.0 0.7 %copy-start.11 = (s32[8]{0:T(128)S(1)}, s32[8]{0:T(128)}, u32[]{:S(2)}) copy-start(s32[8]{0:T(128)} %param.15) | copy-start | bytes 100
  13.4 17.0 %collective-permute-start.6 = (bf16[2,256,128]{2,1,0:T(8,128)(2,1)S(1)}, bf16[2,256,128]{2,1,0:T(8,128)(2,1)S(1)}, u32[]{:S(2)}, u32[]{:S(2)}) collective-permute-start(bf16[2,256,128]{2,1,0:T(8,128)(2,1)S(1)} %get-tuple-element.47), channel_id=1, source_target_pairs={{0,14},{2,12},{4,10},{6,8},{8,6},{10,4},{12,2},{14,0},{1,15},{3,13... | collective-permute-start | bytes 393224 | tf_op jit(solution)/shard_map/ppermute | solution.py:251
  16.6 13.7 %collective-permute-start.3 = (bf16[2,256,128]{2,1,0:T(8,128)(2,1)S(1)}, bf16[2,256,128]{2,1,0:T(8,128)(2,1)S(1)}, u32[]{:S(2)}, u32[]{:S(2)}) collective-permute-start(bf16[2,256,128]{2,1,0:T(8,128)(2,1)S(1)} %get-tuple-element.44), channel_id=1, source_target_pairs={{0,8},{2,10},{4,12},{6,14},{8,0},{10,2},{12,4},{14,6},{1,9},{3,11}... | collective-permute-start | bytes 393224 | tf_op jit(solution)/shard_map/ppermute | solution.py:251
  30.4 2.2 %copy-start.5 = (bf16[4,2,4,128]{3,2,1,0:T(4,128)(2,1)S(1)}, bf16[4,2,4,128]{3,2,1,0:T(4,128)(2,1)}, u32[]{:S(2)}) copy-start(bf16[4,2,4,128]{3,2,1,0:T(4,128)(2,1)} %param.21) | copy-start | bytes 24580
  30.4 2.2 %copy-start.6 = (bf16[4,2,4,128]{3,2,1,0:T(4,128)(2,1)S(1)}, bf16[4,2,4,128]{3,2,1,0:T(4,128)(2,1)}, u32[]{:S(2)}) copy-start(bf16[4,2,4,128]{3,2,1,0:T(4,128)(2,1)} %param.20) | copy-start | bytes 24580
  31.0 6.6 %collective-permute-start.10 = (bf16[2,256,128]{2,1,0:T(8,128)(2,1)S(1)}, bf16[2,256,128]{2,1,0:T(8,128)(2,1)S(1)}, u32[]{:S(2)}, u32[]{:S(2)}) collective-permute-start(bf16[2,256,128]{2,1,0:T(8,128)(2,1)S(1)} %get-tuple-element.31), channel_id=1, source_target_pairs={{0,2},{2,0},{4,6},{6,4},{8,10},{10,8},{12,14},{14,12},{1,3},{3,1},... | collective-permute-start | bytes 393224 | tf_op jit(solution)/shard_map/ppermute | solution.py:251
  32.7 6.2 %copy-start.7 = (f32[64]{0:T(128)S(1)}, f32[64]{0:T(128)}, u32[]{:S(2)}) copy-start(f32[64]{0:T(128)} %param.24) | copy-start | bytes 772
  32.7 6.2 %copy-start.8 = (f32[64]{0:T(128)S(1)}, f32[64]{0:T(128)}, u32[]{:S(2)}) copy-start(f32[64]{0:T(128)} %param.23) | copy-start | bytes 772
  32.7 6.2 %copy-start.9 = (f32[64]{0:T(128)S(1)}, f32[64]{0:T(128)}, u32[]{:S(2)}) copy-start(f32[64]{0:T(128)} %param.22) | copy-start | bytes 772
  32.7 6.4 %copy-start.4 = (f32[4,2,64]{2,1,0:T(2,128)S(1)}, f32[4,2,64]{2,1,0:T(2,128)}, u32[]{:S(2)}) copy-start(f32[4,2,64]{2,1,0:T(2,128)} %param.19) | copy-start | bytes 6148
  32.7 6.6 %copy-start.1 = (bf16[4,2,64,32]{2,3,1,0:T(8,128)(2,1)S(1)}, bf16[4,2,64,32]{2,3,1,0:T(8,128)(2,1)}, u32[]{:S(2)}) copy-start(bf16[4,2,64,32]{2,3,1,0:T(8,128)(2,1)} %param.17) | copy-start | bytes 98308
  32.7 6.9 %copy-start.2 = (bf16[4,2,64,32]{2,3,1,0:T(8,128)(2,1)S(1)}, bf16[4,2,64,32]{2,3,1,0:T(8,128)(2,1)}, u32[]{:S(2)}) copy-start(bf16[4,2,64,32]{2,3,1,0:T(8,128)(2,1)} %param.18) | copy-start | bytes 98308
  33.3 9.0 %copy-start = (bf16[2,64,32,128]{3,2,1,0:T(8,128)(2,1)S(1)}, bf16[2,64,32,128]{3,2,1,0:T(8,128)(2,1)}, u32[]{:S(2)}) copy-start(bf16[2,64,32,128]{3,2,1,0:T(8,128)(2,1)} %param.16) | copy-start | bytes 3145732
  33.3 7.9 %collective-permute-start.11 = (bf16[2,256,128]{2,1,0:T(8,128)(2,1)S(1)}, bf16[2,256,128]{2,1,0:T(8,128)(2,1)S(1)}, u32[]{:S(2)}, u32[]{:S(2)}) collective-permute-start(bf16[2,256,128]{2,1,0:T(8,128)(2,1)S(1)} %get-tuple-element.32), channel_id=1, source_target_pairs={{0,4},{2,6},{4,0},{6,2},{8,12},{10,14},{12,8},{14,10},{1,5},{3,7},... | collective-permute-start | bytes 393224 | tf_op jit(solution)/shard_map/ppermute | solution.py:251
  34.1 8.3 %collective-permute-start.12 = (bf16[2,256,128]{2,1,0:T(8,128)(2,1)S(1)}, bf16[2,256,128]{2,1,0:T(8,128)(2,1)S(1)}, u32[]{:S(2)}, u32[]{:S(2)}) collective-permute-start(bf16[2,256,128]{2,1,0:T(8,128)(2,1)S(1)} %get-tuple-element.33), channel_id=1, source_target_pairs={{0,6},{2,4},{4,2},{6,0},{8,14},{10,12},{12,10},{14,8},{1,7},{3,5},... | collective-permute-start | bytes 393224 | tf_op jit(solution)/shard_map/ppermute | solution.py:251
  35.4 8.8 %collective-permute-start.7 = (bf16[2,256,128]{2,1,0:T(8,128)(2,1)S(1)}, bf16[2,256,128]{2,1,0:T(8,128)(2,1)S(1)}, u32[]{:S(2)}, u32[]{:S(2)}) collective-permute-start(bf16[2,256,128]{2,1,0:T(8,128)(2,1)S(1)} %get-tuple-element.21), channel_id=1, source_target_pairs={{0,2},{2,0},{4,6},{6,4},{8,10},{10,8},{12,14},{14,12},{1,3},{3,1},... | collective-permute-start | bytes 393224 | tf_op jit(solution)/shard_map/ppermute | solution.py:251
  36.9 7.7 %collective-permute-start.8 = (bf16[2,256,128]{2,1,0:T(8,128)(2,1)S(1)}, bf16[2,256,128]{2,1,0:T(8,128)(2,1)S(1)}, u32[]{:S(2)}, u32[]{:S(2)}) collective-permute-start(bf16[2,256,128]{2,1,0:T(8,128)(2,1)S(1)} %get-tuple-element.22), channel_id=1, source_target_pairs={{0,4},{2,6},{4,0},{6,2},{8,12},{10,14},{12,8},{14,10},{1,5},{3,7},... | collective-permute-start | bytes 393224 | tf_op jit(solution)/shard_map/ppermute | solution.py:251
  37.6 9.1 %collective-permute-start.9 = (bf16[2,256,128]{2,1,0:T(8,128)(2,1)S(1)}, bf16[2,256,128]{2,1,0:T(8,128)(2,1)S(1)}, u32[]{:S(2)}, u32[]{:S(2)}) collective-permute-start(bf16[2,256,128]{2,1,0:T(8,128)(2,1)S(1)} %get-tuple-element.23), channel_id=1, source_target_pairs={{0,6},{2,4},{4,2},{6,0},{8,14},{10,12},{12,10},{14,8},{1,7},{3,5},... | collective-permute-start | bytes 393224 | tf_op jit(solution)/shard_map/ppermute | solution.py:251
  40.1 0.7 %copy-start.3 = (f32[64,32]{0,1:T(8,128)S(1)}, f32[64,32]{0,1:T(8,128)}, u32[]{:S(2)}) copy-start(f32[64,32]{0,1:T(8,128)} %param.25) | copy-start | bytes 24580

commit v4 on v3

--- a/solution.py
+++ b/solution.py
@@ -16,12 +16,12 @@
 ANY = pl.BlockSpec(memory_space=pl.ANY)
 
 
-def gather_kernel(group, slots_ref, held_ref, *out_refs):
+def gather_kernel(slots_ref, held_ref, *out_refs):
     for k, out_ref in enumerate(out_refs):
         rows = out_ref.shape[0]
 
         def one(r):
-            out_ref[r] = held_ref[slots_ref[k * rows + r], group]
+            out_ref[r] = held_ref[slots_ref[k * rows + r]]
 
         if rows <= 16:
             for r in range(rows):
@@ -30,14 +30,14 @@
             pl.loop(0, rows)(one)
 
 
-def gather_pieces(group, slots, held, parts):
-    shape = (slots.shape[0] // parts,) + held.shape[2:]
+def gather_pieces(slots, held, parts):
+    shape = (slots.shape[0] // parts,) + held.shape[1:]
     return pl.pallas_call(
-        functools.partial(gather_kernel, group),
+        gather_kernel,
         in_specs=[SMEM, VMEM],
         out_specs=[VMEM] * parts,
         out_shape=[jax.ShapeDtypeStruct(shape, held.dtype)] * parts,
-        compiler_params=pltpu.CompilerParams(vmem_limit_bytes=4 * 1024 * 1024),
+        compiler_params=pltpu.CompilerParams(vmem_limit_bytes=2 * 1024 * 1024),
     )(slots, held)
 
 
@@ -139,7 +139,7 @@
             wide(groups, 6 * both, 2 * rows * entries),
             wide(groups, both, rows * entries),
         ],
-        compiler_params=pltpu.CompilerParams(vmem_limit_bytes=8 * 1024 * 1024),
+        compiler_params=pltpu.CompilerParams(vmem_limit_bytes=4 * 1024 * 1024),
     )(
         x_new.reshape(both, flat), z_gate.reshape(both, flat),
         over_channels(dt_raw.reshape(both, heads)),
@@ -149,80 +149,124 @@
     )
 
 
-def decode_kernel(rows, group, parts, info_ref, *refs):
-    recv_refs, refs = refs[:parts], refs[parts:]
-    (resident_ref, base_ref, carry_ref, gate_ref, left_ref, right_ref, seen_ref,
-     gain_ref) = refs[:8]
-    decoded_ref, final_ref, ready, seen, out_sem = refs[-5:]
-    span, entries = recv_refs[0].shape[1:]
-    block = parts * span
-    start = group * block
-    lanes = slice(start, start + block)
-
-    def place(p, r):
-        return pl.multiple_of((info_ref[rows + r] ^ p) * span, span)
-
-    def result(p, r):
+def decode_kernel(rows, groups, parts, last, info_ref, *refs):
+    recv_refs, refs = refs[:len(parts)], refs[len(parts):]
+    left_ref, right_ref, seen_ref = refs[:3]
+    span, entries = recv_refs[0].shape[2:]
+    if last:
+        base_ref, carry_ref, gate_ref, gain_ref, before_ref = refs[3:8]
+        decoded_ref, final_ref, ready, seen, out_sem = refs[-5:]
+        seen[...] = before_ref[...]
+    else:
+        resident_ref = refs[3]
+        final_ref, seen, ready, out_sem, stay, in_sem = refs[-6:]
+        seen[...] = jnp.zeros_like(seen)
+    block = final_ref.shape[1] // groups
+    quarters = block // span
+
+    def advance(r, g, initial, slot, at):
+        column = 2 * r * entries
+        here = pl.ds(at, span)
+        moved = lax.dot_general(
+            left_ref[:, here], right_ref[g, :, column:column + 2 * entries],
+            (((0,), (0,)), ((), ())), preferred_element_type=F32)
+        ready[slot, r, g] = (
+            moved[:, entries:] * initial.astype(F32) + moved[:, :entries]).astype(BF16)
+        seen[r, :, here] = lax.dot_general(
+            seen_ref[g, :, r * entries:(r + 1) * entries], initial,
+            (((1,), (1,)), ((), ())), preferred_element_type=F32)
         return pltpu.make_async_copy(
-            ready.at[r, p], final_ref.at[r, pl.ds(start + place(p, r), span)],
-            out_sem.at[p, r])
+            ready.at[slot, r, g], final_ref.at[r, here], out_sem.at[slot, r, g])
+
+    def place(r, g, quarter):
+        return pl.multiple_of(g * block + quarter * span, span)
+
+    def listed_row(r, act):
+        for p, part in enumerate(parts):
+            for g in range(groups):
+                act(p, g, place(r, g, info_ref[rows + r] ^ part))
+
+    def staying_row(r, act):
+        for quarter in range(quarters):
+            for g in range(groups):
+                act(quarter, g, place(r, g, quarter))
+
+    def stays(r):
+        return pltpu.make_async_copy(resident_ref.at[r], stay.at[r], in_sem.at[r])
+
+    def written(r, slot, g, at):
+        return pltpu.make_async_copy(
+            ready.at[slot, r, g], final_ref.at[r, pl.ds(at, span)], out_sem.at[slot, r, g])
 
     for r in range(rows):
-        listed = info_ref[r] == 1
-        at = 2 * r * entries
-        for p in range(parts):
-            here = place(p, r)
-            initial = jnp.where(
-                listed, recv_refs[p][r], resident_ref[r, pl.ds(start + here, span)])
-            moved = lax.dot_general(
-                left_ref[:, pl.ds(pl.multiple_of(start + here, span), span)],
-                right_ref[group, :, at:at + 2 * entries],
-                (((0,), (0,)), ((), ())), preferred_element_type=F32)
-            ready[r, p] = (
-                moved[:, entries:] * initial.astype(F32) + moved[:, :entries]).astype(BF16)
-            result(p, r).start()
-            part = lax.dot_general(
-                seen_ref[group, :, r * entries:(r + 1) * entries], initial,
-                (((1,), (1,)), ((), ())), preferred_element_type=F32)
-            seen[r, :, pl.ds(here, span)] = part
-    total = seen[0]
-    for r in range(1, rows):
-        total = total + seen[r]
-    readout = carry_ref[:, lanes] * total + base_ref[:, lanes]
-    gated = readout * gate_ref[:, lanes]
-    squares = jnp.mean(gated * gated, axis=1, keepdims=True)
-    normed = gated * lax.rsqrt(squares + 1e-05) * gain_ref[:, lanes]
-    if group:
-        decoded_ref[:, :start] = refs[8][...]
-    decoded_ref[:, lanes] = normed.astype(BF16)
+        if not last:
+
+            @pl.when(info_ref[r] == 0)
+            def _():
+                stays(r).start()
+
     for r in range(rows):
-        for p in range(parts):
-            result(p, r).wait()
-
-
-def decode(group, info, recv, resident, ready, gain, earlier):
+
+        @pl.when(info_ref[r] == 1)
+        def _():
+            listed_row(r, lambda p, g, at: advance(r, g, recv_refs[p][r, g], p, at).start())
+
+        if not last:
+
+            @pl.when(info_ref[r] == 0)
+            def _():
+                stays(r).wait()
+                staying_row(r, lambda quarter, g, at: advance(
+                    r, g, stay[r, pl.ds(at, span)], quarter, at).start())
+
+    if last:
+        for g in range(groups):
+            lanes = slice(g * block, (g + 1) * block)
+            total = seen[0, :, lanes]
+            for r in range(1, rows):
+                total = total + seen[r, :, lanes]
+            readout = carry_ref[:, lanes] * total + base_ref[:, lanes]
+            gated = readout * gate_ref[:, lanes]
+            squares = jnp.mean(gated * gated, axis=1, keepdims=True)
+            normed = gated * lax.rsqrt(squares + 1e-05) * gain_ref[:, lanes]
+            decoded_ref[:, lanes] = normed.astype(BF16)
+    for r in range(rows):
+
+        @pl.when(info_ref[r] == 1)
+        def _():
+            listed_row(r, lambda p, g, at: written(r, p, g, at).wait())
+
+        if not last:
+
+            @pl.when(info_ref[r] == 0)
+            def _():
+                staying_row(r, lambda quarter, g, at: written(r, quarter, g, at).wait())
+
+
+def decode(parts, info, recv, resident, ready, gain, earlier):
     rows, flat, entries = resident.shape
-    both = ready[0].shape[0]
-    groups = ready[4].shape[0]
-    block = flat // groups
-    parts, span = len(recv), block // len(recv)
-    count = 1 + parts + 1 + len(ready) + 1
+    groups, span = recv[0].shape[1:3]
+    base, carry, gate, left, right, seen = ready
+    both = base.shape[0]
+    last = len(earlier) > 0
+    operands = [info, *recv, left, right, seen]
+    operands += [base, carry, gate, gain, *earlier] if last else [resident]
+    slots = len(parts) if last else flat // groups // span
+    final = jax.ShapeDtypeStruct((rows, flat, entries), BF16)
     return pl.pallas_call(
-        functools.partial(decode_kernel, rows, group, parts),
-        in_specs=[SMEM] + [VMEM] * (count - 1) + [VMEM, ANY][:len(earlier)],
-        out_specs=[VMEM, ANY],
-        input_output_aliases={count + 1: 1} if earlier else {},
-        scratch_shapes=[
-            pltpu.VMEM((rows, parts, span, entries), BF16),
-            pltpu.VMEM((rows, both, block), F32),
-            pltpu.SemaphoreType.DMA((parts, rows)),
-        ],
-        out_shape=[
-            jax.ShapeDtypeStruct((both, (group + 1) * block), BF16),
-            jax.ShapeDtypeStruct((rows, flat, entries), BF16),
-        ],
-        compiler_params=pltpu.CompilerParams(vmem_limit_bytes=16 * 1024 * 1024),
-    )(info, *recv, resident, *ready, gain, *earlier)
+        functools.partial(decode_kernel, rows, groups, parts, last),
+        in_specs=[SMEM] + [VMEM] * (len(operands) - 2) + [ANY],
+        out_specs=[VMEM, ANY] if last else [ANY, VMEM],
+        input_output_aliases={len(operands) - 1: 1} if last else {},
+        scratch_shapes=[pltpu.VMEM((slots, rows, groups, span, entries), BF16)]
+        + [pltpu.VMEM((rows, both, flat), F32)] * last
+        + [pltpu.SemaphoreType.DMA((slots, rows, groups))]
+        + ([] if last else [
+            pltpu.VMEM((rows, flat, entries), BF16), pltpu.SemaphoreType.DMA((rows,))]),
+        out_shape=[jax.ShapeDtypeStruct((both, flat), BF16), final] if last
+        else [final, jax.ShapeDtypeStruct((rows, both, flat), F32)],
+        compiler_params=pltpu.CompilerParams(vmem_limit_bytes=8 * 1024 * 1024),
+    )(*operands)
 
 
 def local(
@@ -253,7 +297,6 @@
     pieces = prefill_states.reshape(groups, quarter, span, entries)
     here = jnp.arange(shards * row_count, dtype=jnp.int32) // row_count
     few = shards == 8
-    recv = []
     if few:
         arrived = [pieces[:, 0]] + [
             hand(pieces[:, k % quarter], k) for k in range(1, shards)]
@@ -262,21 +305,19 @@
         order = (order * row_count + jnp.arange(row_count)).reshape(half_rows)
         slots = lax.dynamic_slice_in_dim(
             source ^ me, (me // quarter) * half_rows, half_rows)[order]
-        for g in range(groups):
-            sent = gather_pieces(g, slots, held, quarter)
-            recv.append([sent[0]] + [hand(sent[k], k) for k in range(1, quarter)])
+        sent = gather_pieces(slots, held, quarter)
+        recv = [sent[0]] + [hand(sent[k], k) for k in range(1, quarter)]
         mask = (source ^ here) % quarter
     else:
         pieces = jnp.moveaxis(pieces, 0, 1)
         held = exchange(jnp.concatenate([pieces, pieces]).reshape(
             shards, groups * span, entries)).reshape(shards, groups, span, entries)
         slots = lax.dynamic_slice_in_dim(source, (me // quarter) * half_rows, half_rows)
-        for g in range(groups):
-            sent, = gather_pieces(g, slots, held, 1)
-            sent = exchange(sent.reshape(quarter, row_count * span, entries), halves)
-            sent = jnp.moveaxis(sent.reshape(quarter, row_count, span, entries), 1, 0)
-            sent = sent.reshape(row_count, 4, quarter * span // 4, entries)
-            recv.append([sent[:, p] for p in range(4)])
+        sent, = gather_pieces(slots, held, 1)
+        sent = exchange(sent.reshape(quarter, row_count * groups * span, entries), halves)
+        sent = jnp.moveaxis(sent.reshape(quarter, row_count, groups, span, entries), 0, 2)
+        sent = sent.reshape(row_count, groups, 4, quarter * span // 4, entries)
+        recv = [sent[:, :, p] for p in range(4)]
         mask = jnp.zeros_like(source)
 
     groups = local_heads // (HEADS // GROUPS)
@@ -290,10 +331,9 @@
         lax.dynamic_slice_in_dim(listed, me * row_count, row_count),
         lax.dynamic_slice_in_dim(mask, me * row_count, row_count)])
     resident = resident_states.reshape(row_count, flat, entries)
-    outs = ()
-    for g in range(groups):
-        outs = decode(g, info, recv[g], resident, ready, norm_gain.reshape(1, flat), outs)
-    decoded, final = outs
+    gain = norm_gain.reshape(1, flat)
+    final, seen = decode((0, 1, 2), info, recv[:3], resident, ready, gain, ())
+    decoded, final = decode((3,), info, recv[3:], resident, ready, gain, (seen, final))
     return (decoded.reshape(x_new.shape), final.reshape(resident_states.shape))
 
 

time: 49.6 us -> 48 us (0.968)
  starting transfers between devices: 19.5 us -> 16.1 us
  waiting for transfers between devices: 17 us -> 18.3 us
  local copies, waits for them, and re-layouts: 6.59 us -> 7.25 us
    ppermute x13 -> x10, starting transfers between devices: 19.5 us -> 16.1 us  [hand(): return lax.ppermute(value, 'rows', [(i, i ^ k) for i in range(shards)])]
    ppermute x13 -> x10, waiting for transfers between devices: 17 us -> 18.3 us  [hand(): return lax.ppermute(value, 'rows', [(i, i ^ k) for i in range(shards)])]
    unnamed x35, local copies, waits for them, and re-layouts: 3.42 us -> 4.08 us
    pallas_call x4 -> x3, Pallas kernels: 4.7 us -> 4.45 us  [the longest x2 3.84 us: decode(): pl.pallas_call(functools.partial(decode_kernel, rows, groups, parts, last...]
  transfers between devices with their start and end apart: 13 -> 10, of which waited for: 6 -> 6; matrix products, arithmetic and copies ran while one was open for 7% -> 8% of each run, Pallas kernels for 5% -> 5%
where the time goes in v4:
time: 48 us; the launch traced here: 47.6 us
  waiting for transfers between devices  18.3 us (38%)
  starting transfers between devices  16.1 us (34%)
  local copies, waits for them, and re-layouts  7.25 us (15%)
  Pallas kernels  4.67 us (10%)
  between operations  0.95 us (2%)
    ppermute x10, waiting for transfers between devices, hand(): return lax.ppermute(value, 'rows', [(i, i ^ k) for i in range(shards)])  18.3 us
    ppermute x10, starting transfers between devices, hand(): return lax.ppermute(value, 'rows', [(i, i ^ k) for i in range(shards)])  16.1 us
    unnamed x35, local copies, waits for them, and re-layouts  4.08 us
    pallas_call x2, Pallas kernels, decode(): pl.pallas_call(functools.partial(decode_kernel, rows, groups, parts, last...  3.84 us
    squeeze x1, local copies, waits for them, and re-layouts, local(): pieces[:, k % quarter]  1.14 us
  transfers between devices with their start and end apart: 10, of which 6 were waited for; matrix products, arithmetic and copies ran while one was open for 8% of the time, Pallas kernels for 5%

profile of v4, /device:TPU:0, one launch (start us, length us, event | category | flops | bytes accessed | tf_op | source)
XLA Modules:
  0.0 47.6 jit_solution(11866402705686018605)
XLA Ops:
  0.6 1.1 %slice_bitcast_fusion.3 = (bf16[2,256,128]{2,1,0:T(8,128)(2,1)S(1)}, bf16[2,256,128]{2,1,0:T(8,128)(2,1)S(1)}, bf16[2,256,128]{2,1,0:T(8,128)(2,1)S(1)}, bf16[2,256,128]{2,1,0:T(8,128)(2,1)S(1)}) fusion(bf16[2,4,256,128]{3,2,1,0:T(8,128)(2,1)} %bitcast.56), kind=kLoop, calls=%fused_computation.12 | loop fusion | bytes 1048576 | tf_op jit(solution)/shard_map/squeeze | solution.py:302
  1.8 3.0 %collective-permute-start = (bf16[2,256,128]{2,1,0:T(8,128)(2,1)S(1)}, bf16[2,256,128]{2,1,0:T(8,128)(2,1)S(1)}, u32[]{:S(2)}, u32[]{:S(2)}) collective-permute-start(bf16[2,256,128]{2,1,0:T(8,128)(2,1)S(1)} %get-tuple-element.38), channel_id=1, source_target_pairs={{0,2},{2,0},{4,6},{6,4},{8,10},{10,8},{12,14},{14,12},{1,3},{3,1},... | collective-permute-start | bytes 393224 | tf_op jit(solution)/shard_map/ppermute | solution.py:295
  4.8 2.6 %collective-permute-start.4 = (bf16[2,256,128]{2,1,0:T(8,128)(2,1)S(1)}, bf16[2,256,128]{2,1,0:T(8,128)(2,1)S(1)}, u32[]{:S(2)}, u32[]{:S(2)}) collective-permute-start(bf16[2,256,128]{2,1,0:T(8,128)(2,1)S(1)} %get-tuple-element.38), channel_id=1, source_target_pairs={{0,10},{2,8},{4,14},{6,12},{8,2},{10,0},{12,6},{14,4},{1,11},{3,9}... | collective-permute-start | bytes 393224 | tf_op jit(solution)/shard_map/ppermute | solution.py:295
  7.3 1.6 %collective-permute-start.1 = (bf16[2,256,128]{2,1,0:T(8,128)(2,1)S(1)}, bf16[2,256,128]{2,1,0:T(8,128)(2,1)S(1)}, u32[]{:S(2)}, u32[]{:S(2)}) collective-permute-start(bf16[2,256,128]{2,1,0:T(8,128)(2,1)S(1)} %get-tuple-element.37), channel_id=1, source_target_pairs={{0,4},{2,6},{4,0},{6,2},{8,12},{10,14},{12,8},{14,10},{1,5},{3,7},... | collective-permute-start | bytes 393224 | tf_op jit(solution)/shard_map/ppermute | solution.py:295
  8.9 1.8 %collective-permute-start.2 = (bf16[2,256,128]{2,1,0:T(8,128)(2,1)S(1)}, bf16[2,256,128]{2,1,0:T(8,128)(2,1)S(1)}, u32[]{:S(2)}, u32[]{:S(2)}) collective-permute-start(bf16[2,256,128]{2,1,0:T(8,128)(2,1)S(1)} %get-tuple-element.39), channel_id=1, source_target_pairs={{0,6},{2,4},{4,2},{6,0},{8,14},{10,12},{12,10},{14,8},{1,7},{3,5},... | collective-permute-start | bytes 393224 | tf_op jit(solution)/shard_map/ppermute | solution.py:295
  10.7 0.9 %bitcast_dynamic-update-slice_fusion = bf16[8,2,256,128]{3,2,1,0:T(8,128)(2,1)S(1)} fusion(bf16[2,4,256,128]{3,2,1,0:T(8,128)(2,1)} %bitcast.57), kind=kLoop, calls=%fused_computation.4 | loop fusion | bytes 262144
  11.7 0.1 iota_add_fusion
  11.8 0.1 add.64
  11.8 0.6 %copy-done.10 = s32[8]{0:T(128)S(1)} copy-done((s32[8]{0:T(128)S(1)}, s32[8]{0:T(128)}, u32[]{:S(2)}) %copy-start.10) | copy-done | bytes 56
  12.5 0.0 copy-done.11
  12.5 0.1 select_reduce_fusion
  12.6 0.1 dynamic_slice.17
  12.7 0.6 %gather_fusion = s32[8]{0:T(128)S(1)} fusion(s32[8]{0:T(128)S(1)} %dynamic_slice.17, s32[1024]{0:T(1024)S(1)} %pad_clamp_fusion), kind=kCustom, calls=%fused_computation | custom fusion | bytes 96 | tf_op jit(solution)/shard_map/gather | solution.py:306
  13.4 0.1 fusion
  13.5 3.0 %collective-permute-start.6 = (bf16[2,256,128]{2,1,0:T(8,128)(2,1)S(1)}, bf16[2,256,128]{2,1,0:T(8,128)(2,1)S(1)}, u32[]{:S(2)}, u32[]{:S(2)}) collective-permute-start(bf16[2,256,128]{2,1,0:T(8,128)(2,1)S(1)} %get-tuple-element.39), channel_id=1, source_target_pairs={{0,14},{2,12},{4,10},{6,8},{8,6},{10,4},{12,2},{14,0},{1,15},{3,13... | collective-permute-start | bytes 393224 | tf_op jit(solution)/shard_map/ppermute | solution.py:295
  16.5 0.1 collective-permute-done.1
  16.6 0.6 %collective-permute-start.3 = (bf16[2,256,128]{2,1,0:T(8,128)(2,1)S(1)}, bf16[2,256,128]{2,1,0:T(8,128)(2,1)S(1)}, u32[]{:S(2)}, u32[]{:S(2)}) collective-permute-start(bf16[2,256,128]{2,1,0:T(8,128)(2,1)S(1)} %get-tuple-element.36), channel_id=1, source_target_pairs={{0,8},{2,10},{4,12},{6,14},{8,0},{10,2},{12,4},{14,6},{1,9},{3,11}... | collective-permute-start | bytes 393224 | tf_op jit(solution)/shard_map/ppermute | solution.py:295
  17.1 3.8 %collective-permute-done.2 = bf16[2,256,128]{2,1,0:T(8,128)(2,1)S(1)} collective-permute-done((bf16[2,256,128]{2,1,0:T(8,128)(2,1)S(1)}, bf16[2,256,128]{2,1,0:T(8,128)(2,1)S(1)}, u32[]{:S(2)}, u32[]{:S(2)}) %collective-permute-start.2) | collective-permute-done | bytes 131104 | tf_op jit(solution)/shard_map/ppermute | solution.py:295
  20.9 9.3 %collective-permute-done.3 = bf16[2,256,128]{2,1,0:T(8,128)(2,1)S(1)} collective-permute-done((bf16[2,256,128]{2,1,0:T(8,128)(2,1)S(1)}, bf16[2,256,128]{2,1,0:T(8,128)(2,1)S(1)}, u32[]{:S(2)}, u32[]{:S(2)}) %collective-permute-start.3) | collective-permute-done | bytes 131104 | tf_op jit(solution)/shard_map/ppermute | solution.py:295
  30.4 0.6 %shard_map.140 = (bf16[2,2,256,128]{3,2,1,0:T(8,128)(2,1)S(1)}, bf16[2,2,256,128]{3,2,1,0:T(8,128)(2,1)S(1)}, bf16[2,2,256,128]{3,2,1,0:T(8,128)(2,1)S(1)}, bf16[2,2,256,128]{3,2,1,0:T(8,128)(2,1)S(1)}) custom-call(s32[8]{0:T(128)S(1)} %gather_fusion, bf16[8,2,256,128]{3,2,1,0:T(8,128)(2,1)S(1)} %bitcast_dynamic-update-slice_fusion.1.held_ref), custom_call_target="tpu_custom_call" | custom-call | tf_op jit(solution)/shard_map/pallas_call | solution.py:35
  31.1 1.6 %collective-permute-start.8 = (bf16[2,2,256,128]{3,2,1,0:T(8,128)(2,1)S(1)}, bf16[2,2,256,128]{3,2,1,0:T(8,128)(2,1)S(1)}, u32[]{:S(2)}, u32[]{:S(2)}) collective-permute-start(bf16[2,2,256,128]{3,2,1,0:T(8,128)(2,1)S(1)} %get-tuple-element.24), channel_id=1, source_target_pairs={{0,2},{2,0},{4,6},{6,4},{8,10},{10,8},{12,14},{14,12},{1,3},{3,1},... | collective-permute-start | bytes 786440 | tf_op jit(solution)/shard_map/ppermute | solution.py:295
  32.7 0.7 %collective-permute-start.9 = (bf16[2,2,256,128]{3,2,1,0:T(8,128)(2,1)S(1)}, bf16[2,2,256,128]{3,2,1,0:T(8,128)(2,1)S(1)}, u32[]{:S(2)}, u32[]{:S(2)}) collective-permute-start(bf16[2,2,256,128]{3,2,1,0:T(8,128)(2,1)S(1)} %get-tuple-element.25), channel_id=1, source_target_pairs={{0,4},{2,6},{4,0},{6,2},{8,12},{10,14},{12,8},{14,10},{1,5},{3,7},... | collective-permute-start | bytes 786440 | tf_op jit(solution)/shard_map/ppermute | solution.py:295
  33.4 1.3 %collective-permute-start.7 = (bf16[2,2,256,128]{3,2,1,0:T(8,128)(2,1)S(1)}, bf16[2,2,256,128]{3,2,1,0:T(8,128)(2,1)S(1)}, u32[]{:S(2)}, u32[]{:S(2)}) collective-permute-start(bf16[2,2,256,128]{3,2,1,0:T(8,128)(2,1)S(1)} %get-tuple-element.16), channel_id=1, source_target_pairs={{0,6},{2,4},{4,2},{6,0},{8,14},{10,12},{12,10},{14,8},{1,7},{3,5},... | collective-permute-start | bytes 786440 | tf_op jit(solution)/shard_map/ppermute | solution.py:295
  34.7 0.1 dynamic_slice.16
  34.7 0.1 dynamic_slice.15
  34.8 0.1 broadcast_in_dim.34
  35.0 0.1 reshape.81.dt_ref
  35.1 0.1 copy.36
  35.3 0.2 reshape.79.x_ref
  35.4 0.1 copy.37
  35.6 0.2 reshape.80.z_ref
  35.8 0.6 %copy-done.7 = f32[64]{0:T(128)S(1)} copy-done((f32[64]{0:T(128)S(1)}, f32[64]{0:T(128)}, u32[]{:S(2)}) %copy-start.7) | copy-done | bytes 280
  36.4 0.0 copy-done.8
  36.4 0.0 copy-done.9
  36.4 0.1 broadcast_in_dim.35
  36.5 0.1 reshape.84.head_ref
  36.7 0.6 %copy-done.3 = f32[64,32]{0,1:T(8,128)S(1)} copy-done((f32[64,32]{0,1:T(8,128)S(1)}, f32[64,32]{0,1:T(8,128)}, u32[]{:S(2)}) %copy-start.3) | copy-done | bytes 8216
  37.3 0.1 copy.40
  37.3 0.1 reshape.85.refs_7_
  37.4 0.2 shard_map.141
  37.7 0.1 pad_add_fusion.info_ref
  37.7 1.7 %collective-permute-done.8.refs_1_ = bf16[2,2,256,128]{3,2,1,0:T(8,128)(2,1)S(1)} collective-permute-done((bf16[2,2,256,128]{3,2,1,0:T(8,128)(2,1)S(1)}, bf16[2,2,256,128]{3,2,1,0:T(8,128)(2,1)S(1)}, u32[]{:S(2)}, u32[]{:S(2)}) %collective-permute-start.8) | collective-permute-done | bytes 262176 | tf_op jit(solution)/shard_map/ppermute | solution.py:295
  39.4 2.5 %collective-permute-done.9.refs_2_ = bf16[2,2,256,128]{3,2,1,0:T(8,128)(2,1)S(1)} collective-permute-done((bf16[2,2,256,128]{3,2,1,0:T(8,128)(2,1)S(1)}, bf16[2,2,256,128]{3,2,1,0:T(8,128)(2,1)S(1)}, u32[]{:S(2)}, u32[]{:S(2)}) %collective-permute-start.9) | collective-permute-done | bytes 262176 | tf_op jit(solution)/shard_map/ppermute | solution.py:295
  41.9 2.3 %shard_map.142 = (bf16[2,2048,128]{2,1,0:T(8,128)(2,1)}, f32[2,8,2048]{2,1,0:T(8,128)S(1)}) custom-call(s32[4]{0:T(128)S(1)} %pad_add_fusion.info_ref, bf16[2,2,256,128]{3,2,1,0:T(8,128)(2,1)S(1)} %get-tuple-element.23.refs_0_, bf16[2,2,256,128]{3,2,1,0:T(8,128)(2,1)S(1)} %collective-permute-done.8.refs_1_, ...), custom_call_target="tpu_custom_call" | custom-call | tf_op jit(solution)/shard_map/pallas_call | solution.py:256
  44.3 0.9 %collective-permute-done.7.refs_0_ = bf16[2,2,256,128]{3,2,1,0:T(8,128)(2,1)S(1)} collective-permute-done((bf16[2,2,256,128]{3,2,1,0:T(8,128)(2,1)S(1)}, bf16[2,2,256,128]{3,2,1,0:T(8,128)(2,1)S(1)}, u32[]{:S(2)}, u32[]{:S(2)}) %collective-permute-start.7) | collective-permute-done | bytes 262176 | tf_op jit(solution)/shard_map/ppermute | solution.py:295
  45.2 1.5 %shard_map.143 = (bf16[8,2048]{1,0:T(8,128)(2,1)S(1)}, bf16[2,2048,128]{2,1,0:T(8,128)(2,1)}) custom-call(s32[4]{0:T(128)S(1)} %pad_add_fusion.info_ref, bf16[2,2,256,128]{3,2,1,0:T(8,128)(2,1)S(1)} %collective-permute-done.7.refs_0_, bf16[48,2048]{1,0:T(8,128)(2,1)S(1)} %get-tuple-element.17.refs_3_.refs_1_, ...), custom_call_target="tpu_custom_call", output_to_operand_aliasing={{1}: (10, {})} | custom-call | tf_op jit(solution)/shard_map/pallas_call | solution.py:256
  46.7 0.1 reshape.87
  46.8 0.7 %copy.41 = bf16[4,2,64,32]{2,3,1,0:T(8,128)(2,1)} copy(bf16[4,2,64,32]{3,2,1,0:T(8,128)(2,1)S(1)} %reshape.87) | data formatting | bytes 65536
  (39 shorter events, 0.3 us)
Async XLA Ops:
  1.8 11.7 %collective-permute-start = (bf16[2,256,128]{2,1,0:T(8,128)(2,1)S(1)}, bf16[2,256,128]{2,1,0:T(8,128)(2,1)S(1)}, u32[]{:S(2)}, u32[]{:S(2)}) collective-permute-start(bf16[2,256,128]{2,1,0:T(8,128)(2,1)S(1)} %get-tuple-element.38), channel_id=1, source_target_pairs={{0,2},{2,0},{4,6},{6,4},{8,10},{10,8},{12,14},{14,12},{1,3},{3,1},... | collective-permute-start | bytes 393224 | tf_op jit(solution)/shard_map/ppermute | solution.py:295
  4.8 25.5 %collective-permute-start.4 = (bf16[2,256,128]{2,1,0:T(8,128)(2,1)S(1)}, bf16[2,256,128]{2,1,0:T(8,128)(2,1)S(1)}, u32[]{:S(2)}, u32[]{:S(2)}) collective-permute-start(bf16[2,256,128]{2,1,0:T(8,128)(2,1)S(1)} %get-tuple-element.38), channel_id=1, source_target_pairs={{0,10},{2,8},{4,14},{6,12},{8,2},{10,0},{12,6},{14,4},{1,11},{3,9}... | collective-permute-start | bytes 393224 | tf_op jit(solution)/shard_map/ppermute | solution.py:295
  7.3 9.2 %collective-permute-start.1 = (bf16[2,256,128]{2,1,0:T(8,128)(2,1)S(1)}, bf16[2,256,128]{2,1,0:T(8,128)(2,1)S(1)}, u32[]{:S(2)}, u32[]{:S(2)}) collective-permute-start(bf16[2,256,128]{2,1,0:T(8,128)(2,1)S(1)} %get-tuple-element.37), channel_id=1, source_target_pairs={{0,4},{2,6},{4,0},{6,2},{8,12},{10,14},{12,8},{14,10},{1,5},{3,7},... | collective-permute-start | bytes 393224 | tf_op jit(solution)/shard_map/ppermute | solution.py:295
  8.9 21.4 %collective-permute-start.5 = (bf16[2,256,128]{2,1,0:T(8,128)(2,1)S(1)}, bf16[2,256,128]{2,1,0:T(8,128)(2,1)S(1)}, u32[]{:S(2)}, u32[]{:S(2)}) collective-permute-start(bf16[2,256,128]{2,1,0:T(8,128)(2,1)S(1)} %get-tuple-element.37), channel_id=1, source_target_pairs={{0,12},{2,14},{4,8},{6,10},{8,4},{10,6},{12,0},{14,2},{1,13},{3,15... | collective-permute-start | bytes 393224 | tf_op jit(solution)/shard_map/ppermute | solution.py:295
  8.9 12.0 %collective-permute-start.2 = (bf16[2,256,128]{2,1,0:T(8,128)(2,1)S(1)}, bf16[2,256,128]{2,1,0:T(8,128)(2,1)S(1)}, u32[]{:S(2)}, u32[]{:S(2)}) collective-permute-start(bf16[2,256,128]{2,1,0:T(8,128)(2,1)S(1)} %get-tuple-element.39), channel_id=1, source_target_pairs={{0,6},{2,4},{4,2},{6,0},{8,14},{10,12},{12,10},{14,8},{1,7},{3,5},... | collective-permute-start | bytes 393224 | tf_op jit(solution)/shard_map/ppermute | solution.py:295
  11.8 0.7 %copy-start.10 = (s32[8]{0:T(128)S(1)}, s32[8]{0:T(128)}, u32[]{:S(2)}) copy-start(s32[8]{0:T(128)} %param.14) | copy-start | bytes 100
  11.8 0.7 %copy-start.11 = (s32[8]{0:T(128)S(1)}, s32[8]{0:T(128)}, u32[]{:S(2)}) copy-start(s32[8]{0:T(128)} %param.15) | copy-start | bytes 100
  13.5 16.9 %collective-permute-start.6 = (bf16[2,256,128]{2,1,0:T(8,128)(2,1)S(1)}, bf16[2,256,128]{2,1,0:T(8,128)(2,1)S(1)}, u32[]{:S(2)}, u32[]{:S(2)}) collective-permute-start(bf16[2,256,128]{2,1,0:T(8,128)(2,1)S(1)} %get-tuple-element.39), channel_id=1, source_target_pairs={{0,14},{2,12},{4,10},{6,8},{8,6},{10,4},{12,2},{14,0},{1,15},{3,13... | collective-permute-start | bytes 393224 | tf_op jit(solution)/shard_map/ppermute | solution.py:295
  16.6 13.7 %collective-permute-start.3 = (bf16[2,256,128]{2,1,0:T(8,128)(2,1)S(1)}, bf16[2,256,128]{2,1,0:T(8,128)(2,1)S(1)}, u32[]{:S(2)}, u32[]{:S(2)}) collective-permute-start(bf16[2,256,128]{2,1,0:T(8,128)(2,1)S(1)} %get-tuple-element.36), channel_id=1, source_target_pairs={{0,8},{2,10},{4,12},{6,14},{8,0},{10,2},{12,4},{14,6},{1,9},{3,11}... | collective-permute-start | bytes 393224 | tf_op jit(solution)/shard_map/ppermute | solution.py:295
  30.4 4.3 %copy-start.5 = (bf16[4,2,4,128]{3,2,1,0:T(4,128)(2,1)S(1)}, bf16[4,2,4,128]{3,2,1,0:T(4,128)(2,1)}, u32[]{:S(2)}) copy-start(bf16[4,2,4,128]{3,2,1,0:T(4,128)(2,1)} %param.21) | copy-start | bytes 24580
  30.4 4.2 %copy-start.6 = (bf16[4,2,4,128]{3,2,1,0:T(4,128)(2,1)S(1)}, bf16[4,2,4,128]{3,2,1,0:T(4,128)(2,1)}, u32[]{:S(2)}) copy-start(bf16[4,2,4,128]{3,2,1,0:T(4,128)(2,1)} %param.20) | copy-start | bytes 24580
  30.4 4.4 %copy-start.4 = (f32[4,2,64]{2,1,0:T(2,128)S(1)}, f32[4,2,64]{2,1,0:T(2,128)}, u32[]{:S(2)}) copy-start(f32[4,2,64]{2,1,0:T(2,128)} %param.19) | copy-start | bytes 6148
  30.4 4.7 %copy-start.1 = (bf16[4,2,64,32]{2,3,1,0:T(8,128)(2,1)S(1)}, bf16[4,2,64,32]{2,3,1,0:T(8,128)(2,1)}, u32[]{:S(2)}) copy-start(bf16[4,2,64,32]{2,3,1,0:T(8,128)(2,1)} %param.17) | copy-start | bytes 98308
  30.4 5.0 %copy-start.2 = (bf16[4,2,64,32]{2,3,1,0:T(8,128)(2,1)S(1)}, bf16[4,2,64,32]{2,3,1,0:T(8,128)(2,1)}, u32[]{:S(2)}) copy-start(bf16[4,2,64,32]{2,3,1,0:T(8,128)(2,1)} %param.18) | copy-start | bytes 98308
  31.1 10.8 %copy-start = (bf16[2,64,32,128]{3,2,1,0:T(8,128)(2,1)S(1)}, bf16[2,64,32,128]{3,2,1,0:T(8,128)(2,1)}, u32[]{:S(2)}) copy-start(bf16[2,64,32,128]{3,2,1,0:T(8,128)(2,1)} %param.16) | copy-start | bytes 3145732
  31.1 8.3 %collective-permute-start.8 = (bf16[2,2,256,128]{3,2,1,0:T(8,128)(2,1)S(1)}, bf16[2,2,256,128]{3,2,1,0:T(8,128)(2,1)S(1)}, u32[]{:S(2)}, u32[]{:S(2)}) collective-permute-start(bf16[2,2,256,128]{3,2,1,0:T(8,128)(2,1)S(1)} %get-tuple-element.24), channel_id=1, source_target_pairs={{0,2},{2,0},{4,6},{6,4},{8,10},{10,8},{12,14},{14,12},{1,3},{3,1},... | collective-permute-start | bytes 786440 | tf_op jit(solution)/shard_map/ppermute | solution.py:295
  32.7 9.2 %collective-permute-start.9 = (bf16[2,2,256,128]{3,2,1,0:T(8,128)(2,1)S(1)}, bf16[2,2,256,128]{3,2,1,0:T(8,128)(2,1)S(1)}, u32[]{:S(2)}, u32[]{:S(2)}) collective-permute-start(bf16[2,2,256,128]{3,2,1,0:T(8,128)(2,1)S(1)} %get-tuple-element.25), channel_id=1, source_target_pairs={{0,4},{2,6},{4,0},{6,2},{8,12},{10,14},{12,8},{14,10},{1,5},{3,7},... | collective-permute-start | bytes 786440 | tf_op jit(solution)/shard_map/ppermute | solution.py:295
  33.4 11.8 %collective-permute-start.7 = (bf16[2,2,256,128]{3,2,1,0:T(8,128)(2,1)S(1)}, bf16[2,2,256,128]{3,2,1,0:T(8,128)(2,1)S(1)}, u32[]{:S(2)}, u32[]{:S(2)}) collective-permute-start(bf16[2,2,256,128]{3,2,1,0:T(8,128)(2,1)S(1)} %get-tuple-element.16), channel_id=1, source_target_pairs={{0,6},{2,4},{4,2},{6,0},{8,14},{10,12},{12,10},{14,8},{1,7},{3,5},... | collective-permute-start | bytes 786440 | tf_op jit(solution)/shard_map/ppermute | solution.py:295
  35.7 0.7 %copy-start.7 = (f32[64]{0:T(128)S(1)}, f32[64]{0:T(128)}, u32[]{:S(2)}) copy-start(f32[64]{0:T(128)} %param.24) | copy-start | bytes 772
  35.8 0.7 %copy-start.8 = (f32[64]{0:T(128)S(1)}, f32[64]{0:T(128)}, u32[]{:S(2)}) copy-start(f32[64]{0:T(128)} %param.23) | copy-start | bytes 772
  35.8 0.7 %copy-start.9 = (f32[64]{0:T(128)S(1)}, f32[64]{0:T(128)}, u32[]{:S(2)}) copy-start(f32[64]{0:T(128)} %param.22) | copy-start | bytes 772
  36.5 0.7 %copy-start.3 = (f32[64,32]{0,1:T(8,128)S(1)}, f32[64,32]{0,1:T(8,128)}, u32[]{:S(2)}) copy-start(f32[64,32]{0,1:T(8,128)} %param.25) | copy-start | bytes 24580

commit v5 on v4

--- a/solution.py
+++ b/solution.py
@@ -52,7 +52,7 @@
 
 def prepare_kernel(
     rows, x_ref, z_ref, dt_ref, b_ref, c_ref, head_ref,
-    base_ref, carry_ref, gate_ref, left_ref, right_ref, seen_ref,
+    base_ref, carry_ref, gate_ref, left_ref, right_ref, seen_ref, head_of_ref, channel_of_ref,
 ):
     both, flat = x_ref.shape
     steps = both // rows
@@ -60,6 +60,14 @@
     entries = b_ref.shape[2]
     width = flat // groups
     row = lax.broadcasted_iota(jnp.int32, (both, 1), 0)
+    heads, channels = head_of_ref.shape[1], channel_of_ref.shape[0]
+    lane = lax.broadcasted_iota(jnp.int32, (flat, heads), 0)
+    first = lax.broadcasted_iota(jnp.int32, (flat, heads), 1) * channels
+    inside = (lane >= first) & (lane < first + channels)
+    head_of_ref[...] = jnp.where(inside, 1.0, 0.0).astype(BF16)
+    lane = lax.broadcasted_iota(jnp.int32, (channels, flat), 1) % channels
+    channel = lax.broadcasted_iota(jnp.int32, (channels, flat), 0)
+    channel_of_ref[...] = jnp.where(lane == channel, 1.0, 0.0).astype(BF16)
 
     def earlier(value, by):
         return value if by == 0 else pltpu.roll(value, by * rows, 0)
@@ -132,12 +140,14 @@
     return pl.pallas_call(
         functools.partial(prepare_kernel, rows),
         in_specs=[VMEM] * 6,
-        out_specs=[VMEM] * 6,
+        out_specs=[VMEM] * 8,
         out_shape=[
             wide(both, flat), wide(both, flat), wide(both, flat),
             jax.ShapeDtypeStruct((6 * both, flat), BF16),
             wide(groups, 6 * both, 2 * rows * entries),
             wide(groups, both, rows * entries),
+            jax.ShapeDtypeStruct((flat, heads), BF16),
+            jax.ShapeDtypeStruct((channels, flat), BF16),
         ],
         compiler_params=pltpu.CompilerParams(vmem_limit_bytes=4 * 1024 * 1024),
     )(
@@ -154,8 +164,9 @@
     left_ref, right_ref, seen_ref = refs[:3]
     span, entries = recv_refs[0].shape[2:]
     if last:
-        base_ref, carry_ref, gate_ref, gain_ref, before_ref = refs[3:8]
-        decoded_ref, final_ref, ready, seen, out_sem = refs[-5:]
+        (base_ref, carry_ref, gate_ref, gain_ref, head_of_ref, channel_of_ref,
+         before_ref) = refs[3:10]
+        decoded_ref, final_ref, ready, seen, out_sem, turned, turn_sem = refs[-7:]
         seen[...] = before_ref[...]
     else:
         resident_ref = refs[3]
@@ -220,6 +231,7 @@
                     r, g, stay[r, pl.ds(at, span)], quarter, at).start())
 
     if last:
+        normed = []
         for g in range(groups):
             lanes = slice(g * block, (g + 1) * block)
             total = seen[0, :, lanes]
@@ -228,8 +240,17 @@
             readout = carry_ref[:, lanes] * total + base_ref[:, lanes]
             gated = readout * gate_ref[:, lanes]
             squares = jnp.mean(gated * gated, axis=1, keepdims=True)
-            normed = gated * lax.rsqrt(squares + 1e-05) * gain_ref[:, lanes]
-            decoded_ref[:, lanes] = normed.astype(BF16)
+            normed.append(gated * lax.rsqrt(squares + 1e-05) * gain_ref[:, lanes])
+        normed = jnp.concatenate(normed, axis=1)
+        both, flat = normed.shape
+        channels = channel_of_ref.shape[0]
+        spread = jnp.broadcast_to(normed[:, None], (both, channels, flat)).astype(BF16)
+        spread = spread * channel_of_ref[...][None]
+        turned[...] = jnp.dot(
+            spread.reshape(both * channels, flat), head_of_ref[...],
+            preferred_element_type=F32).astype(BF16).reshape(turned.shape)
+        turn = pltpu.make_async_copy(turned, decoded_ref, turn_sem)
+        turn.start()
     for r in range(rows):
 
         @pl.when(info_ref[r] == 1)
@@ -241,29 +262,33 @@
             @pl.when(info_ref[r] == 0)
             def _():
                 staying_row(r, lambda quarter, g, at: written(r, quarter, g, at).wait())
+    if last:
+        turn.wait()
 
 
 def decode(parts, info, recv, resident, ready, gain, earlier):
     rows, flat, entries = resident.shape
     groups, span = recv[0].shape[1:3]
-    base, carry, gate, left, right, seen = ready
+    base, carry, gate, left, right, seen, head_of, channel_of = ready
     both = base.shape[0]
     last = len(earlier) > 0
     operands = [info, *recv, left, right, seen]
-    operands += [base, carry, gate, gain, *earlier] if last else [resident]
+    operands += (
+        [base, carry, gate, gain, head_of, channel_of, *earlier] if last else [resident])
+    turned = (both, channel_of.shape[0], head_of.shape[1])
     slots = len(parts) if last else flat // groups // span
     final = jax.ShapeDtypeStruct((rows, flat, entries), BF16)
     return pl.pallas_call(
         functools.partial(decode_kernel, rows, groups, parts, last),
         in_specs=[SMEM] + [VMEM] * (len(operands) - 2) + [ANY],
-        out_specs=[VMEM, ANY] if last else [ANY, VMEM],
+        out_specs=[ANY, ANY] if last else [ANY, VMEM],
         input_output_aliases={len(operands) - 1: 1} if last else {},
         scratch_shapes=[pltpu.VMEM((slots, rows, groups, span, entries), BF16)]
         + [pltpu.VMEM((rows, both, flat), F32)] * last
         + [pltpu.SemaphoreType.DMA((slots, rows, groups))]
-        + ([] if last else [
+        + ([pltpu.VMEM(turned, BF16), pltpu.SemaphoreType.DMA(())] if last else [
             pltpu.VMEM((rows, flat, entries), BF16), pltpu.SemaphoreType.DMA((rows,))]),
-        out_shape=[jax.ShapeDtypeStruct((both, flat), BF16), final] if last
+        out_shape=[jax.ShapeDtypeStruct(turned, BF16), final] if last
         else [final, jax.ShapeDtypeStruct((rows, both, flat), F32)],
         compiler_params=pltpu.CompilerParams(vmem_limit_bytes=8 * 1024 * 1024),
     )(*operands)
@@ -298,8 +323,9 @@
     here = jnp.arange(shards * row_count, dtype=jnp.int32) // row_count
     few = shards == 8
     if few:
-        arrived = [pieces[:, 0]] + [
-            hand(pieces[:, k % quarter], k) for k in range(1, shards)]
+        first, rest = lax.optimization_barrier((pieces[:, 1], pieces))
+        cut = [rest[:, 0], first, rest[:, 2], rest[:, 3]]
+        arrived = [cut[0]] + [hand(cut[k % quarter], k) for k in range(1, shards)]
         held = jnp.stack(arrived)
         order = jnp.arange(quarter)[:, None] ^ (me % quarter)
         order = (order * row_count + jnp.arange(row_count)).reshape(half_rows)
@@ -334,7 +360,9 @@
     gain = norm_gain.reshape(1, flat)
     final, seen = decode((0, 1, 2), info, recv[:3], resident, ready, gain, ())
     decoded, final = decode((3,), info, recv[3:], resident, ready, gain, (seen, final))
-    return (decoded.reshape(x_new.shape), final.reshape(resident_states.shape))
+    steps = x_new.shape[0]
+    decoded = decoded.reshape(steps, row_count, channels, local_heads)
+    return (jnp.swapaxes(decoded, 2, 3), final.reshape(resident_states.shape))
 
 
 def solution(mesh):

time: 48 us -> 47.2 us (0.983)
  waiting for transfers between devices: 18.3 us -> 17.2 us
  Pallas kernels: 4.67 us -> 5.67 us
  starting transfers between devices: 16.1 us -> 15.6 us
    ppermute x10, waiting for transfers between devices: 18.3 us -> 17.2 us  [hand(): return lax.ppermute(value, 'rows', [(i, i ^ k) for i in range(shards)])]
    squeeze x1 -> x2, local copies, waits for them, and re-layouts: 1.14 us -> 1.98 us  [the longest x1 1.06 us: local(): cut = [rest[:, 0], first, rest[:, 2], rest[:, 3]]]
    unnamed x35 -> x34, local copies, waits for them, and re-layouts: 4.08 us -> 3.34 us
    pallas_call x2, Pallas kernels: 3.84 us -> 4.35 us  [decode(): pl.pallas_call(functools.partial(decode_kernel, rows, groups, parts, last...]
    ppermute x10, starting transfers between devices: 16.1 us -> 15.6 us  [hand(): return lax.ppermute(value, 'rows', [(i, i ^ k) for i in range(shards)])]
    pallas_call x1, Pallas kernels: 0.22 us -> 0.71 us  [prepare(): pl.pallas_call(functools.partial(prepare_kernel, rows), in_specs=[VMEM] *...]
  transfers between devices with their start and end apart: 10 -> 10, of which waited for: 6 -> 6; matrix products, arithmetic and copies ran while one was open for 8% -> 10% of each run, Pallas kernels for 5% -> 6%
where the time goes in v5:
time: 47.2 us; the launch traced here: 47 us
  waiting for transfers between devices  17.2 us (36%)
  starting transfers between devices  15.6 us (33%)
  local copies, waits for them, and re-layouts  7.21 us (15%)
  Pallas kernels  5.67 us (12%)
  between operations  0.93 us (2%)
    ppermute x10, waiting for transfers between devices, hand(): return lax.ppermute(value, 'rows', [(i, i ^ k) for i in range(shards)])  17.2 us
    ppermute x10, starting transfers between devices, hand(): return lax.ppermute(value, 'rows', [(i, i ^ k) for i in range(shards)])  15.6 us
    pallas_call x2, Pallas kernels, decode(): pl.pallas_call(functools.partial(decode_kernel, rows, groups, parts, last...  4.35 us
    unnamed x34, local copies, waits for them, and re-layouts  3.34 us
    squeeze x1, local copies, waits for them, and re-layouts, local(): cut = [rest[:, 0], first, rest[:, 2], rest[:, 3]]  1.06 us
  transfers between devices with their start and end apart: 10, of which 6 were waited for; matrix products, arithmetic and copies ran while one was open for 10% of the time, Pallas kernels for 6%

profile of v5, /device:TPU:0, one launch (start us, length us, event | category | flops | bytes accessed | tf_op | source)
XLA Modules:
  0.0 47.0 jit_solution(16055864305733793738)
XLA Ops:
  0.6 0.9 %slice_bitcast_fusion.2 = bf16[2,256,128]{2,1,0:T(8,128)(2,1)S(1)} fusion(bf16[2,4,256,128]{3,2,1,0:T(8,128)(2,1)} %bitcast.52), kind=kLoop, calls=%fused_computation.3 | loop fusion | bytes 262144 | tf_op jit(solution)/shard_map/squeeze | solution.py:326
  1.6 3.0 %collective-permute-start = (bf16[2,256,128]{2,1,0:T(8,128)(2,1)S(1)}, bf16[2,256,128]{2,1,0:T(8,128)(2,1)S(1)}, u32[]{:S(2)}, u32[]{:S(2)}) collective-permute-start(bf16[2,256,128]{2,1,0:T(8,128)(2,1)S(1)} %slice_bitcast_fusion.2), channel_id=1, source_target_pairs={{0,2},{2,0},{4,6},{6,4},{8,10},{10,8},{12,14},{14,12},{1,3},{3,1},... | collective-permute-start | bytes 393224 | tf_op jit(solution)/shard_map/ppermute | solution.py:320
  4.6 2.6 %collective-permute-start.4 = (bf16[2,256,128]{2,1,0:T(8,128)(2,1)S(1)}, bf16[2,256,128]{2,1,0:T(8,128)(2,1)S(1)}, u32[]{:S(2)}, u32[]{:S(2)}) collective-permute-start(bf16[2,256,128]{2,1,0:T(8,128)(2,1)S(1)} %slice_bitcast_fusion.2), channel_id=1, source_target_pairs={{0,10},{2,8},{4,14},{6,12},{8,2},{10,0},{12,6},{14,4},{1,11},{3,9}... | collective-permute-start | bytes 393224 | tf_op jit(solution)/shard_map/ppermute | solution.py:320
  7.1 1.1 %slice_bitcast_fusion.3 = (bf16[2,256,128]{2,1,0:T(8,128)(2,1)S(1)}, bf16[2,256,128]{2,1,0:T(8,128)(2,1)S(1)}, bf16[2,256,128]{2,1,0:T(8,128)(2,1)S(1)}) fusion(bf16[2,4,256,128]{3,2,1,0:T(8,128)(2,1)} %bitcast.53), kind=kLoop, calls=%fused_computation.12 | loop fusion | bytes 786432 | tf_op jit(solution)/shard_map/squeeze | solution.py:327
  8.2 1.6 %collective-permute-start.1 = (bf16[2,256,128]{2,1,0:T(8,128)(2,1)S(1)}, bf16[2,256,128]{2,1,0:T(8,128)(2,1)S(1)}, u32[]{:S(2)}, u32[]{:S(2)}) collective-permute-start(bf16[2,256,128]{2,1,0:T(8,128)(2,1)S(1)} %get-tuple-element.40), channel_id=1, source_target_pairs={{0,4},{2,6},{4,0},{6,2},{8,12},{10,14},{12,8},{14,10},{1,5},{3,7},... | collective-permute-start | bytes 393224 | tf_op jit(solution)/shard_map/ppermute | solution.py:320
  9.8 1.8 %collective-permute-start.2 = (bf16[2,256,128]{2,1,0:T(8,128)(2,1)S(1)}, bf16[2,256,128]{2,1,0:T(8,128)(2,1)S(1)}, u32[]{:S(2)}, u32[]{:S(2)}) collective-permute-start(bf16[2,256,128]{2,1,0:T(8,128)(2,1)S(1)} %get-tuple-element.39), channel_id=1, source_target_pairs={{0,6},{2,4},{4,2},{6,0},{8,14},{10,12},{12,10},{14,8},{1,7},{3,5},... | collective-permute-start | bytes 393224 | tf_op jit(solution)/shard_map/ppermute | solution.py:320
  11.6 0.9 %bitcast_dynamic-update-slice_fusion.7 = bf16[8,2,256,128]{3,2,1,0:T(8,128)(2,1)S(1)} fusion(bf16[2,4,256,128]{3,2,1,0:T(8,128)(2,1)} %bitcast.54), kind=kLoop, calls=%fused_computation.11 | loop fusion | bytes 262144
  12.6 0.1 iota_add_fusion
  12.7 0.1 add.64
  12.8 0.6 %copy-done.10 = s32[8]{0:T(128)S(1)} copy-done((s32[8]{0:T(128)S(1)}, s32[8]{0:T(128)}, u32[]{:S(2)}) %copy-start.10) | copy-done | bytes 56
  13.4 0.0 copy-done.11
  13.4 0.1 select_reduce_fusion
  13.6 0.1 dynamic_slice.17
  13.6 0.6 %gather_fusion = s32[8]{0:T(128)S(1)} fusion(s32[8]{0:T(128)S(1)} %dynamic_slice.17, s32[1024]{0:T(1024)S(1)} %pad_clamp_fusion), kind=kCustom, calls=%fused_computation | custom fusion | bytes 96 | tf_op jit(solution)/shard_map/gather | solution.py:332
  14.3 0.1 fusion
  14.4 3.0 %collective-permute-start.6 = (bf16[2,256,128]{2,1,0:T(8,128)(2,1)S(1)}, bf16[2,256,128]{2,1,0:T(8,128)(2,1)S(1)}, u32[]{:S(2)}, u32[]{:S(2)}) collective-permute-start(bf16[2,256,128]{2,1,0:T(8,128)(2,1)S(1)} %get-tuple-element.39), channel_id=1, source_target_pairs={{0,14},{2,12},{4,10},{6,8},{8,6},{10,4},{12,2},{14,0},{1,15},{3,13... | collective-permute-start | bytes 393224 | tf_op jit(solution)/shard_map/ppermute | solution.py:320
  17.4 1.1 %collective-permute-done.1 = bf16[2,256,128]{2,1,0:T(8,128)(2,1)S(1)} collective-permute-done((bf16[2,256,128]{2,1,0:T(8,128)(2,1)S(1)}, bf16[2,256,128]{2,1,0:T(8,128)(2,1)S(1)}, u32[]{:S(2)}, u32[]{:S(2)}) %collective-permute-start.1) | collective-permute-done | bytes 131104 | tf_op jit(solution)/shard_map/ppermute | solution.py:320
  18.5 4.8 %collective-permute-done.2 = bf16[2,256,128]{2,1,0:T(8,128)(2,1)S(1)} collective-permute-done((bf16[2,256,128]{2,1,0:T(8,128)(2,1)S(1)}, bf16[2,256,128]{2,1,0:T(8,128)(2,1)S(1)}, u32[]{:S(2)}, u32[]{:S(2)}) %collective-permute-start.2) | collective-permute-done | bytes 131104 | tf_op jit(solution)/shard_map/ppermute | solution.py:320
  23.3 6.7 %collective-permute-done.3 = bf16[2,256,128]{2,1,0:T(8,128)(2,1)S(1)} collective-permute-done((bf16[2,256,128]{2,1,0:T(8,128)(2,1)S(1)}, bf16[2,256,128]{2,1,0:T(8,128)(2,1)S(1)}, u32[]{:S(2)}, u32[]{:S(2)}) %collective-permute-start.3) | collective-permute-done | bytes 131104 | tf_op jit(solution)/shard_map/ppermute | solution.py:320
  30.2 0.0 copy-start.6
  30.2 0.0 copy-start.4
  30.2 0.6 %shard_map.140 = (bf16[2,2,256,128]{3,2,1,0:T(8,128)(2,1)S(1)}, bf16[2,2,256,128]{3,2,1,0:T(8,128)(2,1)S(1)}, bf16[2,2,256,128]{3,2,1,0:T(8,128)(2,1)S(1)}, bf16[2,2,256,128]{3,2,1,0:T(8,128)(2,1)S(1)}) custom-call(s32[8]{0:T(128)S(1)} %gather_fusion, bf16[8,2,256,128]{3,2,1,0:T(8,128)(2,1)S(1)} %bitcast_dynamic-update-slice_fusion.held_ref), custom_call_target="tpu_custom_call" | custom-call | tf_op jit(solution)/shard_map/pallas_call | solution.py:35
  30.9 1.6 %collective-permute-start.8 = (bf16[2,2,256,128]{3,2,1,0:T(8,128)(2,1)S(1)}, bf16[2,2,256,128]{3,2,1,0:T(8,128)(2,1)S(1)}, u32[]{:S(2)}, u32[]{:S(2)}) collective-permute-start(bf16[2,2,256,128]{3,2,1,0:T(8,128)(2,1)S(1)} %get-tuple-element.32), channel_id=1, source_target_pairs={{0,2},{2,0},{4,6},{6,4},{8,10},{10,8},{12,14},{14,12},{1,3},{3,1},... | collective-permute-start | bytes 786440 | tf_op jit(solution)/shard_map/ppermute | solution.py:320
  32.4 0.7 %collective-permute-start.9 = (bf16[2,2,256,128]{3,2,1,0:T(8,128)(2,1)S(1)}, bf16[2,2,256,128]{3,2,1,0:T(8,128)(2,1)S(1)}, u32[]{:S(2)}, u32[]{:S(2)}) collective-permute-start(bf16[2,2,256,128]{3,2,1,0:T(8,128)(2,1)S(1)} %get-tuple-element.33), channel_id=1, source_target_pairs={{0,4},{2,6},{4,0},{6,2},{8,12},{10,14},{12,8},{14,10},{1,5},{3,7},... | collective-permute-start | bytes 786440 | tf_op jit(solution)/shard_map/ppermute | solution.py:320
  33.2 1.3 %collective-permute-start.7 = (bf16[2,2,256,128]{3,2,1,0:T(8,128)(2,1)S(1)}, bf16[2,2,256,128]{3,2,1,0:T(8,128)(2,1)S(1)}, u32[]{:S(2)}, u32[]{:S(2)}) collective-permute-start(bf16[2,2,256,128]{3,2,1,0:T(8,128)(2,1)S(1)} %get-tuple-element.22), channel_id=1, source_target_pairs={{0,6},{2,4},{4,2},{6,0},{8,14},{10,12},{12,10},{14,8},{1,7},{3,5},... | collective-permute-start | bytes 786440 | tf_op jit(solution)/shard_map/ppermute | solution.py:320
  34.4 0.1 dynamic_slice.16
  34.5 0.1 dynamic_slice.15
  34.6 0.1 broadcast_in_dim.34
  34.7 0.1 reshape.81.dt_ref
  34.9 0.1 copy.34
  35.0 0.2 reshape.79.x_ref
  35.2 0.1 copy.35
  35.4 0.2 reshape.80.z_ref
  35.6 0.6 %copy-done.7 = f32[64]{0:T(128)S(1)} copy-done((f32[64]{0:T(128)S(1)}, f32[64]{0:T(128)}, u32[]{:S(2)}) %copy-start.7) | copy-done | bytes 280
  36.2 0.0 copy-done.8
  36.2 0.0 copy-done.9
  36.2 0.1 broadcast_in_dim.35
  36.3 0.1 reshape.84.head_ref
  36.4 0.6 %copy-done.3 = f32[64,32]{0,1:T(8,128)S(1)} copy-done((f32[64,32]{0,1:T(8,128)S(1)}, f32[64,32]{0,1:T(8,128)}, u32[]{:S(2)}) %copy-start.3) | copy-done | bytes 8216
  37.0 0.1 copy.38
  37.1 0.1 reshape.85.refs_7_
  37.2 0.7 %shard_map.141 = (f32[8,2048]{1,0:T(8,128)S(1)}, f32[8,2048]{1,0:T(8,128)S(1)}, f32[8,2048]{1,0:T(8,128)S(1)}, bf16[48,2048]{1,0:T(8,128)(2,1)S(1)}, bf16[2,48,5...) custom-call(bf16[8,2048]{1,0:T(8,128)(2,1)S(1)} %reshape.79.x_ref, ...), custom_call_target="tpu_custom_call" | custom-call | tf_op jit(solution)/shard_map/pallas_call | solution.py:140
  37.9 0.1 pad_add_fusion.info_ref
  38.0 1.3 %collective-permute-done.8.refs_1_ = bf16[2,2,256,128]{3,2,1,0:T(8,128)(2,1)S(1)} collective-permute-done((bf16[2,2,256,128]{3,2,1,0:T(8,128)(2,1)S(1)}, bf16[2,2,256,128]{3,2,1,0:T(8,128)(2,1)S(1)}, u32[]{:S(2)}, u32[]{:S(2)}) %collective-permute-start.8) | collective-permute-done | bytes 262176 | tf_op jit(solution)/shard_map/ppermute | solution.py:320
  39.3 2.4 %collective-permute-done.9.refs_2_ = bf16[2,2,256,128]{3,2,1,0:T(8,128)(2,1)S(1)} collective-permute-done((bf16[2,2,256,128]{3,2,1,0:T(8,128)(2,1)S(1)}, bf16[2,2,256,128]{3,2,1,0:T(8,128)(2,1)S(1)}, u32[]{:S(2)}, u32[]{:S(2)}) %collective-permute-start.9) | collective-permute-done | bytes 262176 | tf_op jit(solution)/shard_map/ppermute | solution.py:320
  41.7 2.3 %shard_map.142 = (bf16[2,2048,128]{2,1,0:T(8,128)(2,1)}, f32[2,8,2048]{2,1,0:T(8,128)S(1)}) custom-call(s32[4]{0:T(128)S(1)} %pad_add_fusion.info_ref, bf16[2,2,256,128]{3,2,1,0:T(8,128)(2,1)S(1)} %get-tuple-element.31.refs_0_, bf16[2,2,256,128]{3,2,1,0:T(8,128)(2,1)S(1)} %collective-permute-done.8.refs_1_, ...), custom_call_target="tpu_custom_call" | custom-call | tf_op jit(solution)/shard_map/pallas_call | solution.py:281
  44.0 0.9 %collective-permute-done.7.refs_0_ = bf16[2,2,256,128]{3,2,1,0:T(8,128)(2,1)S(1)} collective-permute-done((bf16[2,2,256,128]{3,2,1,0:T(8,128)(2,1)S(1)}, bf16[2,2,256,128]{3,2,1,0:T(8,128)(2,1)S(1)}, u32[]{:S(2)}, u32[]{:S(2)}) %collective-permute-start.7) | collective-permute-done | bytes 262176 | tf_op jit(solution)/shard_map/ppermute | solution.py:320
  45.0 2.0 %shard_map.143 = (bf16[8,32,64]{2,1,0:T(8,128)(2,1)}, bf16[2,2048,128]{2,1,0:T(8,128)(2,1)}) custom-call(s32[4]{0:T(128)S(1)} %pad_add_fusion.info_ref, bf16[2,2,256,128]{3,2,1,0:T(8,128)(2,1)S(1)} %collective-permute-done.7.refs_0_, bf16[48,2048]{1,0:T(8,128)(2,1)S(1)} %get-tuple-element.23.refs_3_.refs_1_, ...), custom_call_target="tpu_custom_call", output_to_operand_aliasing={{1}: (12, {})} | custom-call | tf_op jit(solution)/shard_map/pallas_call | solution.py:281
  (38 shorter events, 0.3 us)
Async XLA Ops:
  1.6 12.8 %collective-permute-start = (bf16[2,256,128]{2,1,0:T(8,128)(2,1)S(1)}, bf16[2,256,128]{2,1,0:T(8,128)(2,1)S(1)}, u32[]{:S(2)}, u32[]{:S(2)}) collective-permute-start(bf16[2,256,128]{2,1,0:T(8,128)(2,1)S(1)} %slice_bitcast_fusion.2), channel_id=1, source_target_pairs={{0,2},{2,0},{4,6},{6,4},{8,10},{10,8},{12,14},{14,12},{1,3},{3,1},... | collective-permute-start | bytes 393224 | tf_op jit(solution)/shard_map/ppermute | solution.py:320
  4.6 25.5 %collective-permute-start.4 = (bf16[2,256,128]{2,1,0:T(8,128)(2,1)S(1)}, bf16[2,256,128]{2,1,0:T(8,128)(2,1)S(1)}, u32[]{:S(2)}, u32[]{:S(2)}) collective-permute-start(bf16[2,256,128]{2,1,0:T(8,128)(2,1)S(1)} %slice_bitcast_fusion.2), channel_id=1, source_target_pairs={{0,10},{2,8},{4,14},{6,12},{8,2},{10,0},{12,6},{14,4},{1,11},{3,9}... | collective-permute-start | bytes 393224 | tf_op jit(solution)/shard_map/ppermute | solution.py:320
  8.2 10.3 %collective-permute-start.1 = (bf16[2,256,128]{2,1,0:T(8,128)(2,1)S(1)}, bf16[2,256,128]{2,1,0:T(8,128)(2,1)S(1)}, u32[]{:S(2)}, u32[]{:S(2)}) collective-permute-start(bf16[2,256,128]{2,1,0:T(8,128)(2,1)S(1)} %get-tuple-element.40), channel_id=1, source_target_pairs={{0,4},{2,6},{4,0},{6,2},{8,12},{10,14},{12,8},{14,10},{1,5},{3,7},... | collective-permute-start | bytes 393224 | tf_op jit(solution)/shard_map/ppermute | solution.py:320
  9.8 20.3 %collective-permute-start.5 = (bf16[2,256,128]{2,1,0:T(8,128)(2,1)S(1)}, bf16[2,256,128]{2,1,0:T(8,128)(2,1)S(1)}, u32[]{:S(2)}, u32[]{:S(2)}) collective-permute-start(bf16[2,256,128]{2,1,0:T(8,128)(2,1)S(1)} %get-tuple-element.40), channel_id=1, source_target_pairs={{0,12},{2,14},{4,8},{6,10},{8,4},{10,6},{12,0},{14,2},{1,13},{3,15... | collective-permute-start | bytes 393224 | tf_op jit(solution)/shard_map/ppermute | solution.py:320
  9.8 13.4 %collective-permute-start.2 = (bf16[2,256,128]{2,1,0:T(8,128)(2,1)S(1)}, bf16[2,256,128]{2,1,0:T(8,128)(2,1)S(1)}, u32[]{:S(2)}, u32[]{:S(2)}) collective-permute-start(bf16[2,256,128]{2,1,0:T(8,128)(2,1)S(1)} %get-tuple-element.39), channel_id=1, source_target_pairs={{0,6},{2,4},{4,2},{6,0},{8,14},{10,12},{12,10},{14,8},{1,7},{3,5},... | collective-permute-start | bytes 393224 | tf_op jit(solution)/shard_map/ppermute | solution.py:320
  12.7 0.7 %copy-start.10 = (s32[8]{0:T(128)S(1)}, s32[8]{0:T(128)}, u32[]{:S(2)}) copy-start(s32[8]{0:T(128)} %param.14) | copy-start | bytes 100
  12.7 0.7 %copy-start.11 = (s32[8]{0:T(128)S(1)}, s32[8]{0:T(128)}, u32[]{:S(2)}) copy-start(s32[8]{0:T(128)} %param.15) | copy-start | bytes 100
  14.4 15.8 %collective-permute-start.6 = (bf16[2,256,128]{2,1,0:T(8,128)(2,1)S(1)}, bf16[2,256,128]{2,1,0:T(8,128)(2,1)S(1)}, u32[]{:S(2)}, u32[]{:S(2)}) collective-permute-start(bf16[2,256,128]{2,1,0:T(8,128)(2,1)S(1)} %get-tuple-element.39), channel_id=1, source_target_pairs={{0,14},{2,12},{4,10},{6,8},{8,6},{10,4},{12,2},{14,0},{1,15},{3,13... | collective-permute-start | bytes 393224 | tf_op jit(solution)/shard_map/ppermute | solution.py:320
  18.5 11.6 %collective-permute-start.3 = (bf16[2,256,128]{2,1,0:T(8,128)(2,1)S(1)}, bf16[2,256,128]{2,1,0:T(8,128)(2,1)S(1)}, u32[]{:S(2)}, u32[]{:S(2)}) collective-permute-start(bf16[2,256,128]{2,1,0:T(8,128)(2,1)S(1)} %get-tuple-element.38), channel_id=1, source_target_pairs={{0,8},{2,10},{4,12},{6,14},{8,0},{10,2},{12,4},{14,6},{1,9},{3,11}... | collective-permute-start | bytes 393224 | tf_op jit(solution)/shard_map/ppermute | solution.py:320
  30.2 4.3 %copy-start.5 = (bf16[4,2,4,128]{3,2,1,0:T(4,128)(2,1)S(1)}, bf16[4,2,4,128]{3,2,1,0:T(4,128)(2,1)}, u32[]{:S(2)}) copy-start(bf16[4,2,4,128]{3,2,1,0:T(4,128)(2,1)} %param.21) | copy-start | bytes 24580
  30.2 4.2 %copy-start.6 = (bf16[4,2,4,128]{3,2,1,0:T(4,128)(2,1)S(1)}, bf16[4,2,4,128]{3,2,1,0:T(4,128)(2,1)}, u32[]{:S(2)}) copy-start(bf16[4,2,4,128]{3,2,1,0:T(4,128)(2,1)} %param.20) | copy-start | bytes 24580
  30.2 4.4 %copy-start.4 = (f32[4,2,64]{2,1,0:T(2,128)S(1)}, f32[4,2,64]{2,1,0:T(2,128)}, u32[]{:S(2)}) copy-start(f32[4,2,64]{2,1,0:T(2,128)} %param.19) | copy-start | bytes 6148
  30.2 4.7 %copy-start.1 = (bf16[4,2,64,32]{2,3,1,0:T(8,128)(2,1)S(1)}, bf16[4,2,64,32]{2,3,1,0:T(8,128)(2,1)}, u32[]{:S(2)}) copy-start(bf16[4,2,64,32]{2,3,1,0:T(8,128)(2,1)} %param.17) | copy-start | bytes 98308
  30.2 5.0 %copy-start.2 = (bf16[4,2,64,32]{2,3,1,0:T(8,128)(2,1)S(1)}, bf16[4,2,64,32]{2,3,1,0:T(8,128)(2,1)}, u32[]{:S(2)}) copy-start(bf16[4,2,64,32]{2,3,1,0:T(8,128)(2,1)} %param.18) | copy-start | bytes 98308
  30.8 10.8 %copy-start = (bf16[2,64,32,128]{3,2,1,0:T(8,128)(2,1)S(1)}, bf16[2,64,32,128]{3,2,1,0:T(8,128)(2,1)}, u32[]{:S(2)}) copy-start(bf16[2,64,32,128]{3,2,1,0:T(8,128)(2,1)} %param.16) | copy-start | bytes 3145732
  30.9 8.4 %collective-permute-start.8 = (bf16[2,2,256,128]{3,2,1,0:T(8,128)(2,1)S(1)}, bf16[2,2,256,128]{3,2,1,0:T(8,128)(2,1)S(1)}, u32[]{:S(2)}, u32[]{:S(2)}) collective-permute-start(bf16[2,2,256,128]{3,2,1,0:T(8,128)(2,1)S(1)} %get-tuple-element.32), channel_id=1, source_target_pairs={{0,2},{2,0},{4,6},{6,4},{8,10},{10,8},{12,14},{14,12},{1,3},{3,1},... | collective-permute-start | bytes 786440 | tf_op jit(solution)/shard_map/ppermute | solution.py:320
  32.4 9.2 %collective-permute-start.9 = (bf16[2,2,256,128]{3,2,1,0:T(8,128)(2,1)S(1)}, bf16[2,2,256,128]{3,2,1,0:T(8,128)(2,1)S(1)}, u32[]{:S(2)}, u32[]{:S(2)}) collective-permute-start(bf16[2,2,256,128]{3,2,1,0:T(8,128)(2,1)S(1)} %get-tuple-element.33), channel_id=1, source_target_pairs={{0,4},{2,6},{4,0},{6,2},{8,12},{10,14},{12,8},{14,10},{1,5},{3,7},... | collective-permute-start | bytes 786440 | tf_op jit(solution)/shard_map/ppermute | solution.py:320
  33.2 11.8 %collective-permute-start.7 = (bf16[2,2,256,128]{3,2,1,0:T(8,128)(2,1)S(1)}, bf16[2,2,256,128]{3,2,1,0:T(8,128)(2,1)S(1)}, u32[]{:S(2)}, u32[]{:S(2)}) collective-permute-start(bf16[2,2,256,128]{3,2,1,0:T(8,128)(2,1)S(1)} %get-tuple-element.22), channel_id=1, source_target_pairs={{0,6},{2,4},{4,2},{6,0},{8,14},{10,12},{12,10},{14,8},{1,7},{3,5},... | collective-permute-start | bytes 786440 | tf_op jit(solution)/shard_map/ppermute | solution.py:320
  35.5 0.7 %copy-start.7 = (f32[64]{0:T(128)S(1)}, f32[64]{0:T(128)}, u32[]{:S(2)}) copy-start(f32[64]{0:T(128)} %param.24) | copy-start | bytes 772
  35.5 0.7 %copy-start.8 = (f32[64]{0:T(128)S(1)}, f32[64]{0:T(128)}, u32[]{:S(2)}) copy-start(f32[64]{0:T(128)} %param.23) | copy-start | bytes 772
  35.5 0.7 %copy-start.9 = (f32[64]{0:T(128)S(1)}, f32[64]{0:T(128)}, u32[]{:S(2)}) copy-start(f32[64]{0:T(128)} %param.22) | copy-start | bytes 772
  36.3 0.7 %copy-start.3 = (f32[64,32]{0,1:T(8,128)S(1)}, f32[64,32]{0,1:T(8,128)}, u32[]{:S(2)}) copy-start(f32[64,32]{0,1:T(8,128)} %param.25) | copy-start | bytes 24580

commit v6 on v5

--- a/solution.py
+++ b/solution.py
@@ -21,7 +21,7 @@
         rows = out_ref.shape[0]
 
         def one(r):
-            out_ref[r] = held_ref[slots_ref[k * rows + r]]
+            out_ref[r] = held_ref[slots_ref[0, k * rows + r]]
 
         if rows <= 16:
             for r in range(rows):
@@ -34,11 +34,11 @@
     shape = (slots.shape[0] // parts,) + held.shape[1:]
     return pl.pallas_call(
         gather_kernel,
-        in_specs=[SMEM, VMEM],
+        in_specs=[VMEM if parts > 1 else SMEM, VMEM],
         out_specs=[VMEM] * parts,
         out_shape=[jax.ShapeDtypeStruct(shape, held.dtype)] * parts,
         compiler_params=pltpu.CompilerParams(vmem_limit_bytes=2 * 1024 * 1024),
-    )(slots, held)
+    )(slots[None], held)
 
 
 def split_terms(value):
@@ -159,7 +159,8 @@
     )
 
 
-def decode_kernel(rows, groups, parts, last, info_ref, *refs):
+def decode_kernel(rows, groups, parts, last, info_row, *refs):
+    info_ref = [info_row[0, i] for i in range(2 * rows)]
     recv_refs, refs = refs[:len(parts)], refs[len(parts):]
     left_ref, right_ref, seen_ref = refs[:3]
     span, entries = recv_refs[0].shape[2:]
@@ -280,7 +281,7 @@
     final = jax.ShapeDtypeStruct((rows, flat, entries), BF16)
     return pl.pallas_call(
         functools.partial(decode_kernel, rows, groups, parts, last),
-        in_specs=[SMEM] + [VMEM] * (len(operands) - 2) + [ANY],
+        in_specs=[VMEM] * (len(operands) - 1) + [ANY],
         out_specs=[ANY, ANY] if last else [ANY, VMEM],
         input_output_aliases={len(operands) - 1: 1} if last else {},
         scratch_shapes=[pltpu.VMEM((slots, rows, groups, span, entries), BF16)]
@@ -355,7 +356,7 @@
         a_rate, dt_bias, skip_d)
     info = jnp.concatenate([
         lax.dynamic_slice_in_dim(listed, me * row_count, row_count),
-        lax.dynamic_slice_in_dim(mask, me * row_count, row_count)])
+        lax.dynamic_slice_in_dim(mask, me * row_count, row_count)])[None]
     resident = resident_states.reshape(row_count, flat, entries)
     gain = norm_gain.reshape(1, flat)
     final, seen = decode((0, 1, 2), info, recv[:3], resident, ready, gain, ())

time: 47.2 us -> 46.4 us (0.983)
  Pallas kernels: 5.67 us -> 4.31 us
  waiting for transfers between devices: 17.2 us -> 17.7 us
    pallas_call x2, Pallas kernels: 4.35 us -> 3.44 us  [decode(): pl.pallas_call(functools.partial(decode_kernel, rows, groups, parts, last...]
where the time goes in v6:
time: 46.4 us; the launch traced here: 46.1 us
  waiting for transfers between devices  17.7 us (38%)
  starting transfers between devices  15.6 us (34%)
  local copies, waits for them, and re-layouts  7.21 us (16%)
  Pallas kernels  4.31 us (9%)
  between operations  0.93 us (2%)
    ppermute x10, waiting for transfers between devices, hand(): return lax.ppermute(value, 'rows', [(i, i ^ k) for i in range(shards)])  17.7 us
    ppermute x10, starting transfers between devices, hand(): return lax.ppermute(value, 'rows', [(i, i ^ k) for i in range(shards)])  15.6 us
    pallas_call x2, Pallas kernels, decode(): pl.pallas_call(functools.partial(decode_kernel, rows, groups, parts, last...  3.44 us
    unnamed x34, local copies, waits for them, and re-layouts  3.34 us
    squeeze x1, local copies, waits for them, and re-layouts, local(): cut = [rest[:, 0], first, rest[:, 2], rest[:, 3]]  1.06 us
  transfers between devices with their start and end apart: 10, of which 6 were waited for; matrix products, arithmetic and copies ran while one was open for 10% of the time, Pallas kernels for 6%

profile of v6, /device:TPU:0, one launch (start us, length us, event | category | flops | bytes accessed | tf_op | source)
XLA Modules:
  0.0 46.1 jit_solution(2658825265134691652)
XLA Ops:
  0.6 0.9 %slice_bitcast_fusion.2 = bf16[2,256,128]{2,1,0:T(8,128)(2,1)S(1)} fusion(bf16[2,4,256,128]{3,2,1,0:T(8,128)(2,1)} %bitcast.56), kind=kLoop, calls=%fused_computation.3 | loop fusion | bytes 262144 | tf_op jit(solution)/shard_map/squeeze | solution.py:327
  1.6 3.0 %collective-permute-start = (bf16[2,256,128]{2,1,0:T(8,128)(2,1)S(1)}, bf16[2,256,128]{2,1,0:T(8,128)(2,1)S(1)}, u32[]{:S(2)}, u32[]{:S(2)}) collective-permute-start(bf16[2,256,128]{2,1,0:T(8,128)(2,1)S(1)} %slice_bitcast_fusion.2), channel_id=1, source_target_pairs={{0,2},{2,0},{4,6},{6,4},{8,10},{10,8},{12,14},{14,12},{1,3},{3,1},... | collective-permute-start | bytes 393224 | tf_op jit(solution)/shard_map/ppermute | solution.py:321
  4.6 2.6 %collective-permute-start.4 = (bf16[2,256,128]{2,1,0:T(8,128)(2,1)S(1)}, bf16[2,256,128]{2,1,0:T(8,128)(2,1)S(1)}, u32[]{:S(2)}, u32[]{:S(2)}) collective-permute-start(bf16[2,256,128]{2,1,0:T(8,128)(2,1)S(1)} %slice_bitcast_fusion.2), channel_id=1, source_target_pairs={{0,10},{2,8},{4,14},{6,12},{8,2},{10,0},{12,6},{14,4},{1,11},{3,9}... | collective-permute-start | bytes 393224 | tf_op jit(solution)/shard_map/ppermute | solution.py:321
  7.1 1.1 %slice_bitcast_fusion.3 = (bf16[2,256,128]{2,1,0:T(8,128)(2,1)S(1)}, bf16[2,256,128]{2,1,0:T(8,128)(2,1)S(1)}, bf16[2,256,128]{2,1,0:T(8,128)(2,1)S(1)}) fusion(bf16[2,4,256,128]{3,2,1,0:T(8,128)(2,1)} %bitcast.57), kind=kLoop, calls=%fused_computation.12 | loop fusion | bytes 786432 | tf_op jit(solution)/shard_map/squeeze | solution.py:328
  8.2 1.6 %collective-permute-start.1 = (bf16[2,256,128]{2,1,0:T(8,128)(2,1)S(1)}, bf16[2,256,128]{2,1,0:T(8,128)(2,1)S(1)}, u32[]{:S(2)}, u32[]{:S(2)}) collective-permute-start(bf16[2,256,128]{2,1,0:T(8,128)(2,1)S(1)} %get-tuple-element.40), channel_id=1, source_target_pairs={{0,4},{2,6},{4,0},{6,2},{8,12},{10,14},{12,8},{14,10},{1,5},{3,7},... | collective-permute-start | bytes 393224 | tf_op jit(solution)/shard_map/ppermute | solution.py:321
  9.8 1.8 %collective-permute-start.2 = (bf16[2,256,128]{2,1,0:T(8,128)(2,1)S(1)}, bf16[2,256,128]{2,1,0:T(8,128)(2,1)S(1)}, u32[]{:S(2)}, u32[]{:S(2)}) collective-permute-start(bf16[2,256,128]{2,1,0:T(8,128)(2,1)S(1)} %get-tuple-element.39), channel_id=1, source_target_pairs={{0,6},{2,4},{4,2},{6,0},{8,14},{10,12},{12,10},{14,8},{1,7},{3,5},... | collective-permute-start | bytes 393224 | tf_op jit(solution)/shard_map/ppermute | solution.py:321
  11.6 0.9 %bitcast_dynamic-update-slice_fusion.7 = bf16[8,2,256,128]{3,2,1,0:T(8,128)(2,1)S(1)} fusion(bf16[2,4,256,128]{3,2,1,0:T(8,128)(2,1)} %bitcast.58), kind=kLoop, calls=%fused_computation.11 | loop fusion | bytes 262144
  12.6 0.1 iota_add_fusion
  12.7 0.1 add.64
  12.8 0.6 %copy-done.10 = s32[8]{0:T(128)S(1)} copy-done((s32[8]{0:T(128)S(1)}, s32[8]{0:T(128)}, u32[]{:S(2)}) %copy-start.10) | copy-done | bytes 56
  13.4 0.0 copy-done.11
  13.4 0.1 select_reduce_fusion
  13.6 0.1 dynamic_slice.17
  13.6 0.6 %gather_fusion = s32[8]{0:T(128)S(1)} fusion(s32[8]{0:T(128)S(1)} %dynamic_slice.17, s32[1024]{0:T(1024)S(1)} %pad_clamp_fusion), kind=kCustom, calls=%fused_computation | custom fusion | bytes 96 | tf_op jit(solution)/shard_map/gather | solution.py:333
  14.3 0.1 fusion
  14.4 3.0 %collective-permute-start.6 = (bf16[2,256,128]{2,1,0:T(8,128)(2,1)S(1)}, bf16[2,256,128]{2,1,0:T(8,128)(2,1)S(1)}, u32[]{:S(2)}, u32[]{:S(2)}) collective-permute-start(bf16[2,256,128]{2,1,0:T(8,128)(2,1)S(1)} %get-tuple-element.39), channel_id=1, source_target_pairs={{0,14},{2,12},{4,10},{6,8},{8,6},{10,4},{12,2},{14,0},{1,15},{3,13... | collective-permute-start | bytes 393224 | tf_op jit(solution)/shard_map/ppermute | solution.py:321
  17.4 1.1 %collective-permute-done.1 = bf16[2,256,128]{2,1,0:T(8,128)(2,1)S(1)} collective-permute-done((bf16[2,256,128]{2,1,0:T(8,128)(2,1)S(1)}, bf16[2,256,128]{2,1,0:T(8,128)(2,1)S(1)}, u32[]{:S(2)}, u32[]{:S(2)}) %collective-permute-start.1) | collective-permute-done | bytes 131104 | tf_op jit(solution)/shard_map/ppermute | solution.py:321
  18.5 4.8 %collective-permute-done.2 = bf16[2,256,128]{2,1,0:T(8,128)(2,1)S(1)} collective-permute-done((bf16[2,256,128]{2,1,0:T(8,128)(2,1)S(1)}, bf16[2,256,128]{2,1,0:T(8,128)(2,1)S(1)}, u32[]{:S(2)}, u32[]{:S(2)}) %collective-permute-start.2) | collective-permute-done | bytes 131104 | tf_op jit(solution)/shard_map/ppermute | solution.py:321
  23.3 6.7 %collective-permute-done.3 = bf16[2,256,128]{2,1,0:T(8,128)(2,1)S(1)} collective-permute-done((bf16[2,256,128]{2,1,0:T(8,128)(2,1)S(1)}, bf16[2,256,128]{2,1,0:T(8,128)(2,1)S(1)}, u32[]{:S(2)}, u32[]{:S(2)}) %collective-permute-start.3) | collective-permute-done | bytes 131104 | tf_op jit(solution)/shard_map/ppermute | solution.py:321
  30.2 0.0 copy-start.6
  30.2 0.0 copy-start.4
  30.2 0.2 shard_map.140
  30.4 1.6 %collective-permute-start.8 = (bf16[2,2,256,128]{3,2,1,0:T(8,128)(2,1)S(1)}, bf16[2,2,256,128]{3,2,1,0:T(8,128)(2,1)S(1)}, u32[]{:S(2)}, u32[]{:S(2)}) collective-permute-start(bf16[2,2,256,128]{3,2,1,0:T(8,128)(2,1)S(1)} %get-tuple-element.32), channel_id=1, source_target_pairs={{0,2},{2,0},{4,6},{6,4},{8,10},{10,8},{12,14},{14,12},{1,3},{3,1},... | collective-permute-start | bytes 786440 | tf_op jit(solution)/shard_map/ppermute | solution.py:321
  32.0 0.7 %collective-permute-start.9 = (bf16[2,2,256,128]{3,2,1,0:T(8,128)(2,1)S(1)}, bf16[2,2,256,128]{3,2,1,0:T(8,128)(2,1)S(1)}, u32[]{:S(2)}, u32[]{:S(2)}) collective-permute-start(bf16[2,2,256,128]{3,2,1,0:T(8,128)(2,1)S(1)} %get-tuple-element.33), channel_id=1, source_target_pairs={{0,4},{2,6},{4,0},{6,2},{8,12},{10,14},{12,8},{14,10},{1,5},{3,7},... | collective-permute-start | bytes 786440 | tf_op jit(solution)/shard_map/ppermute | solution.py:321
  32.7 1.3 %collective-permute-start.7 = (bf16[2,2,256,128]{3,2,1,0:T(8,128)(2,1)S(1)}, bf16[2,2,256,128]{3,2,1,0:T(8,128)(2,1)S(1)}, u32[]{:S(2)}, u32[]{:S(2)}) collective-permute-start(bf16[2,2,256,128]{3,2,1,0:T(8,128)(2,1)S(1)} %get-tuple-element.22), channel_id=1, source_target_pairs={{0,6},{2,4},{4,2},{6,0},{8,14},{10,12},{12,10},{14,8},{1,7},{3,5},... | collective-permute-start | bytes 786440 | tf_op jit(solution)/shard_map/ppermute | solution.py:321
  34.0 0.1 dynamic_slice.16
  34.1 0.1 dynamic_slice.15
  34.2 0.1 broadcast_in_dim.42
  34.3 0.1 reshape.81.dt_ref
  34.5 0.1 copy.34
  34.6 0.2 reshape.79.x_ref
  34.8 0.1 copy.35
  34.9 0.2 reshape.80.z_ref
  35.1 0.6 %copy-done.7 = f32[64]{0:T(128)S(1)} copy-done((f32[64]{0:T(128)S(1)}, f32[64]{0:T(128)}, u32[]{:S(2)}) %copy-start.7) | copy-done | bytes 280
  35.7 0.0 copy-done.8
  35.8 0.0 copy-done.9
  35.8 0.1 broadcast_in_dim.43
  35.9 0.1 reshape.84.head_ref
  36.0 0.6 %copy-done.3 = f32[64,32]{0,1:T(8,128)S(1)} copy-done((f32[64,32]{0,1:T(8,128)S(1)}, f32[64,32]{0,1:T(8,128)}, u32[]{:S(2)}) %copy-start.3) | copy-done | bytes 8216
  36.6 0.1 copy.38
  36.7 0.1 reshape.85.refs_7_
  36.8 0.7 %shard_map.141 = (f32[8,2048]{1,0:T(8,128)S(1)}, f32[8,2048]{1,0:T(8,128)S(1)}, f32[8,2048]{1,0:T(8,128)S(1)}, bf16[48,2048]{1,0:T(8,128)(2,1)S(1)}, bf16[2,48,5...) custom-call(bf16[8,2048]{1,0:T(8,128)(2,1)S(1)} %reshape.79.x_ref, ...), custom_call_target="tpu_custom_call" | custom-call | tf_op jit(solution)/shard_map/pallas_call | solution.py:140
  37.5 0.1 add_bitcast_fusion.info_row
  37.5 1.3 %collective-permute-done.8.refs_1_ = bf16[2,2,256,128]{3,2,1,0:T(8,128)(2,1)S(1)} collective-permute-done((bf16[2,2,256,128]{3,2,1,0:T(8,128)(2,1)S(1)}, bf16[2,2,256,128]{3,2,1,0:T(8,128)(2,1)S(1)}, u32[]{:S(2)}, u32[]{:S(2)}) %collective-permute-start.8) | collective-permute-done | bytes 262176 | tf_op jit(solution)/shard_map/ppermute | solution.py:321
  38.8 2.4 %collective-permute-done.9.refs_2_ = bf16[2,2,256,128]{3,2,1,0:T(8,128)(2,1)S(1)} collective-permute-done((bf16[2,2,256,128]{3,2,1,0:T(8,128)(2,1)S(1)}, bf16[2,2,256,128]{3,2,1,0:T(8,128)(2,1)S(1)}, u32[]{:S(2)}, u32[]{:S(2)}) %collective-permute-start.9) | collective-permute-done | bytes 262176 | tf_op jit(solution)/shard_map/ppermute | solution.py:321
  41.2 1.9 %shard_map.142 = (bf16[2,2048,128]{2,1,0:T(8,128)(2,1)}, f32[2,8,2048]{2,1,0:T(8,128)S(1)}) custom-call(s32[1,4]{1,0:T(1,128)S(1)} %add_bitcast_fusion.info_row, bf16[2,2,256,128]{3,2,1,0:T(8,128)(2,1)S(1)} %get-tuple-element.31.refs_0_, bf16[2,2,256,128]{3,2,1,0:T(8,128)(2,1)S(1)} %collective-permute-done.8.refs_1_, ...), custom_call_target="tpu_custom_call" | custom-call | tf_op jit(solution)/shard_map/pallas_call | solution.py:282
  43.1 1.4 %collective-permute-done.7.refs_0_ = bf16[2,2,256,128]{3,2,1,0:T(8,128)(2,1)S(1)} collective-permute-done((bf16[2,2,256,128]{3,2,1,0:T(8,128)(2,1)S(1)}, bf16[2,2,256,128]{3,2,1,0:T(8,128)(2,1)S(1)}, u32[]{:S(2)}, u32[]{:S(2)}) %collective-permute-start.7) | collective-permute-done | bytes 262176 | tf_op jit(solution)/shard_map/ppermute | solution.py:321
  44.5 1.6 %shard_map.143 = (bf16[8,32,64]{2,1,0:T(8,128)(2,1)}, bf16[2,2048,128]{2,1,0:T(8,128)(2,1)}) custom-call(s32[1,4]{1,0:T(1,128)S(1)} %add_bitcast_fusion.info_row, bf16[2,2,256,128]{3,2,1,0:T(8,128)(2,1)S(1)} %collective-permute-done.7.refs_0_, bf16[48,2048]{1,0:T(8,128)(2,1)S(1)} %get-tuple-element.23.refs_3_.refs_1_, ...), custom_call_target="tpu_custom_call", output_to_operand_aliasing={{1}: (12, {})} | custom-call | tf_op jit(solution)/shard_map/pallas_call | solution.py:282
  (38 shorter events, 0.3 us)
Async XLA Ops:
  1.6 12.8 %collective-permute-start = (bf16[2,256,128]{2,1,0:T(8,128)(2,1)S(1)}, bf16[2,256,128]{2,1,0:T(8,128)(2,1)S(1)}, u32[]{:S(2)}, u32[]{:S(2)}) collective-permute-start(bf16[2,256,128]{2,1,0:T(8,128)(2,1)S(1)} %slice_bitcast_fusion.2), channel_id=1, source_target_pairs={{0,2},{2,0},{4,6},{6,4},{8,10},{10,8},{12,14},{14,12},{1,3},{3,1},... | collective-permute-start | bytes 393224 | tf_op jit(solution)/shard_map/ppermute | solution.py:321
  4.6 25.5 %collective-permute-start.4 = (bf16[2,256,128]{2,1,0:T(8,128)(2,1)S(1)}, bf16[2,256,128]{2,1,0:T(8,128)(2,1)S(1)}, u32[]{:S(2)}, u32[]{:S(2)}) collective-permute-start(bf16[2,256,128]{2,1,0:T(8,128)(2,1)S(1)} %slice_bitcast_fusion.2), channel_id=1, source_target_pairs={{0,10},{2,8},{4,14},{6,12},{8,2},{10,0},{12,6},{14,4},{1,11},{3,9}... | collective-permute-start | bytes 393224 | tf_op jit(solution)/shard_map/ppermute | solution.py:321
  8.2 10.3 %collective-permute-start.1 = (bf16[2,256,128]{2,1,0:T(8,128)(2,1)S(1)}, bf16[2,256,128]{2,1,0:T(8,128)(2,1)S(1)}, u32[]{:S(2)}, u32[]{:S(2)}) collective-permute-start(bf16[2,256,128]{2,1,0:T(8,128)(2,1)S(1)} %get-tuple-element.40), channel_id=1, source_target_pairs={{0,4},{2,6},{4,0},{6,2},{8,12},{10,14},{12,8},{14,10},{1,5},{3,7},... | collective-permute-start | bytes 393224 | tf_op jit(solution)/shard_map/ppermute | solution.py:321
  9.8 20.3 %collective-permute-start.5 = (bf16[2,256,128]{2,1,0:T(8,128)(2,1)S(1)}, bf16[2,256,128]{2,1,0:T(8,128)(2,1)S(1)}, u32[]{:S(2)}, u32[]{:S(2)}) collective-permute-start(bf16[2,256,128]{2,1,0:T(8,128)(2,1)S(1)} %get-tuple-element.40), channel_id=1, source_target_pairs={{0,12},{2,14},{4,8},{6,10},{8,4},{10,6},{12,0},{14,2},{1,13},{3,15... | collective-permute-start | bytes 393224 | tf_op jit(solution)/shard_map/ppermute | solution.py:321
  9.8 13.4 %collective-permute-start.2 = (bf16[2,256,128]{2,1,0:T(8,128)(2,1)S(1)}, bf16[2,256,128]{2,1,0:T(8,128)(2,1)S(1)}, u32[]{:S(2)}, u32[]{:S(2)}) collective-permute-start(bf16[2,256,128]{2,1,0:T(8,128)(2,1)S(1)} %get-tuple-element.39), channel_id=1, source_target_pairs={{0,6},{2,4},{4,2},{6,0},{8,14},{10,12},{12,10},{14,8},{1,7},{3,5},... | collective-permute-start | bytes 393224 | tf_op jit(solution)/shard_map/ppermute | solution.py:321
  12.7 0.7 %copy-start.10 = (s32[8]{0:T(128)S(1)}, s32[8]{0:T(128)}, u32[]{:S(2)}) copy-start(s32[8]{0:T(128)} %param.14) | copy-start | bytes 100
  12.7 0.7 %copy-start.11 = (s32[8]{0:T(128)S(1)}, s32[8]{0:T(128)}, u32[]{:S(2)}) copy-start(s32[8]{0:T(128)} %param.15) | copy-start | bytes 100
  14.4 15.8 %collective-permute-start.6 = (bf16[2,256,128]{2,1,0:T(8,128)(2,1)S(1)}, bf16[2,256,128]{2,1,0:T(8,128)(2,1)S(1)}, u32[]{:S(2)}, u32[]{:S(2)}) collective-permute-start(bf16[2,256,128]{2,1,0:T(8,128)(2,1)S(1)} %get-tuple-element.39), channel_id=1, source_target_pairs={{0,14},{2,12},{4,10},{6,8},{8,6},{10,4},{12,2},{14,0},{1,15},{3,13... | collective-permute-start | bytes 393224 | tf_op jit(solution)/shard_map/ppermute | solution.py:321
  18.5 11.6 %collective-permute-start.3 = (bf16[2,256,128]{2,1,0:T(8,128)(2,1)S(1)}, bf16[2,256,128]{2,1,0:T(8,128)(2,1)S(1)}, u32[]{:S(2)}, u32[]{:S(2)}) collective-permute-start(bf16[2,256,128]{2,1,0:T(8,128)(2,1)S(1)} %get-tuple-element.38), channel_id=1, source_target_pairs={{0,8},{2,10},{4,12},{6,14},{8,0},{10,2},{12,4},{14,6},{1,9},{3,11}... | collective-permute-start | bytes 393224 | tf_op jit(solution)/shard_map/ppermute | solution.py:321
  30.2 3.8 %copy-start.5 = (bf16[4,2,4,128]{3,2,1,0:T(4,128)(2,1)S(1)}, bf16[4,2,4,128]{3,2,1,0:T(4,128)(2,1)}, u32[]{:S(2)}) copy-start(bf16[4,2,4,128]{3,2,1,0:T(4,128)(2,1)} %param.21) | copy-start | bytes 24580
  30.2 3.8 %copy-start.6 = (bf16[4,2,4,128]{3,2,1,0:T(4,128)(2,1)S(1)}, bf16[4,2,4,128]{3,2,1,0:T(4,128)(2,1)}, u32[]{:S(2)}) copy-start(bf16[4,2,4,128]{3,2,1,0:T(4,128)(2,1)} %param.20) | copy-start | bytes 24580
  30.2 4.0 %copy-start.4 = (f32[4,2,64]{2,1,0:T(2,128)S(1)}, f32[4,2,64]{2,1,0:T(2,128)}, u32[]{:S(2)}) copy-start(f32[4,2,64]{2,1,0:T(2,128)} %param.19) | copy-start | bytes 6148
  30.2 4.3 %copy-start.1 = (bf16[4,2,64,32]{2,3,1,0:T(8,128)(2,1)S(1)}, bf16[4,2,64,32]{2,3,1,0:T(8,128)(2,1)}, u32[]{:S(2)}) copy-start(bf16[4,2,64,32]{2,3,1,0:T(8,128)(2,1)} %param.17) | copy-start | bytes 98308
  30.2 4.6 %copy-start.2 = (bf16[4,2,64,32]{2,3,1,0:T(8,128)(2,1)S(1)}, bf16[4,2,64,32]{2,3,1,0:T(8,128)(2,1)}, u32[]{:S(2)}) copy-start(bf16[4,2,64,32]{2,3,1,0:T(8,128)(2,1)} %param.18) | copy-start | bytes 98308
  30.4 10.8 %copy-start = (bf16[2,64,32,128]{3,2,1,0:T(8,128)(2,1)S(1)}, bf16[2,64,32,128]{3,2,1,0:T(8,128)(2,1)}, u32[]{:S(2)}) copy-start(bf16[2,64,32,128]{3,2,1,0:T(8,128)(2,1)} %param.16) | copy-start | bytes 3145732
  30.4 8.4 %collective-permute-start.8 = (bf16[2,2,256,128]{3,2,1,0:T(8,128)(2,1)S(1)}, bf16[2,2,256,128]{3,2,1,0:T(8,128)(2,1)S(1)}, u32[]{:S(2)}, u32[]{:S(2)}) collective-permute-start(bf16[2,2,256,128]{3,2,1,0:T(8,128)(2,1)S(1)} %get-tuple-element.32), channel_id=1, source_target_pairs={{0,2},{2,0},{4,6},{6,4},{8,10},{10,8},{12,14},{14,12},{1,3},{3,1},... | collective-permute-start | bytes 786440 | tf_op jit(solution)/shard_map/ppermute | solution.py:321
  32.0 9.2 %collective-permute-start.9 = (bf16[2,2,256,128]{3,2,1,0:T(8,128)(2,1)S(1)}, bf16[2,2,256,128]{3,2,1,0:T(8,128)(2,1)S(1)}, u32[]{:S(2)}, u32[]{:S(2)}) collective-permute-start(bf16[2,2,256,128]{3,2,1,0:T(8,128)(2,1)S(1)} %get-tuple-element.33), channel_id=1, source_target_pairs={{0,4},{2,6},{4,0},{6,2},{8,12},{10,14},{12,8},{14,10},{1,5},{3,7},... | collective-permute-start | bytes 786440 | tf_op jit(solution)/shard_map/ppermute | solution.py:321
  32.7 11.8 %collective-permute-start.7 = (bf16[2,2,256,128]{3,2,1,0:T(8,128)(2,1)S(1)}, bf16[2,2,256,128]{3,2,1,0:T(8,128)(2,1)S(1)}, u32[]{:S(2)}, u32[]{:S(2)}) collective-permute-start(bf16[2,2,256,128]{3,2,1,0:T(8,128)(2,1)S(1)} %get-tuple-element.22), channel_id=1, source_target_pairs={{0,6},{2,4},{4,2},{6,0},{8,14},{10,12},{12,10},{14,8},{1,7},{3,5},... | collective-permute-start | bytes 786440 | tf_op jit(solution)/shard_map/ppermute | solution.py:321
  35.1 0.7 %copy-start.7 = (f32[64]{0:T(128)S(1)}, f32[64]{0:T(128)}, u32[]{:S(2)}) copy-start(f32[64]{0:T(128)} %param.24) | copy-start | bytes 772
  35.1 0.7 %copy-start.8 = (f32[64]{0:T(128)S(1)}, f32[64]{0:T(128)}, u32[]{:S(2)}) copy-start(f32[64]{0:T(128)} %param.23) | copy-start | bytes 772
  35.1 0.7 %copy-start.9 = (f32[64]{0:T(128)S(1)}, f32[64]{0:T(128)}, u32[]{:S(2)}) copy-start(f32[64]{0:T(128)} %param.22) | copy-start | bytes 772
  35.9 0.7 %copy-start.3 = (f32[64,32]{0,1:T(8,128)S(1)}, f32[64,32]{0,1:T(8,128)}, u32[]{:S(2)}) copy-start(f32[64,32]{0,1:T(8,128)} %param.25) | copy-start | bytes 24580

commit v7 on v6

--- a/solution.py
+++ b/solution.py
@@ -160,7 +160,7 @@
 
 
 def decode_kernel(rows, groups, parts, last, info_row, *refs):
-    info_ref = [info_row[0, i] for i in range(2 * rows)]
+    info_ref = [info_row[0, i] for i in range(info_row.shape[1])]
     recv_refs, refs = refs[:len(parts)], refs[len(parts):]
     left_ref, right_ref, seen_ref = refs[:3]
     span, entries = recv_refs[0].shape[2:]
@@ -196,7 +196,7 @@
     def listed_row(r, act):
         for p, part in enumerate(parts):
             for g in range(groups):
-                act(p, g, place(r, g, info_ref[rows + r] ^ part))
+                act(p, g, place(r, g, info_ref[rows + r] ^ info_ref[2 * rows + part]))
 
     def staying_row(r, act):
         for quarter in range(quarters):
@@ -317,8 +317,13 @@
         return lax.all_to_all(
             value, "rows", split_axis=0, concat_axis=0, tiled=True, axis_index_groups=groups)
 
-    def hand(value, k):
-        return lax.ppermute(value, "rows", [(i, i ^ k) for i in range(shards)])
+    cores = lax.axis_size("head")
+    core = lax.axis_index("head")
+
+    def hand(value, distances):
+        return lax.ppermute(value, ("rows", "head"), [
+            (i * cores + c, (i ^ distances[c % 2]) * cores + c)
+            for i in range(shards) for c in range(cores)])
 
     pieces = prefill_states.reshape(groups, quarter, span, entries)
     here = jnp.arange(shards * row_count, dtype=jnp.int32) // row_count
@@ -326,14 +331,19 @@
     if few:
         first, rest = lax.optimization_barrier((pieces[:, 1], pieces))
         cut = [rest[:, 0], first, rest[:, 2], rest[:, 3]]
-        arrived = [cut[0]] + [hand(cut[k % quarter], k) for k in range(1, shards)]
+        first_hop = [(k, k ^ quarter if k != quarter else k) for k in range(1, shards)]
+        arrived = [cut[0]] + [hand(cut[k % quarter], pair) for k, pair in enumerate(first_hop, 1)]
         held = jnp.stack(arrived)
-        order = jnp.arange(quarter)[:, None] ^ (me % quarter)
+        second_hop = [(0, 0), (1, 1), (2, 2), (3, 3)]
+        distance = jnp.array(second_hop, jnp.int32)[:, core % 2]
+        order = distance[:, None] ^ (me % quarter)
         order = (order * row_count + jnp.arange(row_count)).reshape(half_rows)
+        slots = source ^ me
+        slots = jnp.where((core % 2 == 1) & (slots % quarter != 0), slots ^ quarter, slots)
         slots = lax.dynamic_slice_in_dim(
-            source ^ me, (me // quarter) * half_rows, half_rows)[order]
+            slots, (me // quarter) * half_rows, half_rows)[order]
         sent = gather_pieces(slots, held, quarter)
-        recv = [sent[0]] + [hand(sent[k], k) for k in range(1, quarter)]
+        recv = [sent[0]] + [hand(sent[k], second_hop[k]) for k in range(1, quarter)]
         mask = (source ^ here) % quarter
     else:
         pieces = jnp.moveaxis(pieces, 0, 1)
@@ -346,6 +356,7 @@
         sent = sent.reshape(row_count, groups, 4, quarter * span // 4, entries)
         recv = [sent[:, :, p] for p in range(4)]
         mask = jnp.zeros_like(source)
+        distance = jnp.arange(4, dtype=jnp.int32)
 
     groups = local_heads // (HEADS // GROUPS)
     group_base = lax.axis_index("head") * groups
@@ -356,11 +367,11 @@
         a_rate, dt_bias, skip_d)
     info = jnp.concatenate([
         lax.dynamic_slice_in_dim(listed, me * row_count, row_count),
-        lax.dynamic_slice_in_dim(mask, me * row_count, row_count)])[None]
+        lax.dynamic_slice_in_dim(mask, me * row_count, row_count), distance])[None]
     resident = resident_states.reshape(row_count, flat, entries)
     gain = norm_gain.reshape(1, flat)
-    final, seen = decode((0, 1, 2), info, recv[:3], resident, ready, gain, ())
-    decoded, final = decode((3,), info, recv[3:], resident, ready, gain, (seen, final))
+    final, seen = decode((0, 3), info, [recv[0], recv[3]], resident, ready, gain, ())
+    decoded, final = decode((1, 2), info, recv[1:3], resident, ready, gain, (seen, final))
     steps = x_new.shape[0]
     decoded = decoded.reshape(steps, row_count, channels, local_heads)
     return (jnp.swapaxes(decoded, 2, 3), final.reshape(resident_states.shape))

time: 46.4 us -> 46 us (level)
  waiting for transfers between devices: 17.7 us -> 16.2 us
  local copies, waits for them, and re-layouts: 7.21 us -> 7.87 us
    ppermute x10, waiting for transfers between devices: 17.7 us -> 16.2 us  [hand(): lax.ppermute(value, ('rows', 'head'), [(i * cores + c, (i ^ distances[c %...]
    unnamed x34 -> x36, local copies, waits for them, and re-layouts: 3.34 us -> 4.01 us
  transfers between devices with their start and end apart: 10 -> 10, of which waited for: 6 -> 5; matrix products, arithmetic and copies ran while one was open for 10% -> 10% of each run, Pallas kernels for 6% -> 5%
where the time goes in v7:
time: 46 us; the launch traced here: 45.7 us
  waiting for transfers between devices  16.2 us (35%)
  starting transfers between devices  16 us (35%)
  local copies, waits for them, and re-layouts  7.87 us (17%)
  Pallas kernels  4.35 us (9%)
  between operations  0.94 us (2%)
    ppermute x10, waiting for transfers between devices, hand(): lax.ppermute(value, ('rows', 'head'), [(i * cores + c, (i ^ distances[c %...  16.2 us
    ppermute x10, starting transfers between devices, hand(): lax.ppermute(value, ('rows', 'head'), [(i * cores + c, (i ^ distances[c %...  16 us
    unnamed x36, local copies, waits for them, and re-layouts  4.01 us
    pallas_call x2, Pallas kernels, decode(): pl.pallas_call(functools.partial(decode_kernel, rows, groups, parts, last...  3.48 us
    squeeze x1, local copies, waits for them, and re-layouts, local(): cut = [rest[:, 0], first, rest[:, 2], rest[:, 3]]  1.06 us
    squeeze x1, local copies, waits for them, and re-layouts, local(): first, rest = lax.optimization_barrier((pieces[:, 1], pieces))  0.92 us
  transfers between devices with their start and end apart: 10, of which 5 were waited for; matrix products, arithmetic and copies ran while one was open for 10% of the time, Pallas kernels for 5%

profile of v7, /device:TPU:0, one launch (start us, length us, event | category | flops | bytes accessed | tf_op | source)
XLA Modules:
  0.0 45.7 jit_solution(10426791658135348610)
XLA Ops:
  0.6 0.9 %slice_bitcast_fusion.2 = bf16[2,256,128]{2,1,0:T(8,128)(2,1)S(1)} fusion(bf16[2,4,256,128]{3,2,1,0:T(8,128)(2,1)} %bitcast.60), kind=kLoop, calls=%fused_computation.3 | loop fusion | bytes 262144 | tf_op jit(solution)/shard_map/squeeze | solution.py:332
  1.6 3.0 %collective-permute-start = (bf16[2,256,128]{2,1,0:T(8,128)(2,1)S(1)}, bf16[2,256,128]{2,1,0:T(8,128)(2,1)S(1)}, u32[]{:S(2)}, u32[]{:S(2)}) collective-permute-start(bf16[2,256,128]{2,1,0:T(8,128)(2,1)S(1)} %slice_bitcast_fusion.2), channel_id=1, source_target_pairs={{0,2},{1,11},{2,0},{3,9},{4,6},{5,15},{6,4},{7,13},{8,10},{9,3},{1... | collective-permute-start | bytes 393224 | tf_op jit(solution)/shard_map/ppermute | solution.py:324
  4.6 2.6 %collective-permute-start.4 = (bf16[2,256,128]{2,1,0:T(8,128)(2,1)S(1)}, bf16[2,256,128]{2,1,0:T(8,128)(2,1)S(1)}, u32[]{:S(2)}, u32[]{:S(2)}) collective-permute-start(bf16[2,256,128]{2,1,0:T(8,128)(2,1)S(1)} %slice_bitcast_fusion.2), channel_id=1, source_target_pairs={{0,10},{1,3},{2,8},{3,1},{4,14},{5,7},{6,12},{7,5},{8,2},{9,11},{1... | collective-permute-start | bytes 393224 | tf_op jit(solution)/shard_map/ppermute | solution.py:324
  7.1 1.1 %slice_bitcast_fusion.3 = (bf16[2,256,128]{2,1,0:T(8,128)(2,1)S(1)}, bf16[2,256,128]{2,1,0:T(8,128)(2,1)S(1)}, bf16[2,256,128]{2,1,0:T(8,128)(2,1)S(1)}) fusion(bf16[2,4,256,128]{3,2,1,0:T(8,128)(2,1)} %bitcast.61), kind=kLoop, calls=%fused_computation.12 | loop fusion | bytes 786432 | tf_op jit(solution)/shard_map/squeeze | solution.py:333
  8.2 1.6 %collective-permute-start.1 = (bf16[2,256,128]{2,1,0:T(8,128)(2,1)S(1)}, bf16[2,256,128]{2,1,0:T(8,128)(2,1)S(1)}, u32[]{:S(2)}, u32[]{:S(2)}) collective-permute-start(bf16[2,256,128]{2,1,0:T(8,128)(2,1)S(1)} %get-tuple-element.40), channel_id=1, source_target_pairs={{0,4},{1,13},{2,6},{3,15},{4,0},{5,9},{6,2},{7,11},{8,12},{9,5},{1... | collective-permute-start | bytes 393224 | tf_op jit(solution)/shard_map/ppermute | solution.py:324
  9.8 1.8 %collective-permute-start.2 = (bf16[2,256,128]{2,1,0:T(8,128)(2,1)S(1)}, bf16[2,256,128]{2,1,0:T(8,128)(2,1)S(1)}, u32[]{:S(2)}, u32[]{:S(2)}) collective-permute-start(bf16[2,256,128]{2,1,0:T(8,128)(2,1)S(1)} %get-tuple-element.39), channel_id=1, source_target_pairs={{0,6},{1,15},{2,4},{3,13},{4,2},{5,11},{6,0},{7,9},{8,14},{9,7},{1... | collective-permute-start | bytes 393224 | tf_op jit(solution)/shard_map/ppermute | solution.py:324
  11.6 0.9 %bitcast_dynamic-update-slice_fusion.7 = bf16[8,2,256,128]{3,2,1,0:T(8,128)(2,1)S(1)} fusion(bf16[2,4,256,128]{3,2,1,0:T(8,128)(2,1)} %bitcast.62), kind=kLoop, calls=%fused_computation.11 | loop fusion | bytes 262144
  12.6 0.0 copy-start.10
  12.6 0.7 %copy-done.10 = s32[4,2]{0,1:T(2,128)S(1)} copy-done((s32[4,2]{0,1:T(2,128)S(1)}, s32[4,2]{0,1:T(2,128)}, u32[]{:S(2)}) %copy-start.10) | copy-done | bytes 56
  13.3 0.1 iota_add_fusion
  13.3 0.1 add.81
  13.4 0.6 %copy-done.11 = s32[8]{0:T(128)S(1)} copy-done((s32[8]{0:T(128)S(1)}, s32[8]{0:T(128)}, u32[]{:S(2)}) %copy-start.11) | copy-done | bytes 56
  14.1 0.0 copy-done.12
  14.1 0.1 select_reduce_fusion
  14.2 0.1 dynamic_slice.21
  14.3 0.6 %gather_fusion = s32[8]{0:T(128)S(1)} fusion(s32[8]{0:T(128)S(1)} %dynamic_slice.21, s32[1024]{0:T(1024)S(1)} %pad_clamp_fusion), kind=kCustom, calls=%fused_computation | custom fusion | bytes 96 | tf_op jit(solution)/shard_map/gather | solution.py:343
  15.0 0.1 fusion
  15.0 3.0 %collective-permute-start.6 = (bf16[2,256,128]{2,1,0:T(8,128)(2,1)S(1)}, bf16[2,256,128]{2,1,0:T(8,128)(2,1)S(1)}, u32[]{:S(2)}, u32[]{:S(2)}) collective-permute-start(bf16[2,256,128]{2,1,0:T(8,128)(2,1)S(1)} %get-tuple-element.39), channel_id=1, source_target_pairs={{0,14},{1,7},{2,12},{3,5},{4,10},{5,3},{6,8},{7,1},{8,6},{9,15},{1... | collective-permute-start | bytes 393224 | tf_op jit(solution)/shard_map/ppermute | solution.py:324
  18.1 2.0 %collective-permute-done.1 = bf16[2,256,128]{2,1,0:T(8,128)(2,1)S(1)} collective-permute-done((bf16[2,256,128]{2,1,0:T(8,128)(2,1)S(1)}, bf16[2,256,128]{2,1,0:T(8,128)(2,1)S(1)}, u32[]{:S(2)}, u32[]{:S(2)}) %collective-permute-start.1) | collective-permute-done | bytes 131104 | tf_op jit(solution)/shard_map/ppermute | solution.py:324
  20.1 0.4 collective-permute-start.3
  20.5 2.1 %collective-permute-done.2 = bf16[2,256,128]{2,1,0:T(8,128)(2,1)S(1)} collective-permute-done((bf16[2,256,128]{2,1,0:T(8,128)(2,1)S(1)}, bf16[2,256,128]{2,1,0:T(8,128)(2,1)S(1)}, u32[]{:S(2)}, u32[]{:S(2)}) %collective-permute-start.2) | collective-permute-done | bytes 131104 | tf_op jit(solution)/shard_map/ppermute | solution.py:324
  22.6 7.2 %collective-permute-done.3 = bf16[2,256,128]{2,1,0:T(8,128)(2,1)S(1)} collective-permute-done((bf16[2,256,128]{2,1,0:T(8,128)(2,1)S(1)}, bf16[2,256,128]{2,1,0:T(8,128)(2,1)S(1)}, u32[]{:S(2)}, u32[]{:S(2)}) %collective-permute-start.3) | collective-permute-done | bytes 131104 | tf_op jit(solution)/shard_map/ppermute | solution.py:324
  30.0 0.2 shard_map.149
  30.2 0.7 %collective-permute-start.9 = (bf16[2,2,256,128]{3,2,1,0:T(8,128)(2,1)S(1)}, bf16[2,2,256,128]{3,2,1,0:T(8,128)(2,1)S(1)}, u32[]{:S(2)}, u32[]{:S(2)}) collective-permute-start(bf16[2,2,256,128]{3,2,1,0:T(8,128)(2,1)S(1)} %get-tuple-element.33), channel_id=1, source_target_pairs={{0,6},{1,7},{2,4},{3,5},{4,2},{5,3},{6,0},{7,1},{8,14},{9,15},{10,... | collective-permute-start | bytes 786440 | tf_op jit(solution)/shard_map/ppermute | solution.py:324
  30.9 1.5 %collective-permute-start.7 = (bf16[2,2,256,128]{3,2,1,0:T(8,128)(2,1)S(1)}, bf16[2,2,256,128]{3,2,1,0:T(8,128)(2,1)S(1)}, u32[]{:S(2)}, u32[]{:S(2)}) collective-permute-start(bf16[2,2,256,128]{3,2,1,0:T(8,128)(2,1)S(1)} %get-tuple-element.22), channel_id=1, source_target_pairs={{0,2},{1,3},{2,0},{3,1},{4,6},{5,7},{6,4},{7,5},{8,10},{9,11},{10,... | collective-permute-start | bytes 786440 | tf_op jit(solution)/shard_map/ppermute | solution.py:324
  32.4 1.4 %collective-permute-start.8 = (bf16[2,2,256,128]{3,2,1,0:T(8,128)(2,1)S(1)}, bf16[2,2,256,128]{3,2,1,0:T(8,128)(2,1)S(1)}, u32[]{:S(2)}, u32[]{:S(2)}) collective-permute-start(bf16[2,2,256,128]{3,2,1,0:T(8,128)(2,1)S(1)} %get-tuple-element.23), channel_id=1, source_target_pairs={{0,4},{1,5},{2,6},{3,7},{4,0},{5,1},{6,2},{7,3},{8,12},{9,13},{10,... | collective-permute-start | bytes 786440 | tf_op jit(solution)/shard_map/ppermute | solution.py:324
  33.8 0.1 dynamic_slice.19
  33.8 0.1 dynamic_slice.18
  33.9 0.1 broadcast_in_dim.41
  34.1 0.1 reshape.74.dt_ref
  34.2 0.1 copy.35
  34.4 0.2 reshape.72.x_ref
  34.5 0.1 copy.36
  34.7 0.2 reshape.73.z_ref
  34.9 0.6 %copy-done.7 = f32[64]{0:T(128)S(1)} copy-done((f32[64]{0:T(128)S(1)}, f32[64]{0:T(128)}, u32[]{:S(2)}) %copy-start.7) | copy-done | bytes 280
  35.5 0.0 copy-done.8
  35.5 0.0 copy-done.9
  35.5 0.1 broadcast_in_dim.42
  35.6 0.1 reshape.77.head_ref
  35.8 0.6 %copy-done.3 = f32[64,32]{0,1:T(8,128)S(1)} copy-done((f32[64,32]{0,1:T(8,128)S(1)}, f32[64,32]{0,1:T(8,128)}, u32[]{:S(2)}) %copy-start.3) | copy-done | bytes 8216
  36.4 0.1 copy.39
  36.4 0.1 reshape.78.refs_8_
  36.5 0.7 %shard_map.150 = (f32[8,2048]{1,0:T(8,128)S(1)}, f32[8,2048]{1,0:T(8,128)S(1)}, f32[8,2048]{1,0:T(8,128)S(1)}, bf16[48,2048]{1,0:T(8,128)(2,1)S(1)}, bf16[2,48,5...) custom-call(bf16[8,2048]{1,0:T(8,128)(2,1)S(1)} %reshape.72.x_ref, ...), custom_call_target="tpu_custom_call" | custom-call | tf_op jit(solution)/shard_map/pallas_call | solution.py:140
  37.2 0.1 add_bitcast_fusion.info_row
  37.3 3.1 %collective-permute-done.9.refs_1_ = bf16[2,2,256,128]{3,2,1,0:T(8,128)(2,1)S(1)} collective-permute-done((bf16[2,2,256,128]{3,2,1,0:T(8,128)(2,1)S(1)}, bf16[2,2,256,128]{3,2,1,0:T(8,128)(2,1)S(1)}, u32[]{:S(2)}, u32[]{:S(2)}) %collective-permute-start.9) | collective-permute-done | bytes 262176 | tf_op jit(solution)/shard_map/ppermute | solution.py:324
  40.4 1.8 %shard_map.151 = (bf16[2,2048,128]{2,1,0:T(8,128)(2,1)}, f32[2,8,2048]{2,1,0:T(8,128)S(1)}) custom-call(s32[1,8]{1,0:T(1,128)S(1)} %add_bitcast_fusion.info_row, bf16[2,2,256,128]{3,2,1,0:T(8,128)(2,1)S(1)} %get-tuple-element.32.refs_0_, bf16[2,2,256,128]{3,2,1,0:T(8,128)(2,1)S(1)} %collective-permute-done.9.refs_1_, ...), custom_call_target="tpu_custom_call" | custom-call | tf_op jit(solution)/shard_map/pallas_call | solution.py:282
  42.2 1.8 %collective-permute-done.7.refs_0_ = bf16[2,2,256,128]{3,2,1,0:T(8,128)(2,1)S(1)} collective-permute-done((bf16[2,2,256,128]{3,2,1,0:T(8,128)(2,1)S(1)}, bf16[2,2,256,128]{3,2,1,0:T(8,128)(2,1)S(1)}, u32[]{:S(2)}, u32[]{:S(2)}) %collective-permute-start.7) | collective-permute-done | bytes 262176 | tf_op jit(solution)/shard_map/ppermute | solution.py:324
  44.0 1.7 %shard_map.152 = (bf16[8,32,64]{2,1,0:T(8,128)(2,1)}, bf16[2,2048,128]{2,1,0:T(8,128)(2,1)}) custom-call(s32[1,8]{1,0:T(1,128)S(1)} %add_bitcast_fusion.info_row, bf16[2,2,256,128]{3,2,1,0:T(8,128)(2,1)S(1)} %collective-permute-done.7.refs_0_, bf16[2,2,256,128]{3,2,1,0:T(8,128)(2,1)S(1)} %collective-permute-done.8.refs_1_, ...), custom_call_target="tpu_custom_call", output_to_operand_aliasing={{1}: (13, {})} | custom-call | tf_op jit(solution)/shard_map/pallas_call | solution.py:282
  (40 shorter events, 0.3 us)
Async XLA Ops:
  1.6 13.5 %collective-permute-start = (bf16[2,256,128]{2,1,0:T(8,128)(2,1)S(1)}, bf16[2,256,128]{2,1,0:T(8,128)(2,1)S(1)}, u32[]{:S(2)}, u32[]{:S(2)}) collective-permute-start(bf16[2,256,128]{2,1,0:T(8,128)(2,1)S(1)} %slice_bitcast_fusion.2), channel_id=1, source_target_pairs={{0,2},{1,11},{2,0},{3,9},{4,6},{5,15},{6,4},{7,13},{8,10},{9,3},{1... | collective-permute-start | bytes 393224 | tf_op jit(solution)/shard_map/ppermute | solution.py:324
  4.6 25.3 %collective-permute-start.4 = (bf16[2,256,128]{2,1,0:T(8,128)(2,1)S(1)}, bf16[2,256,128]{2,1,0:T(8,128)(2,1)S(1)}, u32[]{:S(2)}, u32[]{:S(2)}) collective-permute-start(bf16[2,256,128]{2,1,0:T(8,128)(2,1)S(1)} %slice_bitcast_fusion.2), channel_id=1, source_target_pairs={{0,10},{1,3},{2,8},{3,1},{4,14},{5,7},{6,12},{7,5},{8,2},{9,11},{1... | collective-permute-start | bytes 393224 | tf_op jit(solution)/shard_map/ppermute | solution.py:324
  8.2 11.9 %collective-permute-start.1 = (bf16[2,256,128]{2,1,0:T(8,128)(2,1)S(1)}, bf16[2,256,128]{2,1,0:T(8,128)(2,1)S(1)}, u32[]{:S(2)}, u32[]{:S(2)}) collective-permute-start(bf16[2,256,128]{2,1,0:T(8,128)(2,1)S(1)} %get-tuple-element.40), channel_id=1, source_target_pairs={{0,4},{1,13},{2,6},{3,15},{4,0},{5,9},{6,2},{7,11},{8,12},{9,5},{1... | collective-permute-start | bytes 393224 | tf_op jit(solution)/shard_map/ppermute | solution.py:324
  9.8 20.0 %collective-permute-start.5 = (bf16[2,256,128]{2,1,0:T(8,128)(2,1)S(1)}, bf16[2,256,128]{2,1,0:T(8,128)(2,1)S(1)}, u32[]{:S(2)}, u32[]{:S(2)}) collective-permute-start(bf16[2,256,128]{2,1,0:T(8,128)(2,1)S(1)} %get-tuple-element.40), channel_id=1, source_target_pairs={{0,12},{1,5},{2,14},{3,7},{4,8},{5,1},{6,10},{7,3},{8,4},{9,13},{1... | collective-permute-start | bytes 393224 | tf_op jit(solution)/shard_map/ppermute | solution.py:324
  9.8 12.8 %collective-permute-start.2 = (bf16[2,256,128]{2,1,0:T(8,128)(2,1)S(1)}, bf16[2,256,128]{2,1,0:T(8,128)(2,1)S(1)}, u32[]{:S(2)}, u32[]{:S(2)}) collective-permute-start(bf16[2,256,128]{2,1,0:T(8,128)(2,1)S(1)} %get-tuple-element.39), channel_id=1, source_target_pairs={{0,6},{1,15},{2,4},{3,13},{4,2},{5,11},{6,0},{7,9},{8,14},{9,7},{1... | collective-permute-start | bytes 393224 | tf_op jit(solution)/shard_map/ppermute | solution.py:324
  12.6 0.7 %copy-start.10 = (s32[4,2]{0,1:T(2,128)S(1)}, s32[4,2]{0,1:T(2,128)}, u32[]{:S(2)}) copy-start(s32[4,2]{0,1:T(2,128)} %constant.84.clone) | copy-start | bytes 100
  13.4 0.7 %copy-start.11 = (s32[8]{0:T(128)S(1)}, s32[8]{0:T(128)}, u32[]{:S(2)}) copy-start(s32[8]{0:T(128)} %param.15) | copy-start | bytes 100
  13.4 0.7 %copy-start.12 = (s32[8]{0:T(128)S(1)}, s32[8]{0:T(128)}, u32[]{:S(2)}) copy-start(s32[8]{0:T(128)} %param.16) | copy-start | bytes 100
  15.0 14.8 %collective-permute-start.6 = (bf16[2,256,128]{2,1,0:T(8,128)(2,1)S(1)}, bf16[2,256,128]{2,1,0:T(8,128)(2,1)S(1)}, u32[]{:S(2)}, u32[]{:S(2)}) collective-permute-start(bf16[2,256,128]{2,1,0:T(8,128)(2,1)S(1)} %get-tuple-element.39), channel_id=1, source_target_pairs={{0,14},{1,7},{2,12},{3,5},{4,10},{5,3},{6,8},{7,1},{8,6},{9,15},{1... | collective-permute-start | bytes 393224 | tf_op jit(solution)/shard_map/ppermute | solution.py:324
  20.1 9.7 %collective-permute-start.3 = (bf16[2,256,128]{2,1,0:T(8,128)(2,1)S(1)}, bf16[2,256,128]{2,1,0:T(8,128)(2,1)S(1)}, u32[]{:S(2)}, u32[]{:S(2)}) collective-permute-start(bf16[2,256,128]{2,1,0:T(8,128)(2,1)S(1)} %get-tuple-element.38), channel_id=1, source_target_pairs={{0,8},{1,9},{2,10},{3,11},{4,12},{5,13},{6,14},{7,15},{8,0},{9,1},... | collective-permute-start | bytes 393224 | tf_op jit(solution)/shard_map/ppermute | solution.py:324
  29.9 3.8 %copy-start.5 = (bf16[4,2,4,128]{3,2,1,0:T(4,128)(2,1)S(1)}, bf16[4,2,4,128]{3,2,1,0:T(4,128)(2,1)}, u32[]{:S(2)}) copy-start(bf16[4,2,4,128]{3,2,1,0:T(4,128)(2,1)} %param.22) | copy-start | bytes 24580
  29.9 3.8 %copy-start.6 = (bf16[4,2,4,128]{3,2,1,0:T(4,128)(2,1)S(1)}, bf16[4,2,4,128]{3,2,1,0:T(4,128)(2,1)}, u32[]{:S(2)}) copy-start(bf16[4,2,4,128]{3,2,1,0:T(4,128)(2,1)} %param.21) | copy-start | bytes 24580
  30.0 4.0 %copy-start.4 = (f32[4,2,64]{2,1,0:T(2,128)S(1)}, f32[4,2,64]{2,1,0:T(2,128)}, u32[]{:S(2)}) copy-start(f32[4,2,64]{2,1,0:T(2,128)} %param.20) | copy-start | bytes 6148
  30.0 4.3 %copy-start.1 = (bf16[4,2,64,32]{2,3,1,0:T(8,128)(2,1)S(1)}, bf16[4,2,64,32]{2,3,1,0:T(8,128)(2,1)}, u32[]{:S(2)}) copy-start(bf16[4,2,64,32]{2,3,1,0:T(8,128)(2,1)} %param.18) | copy-start | bytes 98308
  30.0 4.6 %copy-start.2 = (bf16[4,2,64,32]{2,3,1,0:T(8,128)(2,1)S(1)}, bf16[4,2,64,32]{2,3,1,0:T(8,128)(2,1)}, u32[]{:S(2)}) copy-start(bf16[4,2,64,32]{2,3,1,0:T(8,128)(2,1)} %param.19) | copy-start | bytes 98308
  30.2 10.2 %copy-start = (bf16[2,64,32,128]{3,2,1,0:T(8,128)(2,1)S(1)}, bf16[2,64,32,128]{3,2,1,0:T(8,128)(2,1)}, u32[]{:S(2)}) copy-start(bf16[2,64,32,128]{3,2,1,0:T(8,128)(2,1)} %param.17) | copy-start | bytes 3145732
  30.2 10.2 %collective-permute-start.9 = (bf16[2,2,256,128]{3,2,1,0:T(8,128)(2,1)S(1)}, bf16[2,2,256,128]{3,2,1,0:T(8,128)(2,1)S(1)}, u32[]{:S(2)}, u32[]{:S(2)}) collective-permute-start(bf16[2,2,256,128]{3,2,1,0:T(8,128)(2,1)S(1)} %get-tuple-element.33), channel_id=1, source_target_pairs={{0,6},{1,7},{2,4},{3,5},{4,2},{5,3},{6,0},{7,1},{8,14},{9,15},{10,... | collective-permute-start | bytes 786440 | tf_op jit(solution)/shard_map/ppermute | solution.py:324
  30.9 13.1 %collective-permute-start.7 = (bf16[2,2,256,128]{3,2,1,0:T(8,128)(2,1)S(1)}, bf16[2,2,256,128]{3,2,1,0:T(8,128)(2,1)S(1)}, u32[]{:S(2)}, u32[]{:S(2)}) collective-permute-start(bf16[2,2,256,128]{3,2,1,0:T(8,128)(2,1)S(1)} %get-tuple-element.22), channel_id=1, source_target_pairs={{0,2},{1,3},{2,0},{3,1},{4,6},{5,7},{6,4},{7,5},{8,10},{9,11},{10,... | collective-permute-start | bytes 786440 | tf_op jit(solution)/shard_map/ppermute | solution.py:324
  32.4 11.7 %collective-permute-start.8 = (bf16[2,2,256,128]{3,2,1,0:T(8,128)(2,1)S(1)}, bf16[2,2,256,128]{3,2,1,0:T(8,128)(2,1)S(1)}, u32[]{:S(2)}, u32[]{:S(2)}) collective-permute-start(bf16[2,2,256,128]{3,2,1,0:T(8,128)(2,1)S(1)} %get-tuple-element.23), channel_id=1, source_target_pairs={{0,4},{1,5},{2,6},{3,7},{4,0},{5,1},{6,2},{7,3},{8,12},{9,13},{10,... | collective-permute-start | bytes 786440 | tf_op jit(solution)/shard_map/ppermute | solution.py:324
  34.8 0.7 %copy-start.7 = (f32[64]{0:T(128)S(1)}, f32[64]{0:T(128)}, u32[]{:S(2)}) copy-start(f32[64]{0:T(128)} %param.25) | copy-start | bytes 772
  34.9 0.7 %copy-start.8 = (f32[64]{0:T(128)S(1)}, f32[64]{0:T(128)}, u32[]{:S(2)}) copy-start(f32[64]{0:T(128)} %param.24) | copy-start | bytes 772
  34.9 0.7 %copy-start.9 = (f32[64]{0:T(128)S(1)}, f32[64]{0:T(128)}, u32[]{:S(2)}) copy-start(f32[64]{0:T(128)} %param.23) | copy-start | bytes 772
  35.6 0.7 %copy-start.3 = (f32[64,32]{0,1:T(8,128)S(1)}, f32[64,32]{0,1:T(8,128)}, u32[]{:S(2)}) copy-start(f32[64,32]{0,1:T(8,128)} %param.26) | copy-start | bytes 24580
